TPU v7x, 256 devices: a whole 4x4x8 slice. The times are simulated.
256 devices in a mesh: seq: 16 (over z, core), head: 4 (over x), dp: 4 (over y).
Axes of the slice: x: 4, y: 4, z: 8, core: 2. Of those that a mesh axis runs over, the one named last changes fastest.
Arguments:
- queries: bfloat16 [4, 768, 32768], P('dp', 'head', 'seq'), may hold values from -170 to 170
- keys: bfloat16 [4, 768, 32768], P('dp', 'head', 'seq'), may hold values from -4 to 4
- values: bfloat16 [4, 768, 32768], P('dp', 'head', 'seq'), may hold values from -4 to 4
- cotangent: bfloat16 [4, 768, 32768], P('dp', 'head', 'seq'), may hold values from -5 to 5
- w_out: bfloat16 [768, 768], P('head'), may hold values from -0.21875 to 0.21875
- lengths: int32 [4], P('dp'), may hold values from 8192 to 32768, as said below
- offsets: int32 [12], P('head'), may hold values from 0 to 15
Outputs:
- mixed: bfloat16 [4, 768, 32768], P('dp', 'head', 'seq')
- query_grad: bfloat16 [4, 768, 32768], P('dp', 'head', 'seq')
- key_grad: bfloat16 [4, 768, 32768], P('dp', 'head', 'seq')
- value_grad: bfloat16 [4, 768, 32768], P('dp', 'head', 'seq')
- weight_grad: float32 [768, 768], P('head')
Inputs may be any that keep to these rules, and one draw needn't show every extreme that they name: `lengths`: one slide in every draw has all 32768 positions.
All inputs are finite; a program needn't handle non-finite values.
Results may differ from a plain program's by a relative error of at most 0.013.
Values may be sent and summed in bfloat16 or wider, within the bound.
No kernel may reach another device: no remote copies, remote signals or barrier semaphores. Data moves between devices by JAX's collectives and lax.ppermute only.
A program may use at most 192 MiB of HBM per device.

v0:
```python
import math

import jax
import jax.numpy as jnp
from jax import lax
from jax.sharding import PartitionSpec as P

SEL = 2048


NEGATIVE = -1e30


def attend(q_rows, k_rows, v_rows, keep_keys):
    factor = q_rows.shape[-1] ** (-0.5)
    scores = jnp.einsum("hqe,hke->hqk", q_rows, k_rows, preferred_element_type=jnp.float32) * factor
    scores = jnp.where(keep_keys[:, None, :], scores, NEGATIVE)
    row_top = jnp.max(scores, axis=-1, keepdims=True)
    expo_terms = jnp.exp(scores - row_top)
    row_total = jnp.sum(expo_terms, axis=-1, keepdims=True)
    row_probs = expo_terms / row_total
    weights = row_probs.astype(jnp.bfloat16)
    result = jnp.einsum("hqk,hke->hqe", weights, v_rows, preferred_element_type=jnp.float32)
    return (result, (row_top + jnp.log(row_total))[..., 0], row_probs, weights)


def attend_back(q_rows, k_rows, v_rows, keep_keys, grad_out, grad_lse):
    factor = q_rows.shape[-1] ** (-0.5)
    unused_out, unused_lse, row_probs, weights = attend(q_rows, k_rows, v_rows, keep_keys)
    grad_bf = grad_out.astype(jnp.bfloat16)
    grad_v = jnp.einsum("hqk,hqe->hke", weights, grad_bf, preferred_element_type=jnp.float32)
    grad_prob = jnp.einsum("hqe,hke->hqk", grad_bf, v_rows, preferred_element_type=jnp.float32)
    delta_row = jnp.sum(row_probs * grad_prob, axis=-1)
    grad_score = (
        row_probs * (grad_prob - delta_row[..., None] + grad_lse[..., None]) * factor
    ).astype(jnp.bfloat16)
    grad_q = jnp.einsum("hqk,hke->hqe", grad_score, k_rows, preferred_element_type=jnp.float32)
    grad_k = jnp.einsum("hqk,hqe->hke", grad_score, q_rows, preferred_element_type=jnp.float32)
    return (grad_q, grad_k, grad_v, delta_row)


def select_rows(source, offsets, sel_rate):
    heads_here, count = (source.shape[0], source.shape[1])
    grid = source.reshape((heads_here, count // sel_rate, sel_rate) + source.shape[2:])
    picker = offsets.reshape((heads_here, 1, 1) + (1,) * (source.ndim - 2))
    return jnp.take_along_axis(grid, picker, axis=2)[:, :, 0]


def place_rows(source, offsets, sel_rate):
    heads_here, count = (source.shape[0], source.shape[1])
    hits = (jnp.arange(sel_rate, dtype=jnp.int32)[None, :] == offsets[:, None]).astype(source.dtype)
    hits = hits.reshape((heads_here, 1, sel_rate) + (1,) * (source.ndim - 2))
    return (source[:, :, None] * hits).reshape((heads_here, count * sel_rate) + source.shape[2:])


def rejoin(stacked):
    moved = jnp.moveaxis(stacked, 0, 1)
    return moved.reshape((moved.shape[0], moved.shape[1] * moved.shape[2]) + moved.shape[3:])


def block_slices(number, q_block, tensors_q, tensors_k):
    q_parts = [lax.dynamic_slice_in_dim(item, number * q_block, q_block, 1) for item in tensors_q]
    k_parts = [item for item in tensors_k]
    return (q_parts, k_parts)


def local_forward(q_heads, k_heads, v_heads, keep_rows):
    count = q_heads.shape[1]
    q_block = min(512, SEL)

    def one_block(number):
        q_parts, k_parts = block_slices(number, q_block, (q_heads,), (k_heads, v_heads, keep_rows))
        result, lse_part, unused_probs, unused_weights = attend(
            q_parts[0], k_parts[0], k_parts[1], k_parts[2]
        )
        return (result, lse_part)

    results, lse_parts = lax.map(one_block, jnp.arange(count // q_block, dtype=jnp.int32))
    return (rejoin(results), rejoin(lse_parts))


def local_backward(q_heads, k_heads, v_heads, keep_rows, dout, dlse):
    count = q_heads.shape[1]
    q_block = min(512, SEL)
    per_segment = SEL // q_block
    segs_here = count // SEL

    def one_block(number):
        q_parts, k_parts = block_slices(
            number, q_block, (q_heads, dout, dlse), (k_heads, v_heads, keep_rows)
        )
        grad_q, grad_k, grad_v, unused_delta = attend_back(
            q_parts[0], k_parts[0], k_parts[1], k_parts[2], q_parts[1], q_parts[2]
        )
        return (grad_q, grad_k, grad_v)

    grad_q, grad_k, grad_v = lax.map(one_block, jnp.arange(count // q_block, dtype=jnp.int32))

    def fold_keys(stacked):
        return rejoin(stacked.reshape((segs_here, per_segment) + stacked.shape[1:]).sum(axis=1))

    return (rejoin(grad_q), fold_keys(grad_k), fold_keys(grad_v))


def shards(queries, keys, values, cotangent, w_out, lengths, offsets):
    tok_rows = queries.shape[2]
    heads_here = offsets.shape[0]
    head_dim = queries.shape[1] // heads_here
    seq_count = lax.axis_size("seq")
    sel_rate = tok_rows * seq_count // SEL
    positions = lax.axis_index("seq") * tok_rows + jnp.arange(tok_rows, dtype=jnp.int32)
    keep_rows = jnp.broadcast_to((positions < lengths[0])[None, :], (heads_here, tok_rows))
    far_positions = jnp.arange(SEL, dtype=jnp.int32)[None, :] * sel_rate + offsets[:, None]
    keep_far = far_positions < lengths[0]

    def split_heads(source):
        return source[0].reshape(heads_here, head_dim, tok_rows).transpose(0, 2, 1)

    def join_heads(source):
        return source.transpose(0, 2, 1).reshape(heads_here * head_dim, tok_rows)

    q_heads, k_heads, v_heads = (split_heads(queries), split_heads(keys), split_heads(values))
    q_pick = select_rows(q_heads, offsets, sel_rate)
    k_pick = select_rows(k_heads, offsets, sel_rate)
    v_pick = select_rows(v_heads, offsets, sel_rate)
    k_far, v_far = (
        lax.all_gather(k_pick, "seq", axis=1, tiled=True),
        lax.all_gather(v_pick, "seq", axis=1, tiled=True),
    )
    out_near, lse_near = local_forward(q_heads, k_heads, v_heads, keep_rows)
    out_pick, lse_pick, unused_probs, unused_weights = attend(q_pick, k_far, v_far, keep_far)
    chosen = place_rows(jnp.ones_like(lse_pick), offsets, sel_rate) > 0
    out_far = place_rows(out_pick, offsets, sel_rate)
    lse_far = jnp.where(chosen, place_rows(lse_pick, offsets, sel_rate), NEGATIVE)
    share_near = jax.nn.sigmoid(lse_near - lse_far)
    share_far = jax.nn.sigmoid(lse_far - lse_near)
    live_rows = keep_rows.astype(jnp.float32)[..., None]
    head_outs = (share_near[..., None] * out_near + share_far[..., None] * out_far) * live_rows
    attn_cols = join_heads(head_outs).astype(jnp.bfloat16)
    terms = lax.dot_general(
        w_out, attn_cols, (((0,), (0,)), ((), ())), preferred_element_type=jnp.float32
    )
    mixed = lax.psum_scatter(terms.astype(jnp.bfloat16), "head", scatter_dimension=0, tiled=True)
    dy_full = lax.all_gather(cotangent[0], "head", axis=0, tiled=True)
    d_attn = jnp.dot(w_out, dy_full, preferred_element_type=jnp.float32).astype(jnp.bfloat16)
    weight_part = lax.dot_general(
        attn_cols, dy_full, (((1,), (1,)), ((), ())), preferred_element_type=jnp.float32
    )
    grad_scale = 1.0 / math.sqrt(tok_rows * seq_count * lax.axis_size("dp"))
    weight_grad = lax.psum(weight_part, ("seq", "dp")) * grad_scale
    grad_rows = split_heads(d_attn[None]).astype(jnp.float32) * live_rows
    dout_near = share_near[..., None] * grad_rows
    dout_far = share_far[..., None] * grad_rows
    dlse_near = share_near * share_far * jnp.sum(grad_rows * (out_near - out_far), axis=-1)
    dout_pick = select_rows(dout_far, offsets, sel_rate)
    dlse_pick = -select_rows(dlse_near, offsets, sel_rate)
    dq_near, dk_near, dv_near = local_backward(
        q_heads, k_heads, v_heads, keep_rows, dout_near, dlse_near
    )
    dq_pick, dk_every, dv_every, delta_pick = attend_back(
        q_pick, k_far, v_far, keep_far, dout_pick, dlse_pick
    )
    dk_pick, dv_pick = (
        lax.psum_scatter(
            dk_every.astype(jnp.bfloat16), "seq", scatter_dimension=1, tiled=True
        ).astype(jnp.float32),
        lax.psum_scatter(
            dv_every.astype(jnp.bfloat16), "seq", scatter_dimension=1, tiled=True
        ).astype(jnp.float32),
    )

    def merge_grads(near_part, far_part):
        return join_heads(near_part + place_rows(far_part, offsets, sel_rate)).astype(jnp.bfloat16)[
            None
        ]

    query_grad = merge_grads(dq_near, dq_pick)
    key_grad = merge_grads(dk_near, dk_pick)
    value_grad = merge_grads(dv_near, dv_pick)
    return (mixed[None], query_grad, key_grad, value_grad, weight_grad)


def solution(mesh):
    return jax.shard_map(
        shards,
        mesh=mesh,
        in_specs=(
            P("dp", "head", "seq"),
            P("dp", "head", "seq"),
            P("dp", "head", "seq"),
            P("dp", "head", "seq"),
            P("head", None),
            P("dp"),
            P("head"),
        ),
        out_specs=(
            P("dp", "head", "seq"),
            P("dp", "head", "seq"),
            P("dp", "head", "seq"),
            P("dp", "head", "seq"),
            P("head", None),
        ),
        check_vma=False,
    )
```

profile of v0, /device:TPU:1, one launch (start us, length us, event | category | flops | bytes accessed | tf_op | source)
XLA Modules:
  0.0 726.8 jit_solution(11356361328635081815)
XLA Ops:
  8.8 44.6 %while.28 = (s32[]{:T(128)}, f32[4,3,512,64]{2,3,1,0:T(8,128)S(1)}, f32[4,3,512]{2,1,0:T(4,128)}, s32[4]{0:T(128)S(1)}, bf16[3,2048,64]{1,2,0:T(8,128)(2,1)}, /*...) while((s32[]{:T(128)}, f32[4,3,512,64]{2,3,1,0:T(8,128)S(1)}, ...), condition=%wide.region_3.4_spmd.clone, body=%wide.region_0.3_spmd.clone.sunk | while | flops 843053568 | bytes 43119312 | solution.py:78
  71.1 23.5 %all-gather = bf16[3,2048,1,64]{1,3,0,2:T(8,128)(2,1)S(1)} all-gather(bf16[3,128,1,64]{1,3,0,2:T(8,128)(2,1)S(1)} %get-tuple-element.254), channel_id=2, replica_groups=mesh['seq'=16,'head'=4,'dp'=4] {'seq'}, dimensions={1}, use_global_device_ids=true | all-gather | bytes 835584 | tf_op jit(solution)/shard_map/all_gather | solution.py:127
  96.9 17.1 %all-gather.1 = bf16[3,2048,1,64]{1,3,0,2:T(8,128)(2,1)S(1)} all-gather(bf16[3,128,1,64]{1,3,0,2:T(8,128)(2,1)S(1)} %get-tuple-element.255), channel_id=3, replica_groups=mesh['seq'=16,'head'=4,'dp'=4] {'seq'}, dimensions={1}, use_global_device_ids=true | all-gather | bytes 835584 | tf_op jit(solution)/shard_map/all_gather | solution.py:128
  155.8 6.6 convolution_convert_fusion.2
  166.5 4.9 reshape.442
  177.3 5.1 reshape.444
  182.8 266.4 %while.29 = (s32[]{:T(128)}, f32[4,3,512,64]{2,3,1,0:T(8,128)S(1)}, f32[4,3,2048,64]{2,3,1,0:T(8,128)}, f32[4,3,2048,64]{2,3,1,0:T(8,128)}, s32[4]{0:T(128)S(1)}...) while((s32[]{:T(128)}, f32[4,3,512,64]{2,3,1,0:T(8,128)S(1)}, ...), condition=%wide.region_12.14_spmd.clone, body=%wide.region_8.13_spmd.clone.sunk | while | flops 2082481152 | bytes 145174224 | solution.py:97
  184.1 9.1 %fusion.177 = (f32[3,512]{1,0:T(4,128)S(1)}, f32[3,512,2048]{2,1,0:T(8,128)}) fusion(pred[2048]{0:T(1024)(128)(4,1)S(1)} %get-tuple-element.458, bf16[3,2048,64]{1,2,0:T(8,128)(2,1)S(1)} %get-tuple-element.454, bf16[3,2048,64]{1,2,0:T(8,128)(2,1)} %get-tuple-element.453, s32[]{:T(128)S(6)} %select_n.163), kind=kOutput, calls=%fused_computation.141.clone.1 | convolution fusion | flops 415238144 | bytes 13574148 | tf_op jit(solution)/shard_map/while/body/eval_jaxpr/sub | solution.py:19
  193.2 7.3 %fusion.176 = f32[3,512,2048]{2,1,0:T(8,128)} fusion(bf16[3,2048,64]{1,2,0:T(8,128)(2,1)S(1)} %get-tuple-element.456, bf16[3,2048,64]{1,2,0:T(8,128)(2,1)} %get-tuple-element.455, s32[]{:T(128)S(6)} %select_n.163), kind=kOutput, calls=%fused_computation.49.clone.1 | convolution fusion | flops 402653184 | bytes 13565956 | tf_op jit(solution)/shard_map/while/body/eval_jaxpr/hqe,hke->hqk/dot_general | solution.py:32
  201.2 20.4 %fusion.179 = f32[4,3,2048,64]{2,3,1,0:T(8,128)} fusion(f32[4,3,2048,64]{2,3,1,0:T(8,128)} %get-tuple-element.435, s32[]{:T(128)} %get-tuple-element.433, f32[3,512,2048]{2,1,0:T(8,128)} %fusion.176, f32[3,512]{1,0:T(4,128)S(1)} %constant_dynamic-slice_fusion.2, bf16[3,2048,64]{1,2,0:T(8,128)(2,1)} %get-tuple-element.453, s32[]{:T(128)S(6)} %select_n.163, ...), kind=kOutput, calls=%fused_computation.38.clone.1 | convolution fusion | flops 427822592 | bytes 52126212 | tf_op jit(solution)/shard_map/while/body/eval_jaxpr/hqk,hqe->hke/dot_general | solution.py:38
  221.7 7.2 fusion.180
  228.8 20.6 %fusion.178 = f32[4,3,512,64]{2,3,1,0:T(8,128)S(1)} fusion(f32[4,3,512,64]{2,3,1,0:T(8,128)S(1)} %get-tuple-element.434, s32[]{:T(128)} %get-tuple-element.433, bf16[3,2048,64]{1,2,0:T(8,128)(2,1)S(1)} %get-tuple-element.454, f32[3,512,2048]{2,1,0:T(8,128)} %fusion.176, f32[3,512]{1,0:T(4,128)S(1)} %constant_dynamic-slice_fusion.2, ...), kind=kOutput, calls=%fused_computation.43.clone.1 | convolution fusion | flops 427822592 | bytes 51536384 | tf_op jit(solution)/shard_map/while/body/eval_jaxpr/hqk,hke->hqe/dot_general | solution.py:37
  250.7 9.1 %fusion.177 = (f32[3,512]{1,0:T(4,128)S(1)}, f32[3,512,2048]{2,1,0:T(8,128)}) fusion(pred[2048]{0:T(1024)(128)(4,1)S(1)} %get-tuple-element.458, bf16[3,2048,64]{1,2,0:T(8,128)(2,1)S(1)} %get-tuple-element.454, bf16[3,2048,64]{1,2,0:T(8,128)(2,1)} %get-tuple-element.453, s32[]{:T(128)S(6)} %select_n.163), kind=kOutput, calls=%fused_computation.141.clone.1 | convolution fusion | flops 415238144 | bytes 13574148 | tf_op jit(solution)/shard_map/while/body/eval_jaxpr/sub | solution.py:19
  259.9 7.3 %fusion.176 = f32[3,512,2048]{2,1,0:T(8,128)} fusion(bf16[3,2048,64]{1,2,0:T(8,128)(2,1)S(1)} %get-tuple-element.456, bf16[3,2048,64]{1,2,0:T(8,128)(2,1)} %get-tuple-element.455, s32[]{:T(128)S(6)} %select_n.163), kind=kOutput, calls=%fused_computation.49.clone.1 | convolution fusion | flops 402653184 | bytes 13565956 | tf_op jit(solution)/shard_map/while/body/eval_jaxpr/hqe,hke->hqk/dot_general | solution.py:32
  267.9 20.4 %fusion.179 = f32[4,3,2048,64]{2,3,1,0:T(8,128)} fusion(f32[4,3,2048,64]{2,3,1,0:T(8,128)} %get-tuple-element.435, s32[]{:T(128)} %get-tuple-element.433, f32[3,512,2048]{2,1,0:T(8,128)} %fusion.176, f32[3,512]{1,0:T(4,128)S(1)} %constant_dynamic-slice_fusion.2, bf16[3,2048,64]{1,2,0:T(8,128)(2,1)} %get-tuple-element.453, s32[]{:T(128)S(6)} %select_n.163, ...), kind=kOutput, calls=%fused_computation.38.clone.1 | convolution fusion | flops 427822592 | bytes 52126212 | tf_op jit(solution)/shard_map/while/body/eval_jaxpr/hqk,hqe->hke/dot_general | solution.py:38
  288.3 7.1 fusion.180
  295.4 20.6 %fusion.178 = f32[4,3,512,64]{2,3,1,0:T(8,128)S(1)} fusion(f32[4,3,512,64]{2,3,1,0:T(8,128)S(1)} %get-tuple-element.434, s32[]{:T(128)} %get-tuple-element.433, bf16[3,2048,64]{1,2,0:T(8,128)(2,1)S(1)} %get-tuple-element.454, f32[3,512,2048]{2,1,0:T(8,128)} %fusion.176, f32[3,512]{1,0:T(4,128)S(1)} %constant_dynamic-slice_fusion.2, ...), kind=kOutput, calls=%fused_computation.43.clone.1 | convolution fusion | flops 427822592 | bytes 51536384 | tf_op jit(solution)/shard_map/while/body/eval_jaxpr/hqk,hke->hqe/dot_general | solution.py:37
  317.3 9.1 %fusion.177 = (f32[3,512]{1,0:T(4,128)S(1)}, f32[3,512,2048]{2,1,0:T(8,128)}) fusion(pred[2048]{0:T(1024)(128)(4,1)S(1)} %get-tuple-element.458, bf16[3,2048,64]{1,2,0:T(8,128)(2,1)S(1)} %get-tuple-element.454, bf16[3,2048,64]{1,2,0:T(8,128)(2,1)} %get-tuple-element.453, s32[]{:T(128)S(6)} %select_n.163), kind=kOutput, calls=%fused_computation.141.clone.1 | convolution fusion | flops 415238144 | bytes 13574148 | tf_op jit(solution)/shard_map/while/body/eval_jaxpr/sub | solution.py:19
  326.4 7.3 %fusion.176 = f32[3,512,2048]{2,1,0:T(8,128)} fusion(bf16[3,2048,64]{1,2,0:T(8,128)(2,1)S(1)} %get-tuple-element.456, bf16[3,2048,64]{1,2,0:T(8,128)(2,1)} %get-tuple-element.455, s32[]{:T(128)S(6)} %select_n.163), kind=kOutput, calls=%fused_computation.49.clone.1 | convolution fusion | flops 402653184 | bytes 13565956 | tf_op jit(solution)/shard_map/while/body/eval_jaxpr/hqe,hke->hqk/dot_general | solution.py:32
  334.4 20.4 %fusion.179 = f32[4,3,2048,64]{2,3,1,0:T(8,128)} fusion(f32[4,3,2048,64]{2,3,1,0:T(8,128)} %get-tuple-element.435, s32[]{:T(128)} %get-tuple-element.433, f32[3,512,2048]{2,1,0:T(8,128)} %fusion.176, f32[3,512]{1,0:T(4,128)S(1)} %constant_dynamic-slice_fusion.2, bf16[3,2048,64]{1,2,0:T(8,128)(2,1)} %get-tuple-element.453, s32[]{:T(128)S(6)} %select_n.163, ...), kind=kOutput, calls=%fused_computation.38.clone.1 | convolution fusion | flops 427822592 | bytes 52126212 | tf_op jit(solution)/shard_map/while/body/eval_jaxpr/hqk,hqe->hke/dot_general | solution.py:38
  354.8 7.1 fusion.180
  361.9 20.6 %fusion.178 = f32[4,3,512,64]{2,3,1,0:T(8,128)S(1)} fusion(f32[4,3,512,64]{2,3,1,0:T(8,128)S(1)} %get-tuple-element.434, s32[]{:T(128)} %get-tuple-element.433, bf16[3,2048,64]{1,2,0:T(8,128)(2,1)S(1)} %get-tuple-element.454, f32[3,512,2048]{2,1,0:T(8,128)} %fusion.176, f32[3,512]{1,0:T(4,128)S(1)} %constant_dynamic-slice_fusion.2, ...), kind=kOutput, calls=%fused_computation.43.clone.1 | convolution fusion | flops 427822592 | bytes 51536384 | tf_op jit(solution)/shard_map/while/body/eval_jaxpr/hqk,hke->hqe/dot_general | solution.py:37
  383.8 9.1 %fusion.177 = (f32[3,512]{1,0:T(4,128)S(1)}, f32[3,512,2048]{2,1,0:T(8,128)}) fusion(pred[2048]{0:T(1024)(128)(4,1)S(1)} %get-tuple-element.458, bf16[3,2048,64]{1,2,0:T(8,128)(2,1)S(1)} %get-tuple-element.454, bf16[3,2048,64]{1,2,0:T(8,128)(2,1)} %get-tuple-element.453, s32[]{:T(128)S(6)} %select_n.163), kind=kOutput, calls=%fused_computation.141.clone.1 | convolution fusion | flops 415238144 | bytes 13574148 | tf_op jit(solution)/shard_map/while/body/eval_jaxpr/sub | solution.py:19
  392.9 7.3 %fusion.176 = f32[3,512,2048]{2,1,0:T(8,128)} fusion(bf16[3,2048,64]{1,2,0:T(8,128)(2,1)S(1)} %get-tuple-element.456, bf16[3,2048,64]{1,2,0:T(8,128)(2,1)} %get-tuple-element.455, s32[]{:T(128)S(6)} %select_n.163), kind=kOutput, calls=%fused_computation.49.clone.1 | convolution fusion | flops 402653184 | bytes 13565956 | tf_op jit(solution)/shard_map/while/body/eval_jaxpr/hqe,hke->hqk/dot_general | solution.py:32
  400.9 20.2 %fusion.179 = f32[4,3,2048,64]{2,3,1,0:T(8,128)} fusion(f32[4,3,2048,64]{2,3,1,0:T(8,128)} %get-tuple-element.435, s32[]{:T(128)} %get-tuple-element.433, f32[3,512,2048]{2,1,0:T(8,128)} %fusion.176, f32[3,512]{1,0:T(4,128)S(1)} %constant_dynamic-slice_fusion.2, bf16[3,2048,64]{1,2,0:T(8,128)(2,1)} %get-tuple-element.453, s32[]{:T(128)S(6)} %select_n.163, ...), kind=kOutput, calls=%fused_computation.38.clone.1 | convolution fusion | flops 427822592 | bytes 52126212 | tf_op jit(solution)/shard_map/while/body/eval_jaxpr/hqk,hqe->hke/dot_general | solution.py:38
  421.2 7.2 fusion.180
  428.4 20.6 %fusion.178 = f32[4,3,512,64]{2,3,1,0:T(8,128)S(1)} fusion(f32[4,3,512,64]{2,3,1,0:T(8,128)S(1)} %get-tuple-element.434, s32[]{:T(128)} %get-tuple-element.433, bf16[3,2048,64]{1,2,0:T(8,128)(2,1)S(1)} %get-tuple-element.454, f32[3,512,2048]{2,1,0:T(8,128)} %fusion.176, f32[3,512]{1,0:T(4,128)S(1)} %constant_dynamic-slice_fusion.2, ...), kind=kOutput, calls=%fused_computation.43.clone.1 | convolution fusion | flops 427822592 | bytes 51536384 | tf_op jit(solution)/shard_map/while/body/eval_jaxpr/hqk,hke->hqe/dot_general | solution.py:37
  450.4 7.8 %fusion.90 = f32[3,128,64]{2,1,0:T(8,128)} fusion(f32[3,128,2048]{2,1,0:T(8,128)} %fusion.101, f32[3,128]{1,0:T(4,128)S(1)} %copy-done.40, bf16[3,2048,1,64]{1,3,0,2:T(8,128)(2,1)} %copy-done.17, f32[3,128,2048]{2,1,0:T(8,128)} %copy-done.9, f32[3,128]{1,0:T(4,128)S(1)} %copy-done.37, f32[3,128]{1,0:T(4,128)S(1)} %copy-done.31), kind=kOutput, calls=%fused_computation.79 | convolution fusion | flops 108530048 | bytes 7180800 | tf_op jit(solution)/shard_map/hqk,hke->hqe/dot_general | solution.py:37
  468.9 4.7 reduce_sum.83
  485.2 6.4 add_convert_fusion
  499.8 174.1 %all-reduce.2.cloned.1.call-done = f32[192,768]{1,0:T(8,128)} async-done(((f32[192,768]{1,0:T(8,128)}), f32[192,768]{1,0:T(8,128)}) %all-reduce.2.cloned.1.call-update) | async-done | bytes 589840 | tf_op jit(solution)/shard_map/psum | solution.py:150
  675.8 41.6 %reduce-scatter.10.cloned.1.call-done = bf16[192,2048]{1,0:T(8,128)(2,1)} async-done(((bf16[768,2048]{1,0:T(8,128)(2,1)}), bf16[192,2048]{1,0:T(8,128)(2,1)}) %reduce-scatter.10.cloned.1.call-update) | async-done | bytes 786448
  (213 shorter events, 155.8 us)
Async XLA Ops:
  7.2 124.9 %copy-start = (bf16[192,768]{1,0:T(8,128)(2,1)S(1)}, bf16[192,768]{1,0:T(8,128)(2,1)}, u32[]{:S(2)}) copy-start(bf16[192,768]{1,0:T(8,128)(2,1)} %param.17) | copy-start | bytes 884740
  7.2 124.9 %all-gather.5.cloned.1.call-start = ((), (), s32[]{:S(2)}) async-start(), calls=%async_computation.4 | async-start | bytes 3932160 | tf_op jit(solution)/shard_map/all_gather | solution.py:144
  7.9 465.7 %reduce-scatter.12.cloned.1.call-start = ((), (), s32[]{:S(2)}) async-start(), calls=%async_computation.6 | async-start | bytes 1114112
  53.5 7.2 copy-start.14
  58.9 6.4 copy-start.41
  71.0 25.3 %copy-start.42 = (pred[3]{0:T(512)(128)(4,1)}, pred[3]{0:T(512)(128)(4,1)S(1)}, u32[]{:S(2)}) copy-start(pred[3]{0:T(512)(128)(4,1)S(1)} %and_bitcast_fusion) | copy-start | bytes 13
  96.3 18.4 %copy-start.9 = (f32[3,128,2048]{2,1,0:T(8,128)}, f32[3,128,2048]{2,1,0:T(8,128)S(1)}, u32[]{:S(2)}) copy-start(f32[3,128,2048]{2,1,0:T(8,128)S(1)} %get-tuple-element.257) | copy-start | bytes 9437188
  96.3 30.6 %copy-start.29 = (f32[3,128]{1,0:T(4,128)}, f32[3,128]{1,0:T(4,128)S(1)}, u32[]{:S(2)}) copy-start(f32[3,128]{1,0:T(4,128)S(1)} %get-tuple-element.256) | copy-start | bytes 4612
  96.9 17.9 %copy-start.35 = (f32[3,128]{1,0:T(4,128)}, f32[3,128]{1,0:T(4,128)S(1)}, u32[]{:S(2)}) copy-start(f32[3,128]{1,0:T(4,128)S(1)} %fusion.83) | copy-start | bytes 4612
  119.1 15.7 %copy-start.4 = (f32[3,2048,64]{1,2,0:T(8,128)}, f32[3,2048,64]{1,2,0:T(8,128)S(1)}, u32[]{:S(2)}) copy-start(f32[3,2048,64]{1,2,0:T(8,128)S(1)} %copy.74) | copy-start | bytes 4718596
  121.2 15.5 %copy-start.6 = (f32[4,3,8,8,512]{4,3,0,2,1:T(8,128)}, f32[4,3,8,8,512]{4,3,0,2,1:T(8,128)S(1)}, u32[]{:S(2)}) copy-start(f32[4,3,8,8,512]{4,3,0,2,1:T(8,128)S(1)} %copy.100) | copy-start | bytes 4718596
  123.7 14.6 %copy-start.18 = (f32[3,2048]{1,0:T(4,128)}, f32[3,2048]{1,0:T(4,128)S(1)}, u32[]{:S(2)}) copy-start(f32[3,2048]{1,0:T(4,128)S(1)} %reshape.364) | copy-start | bytes 73732
  130.1 9.7 %copy-start.25 = (f32[2048]{0:T(1024)}, f32[2048]{0:T(1024)S(1)}, u32[]{:S(2)}) copy-start(f32[2048]{0:T(1024)S(1)} %fusion.116) | copy-start | bytes 24580
  139.8 3.9 copy-start.21
  139.8 3.9 copy-start.23
  139.8 6.7 copy-start.27
  139.8 6.7 copy-start.33
  142.2 4.3 copy-start.28
  143.7 12.1 %copy-start.10 = (f32[3,128,2048]{2,1,0:T(8,128)S(1)}, f32[3,128,2048]{2,1,0:T(8,128)}, u32[]{:S(2)}) copy-start(f32[3,128,2048]{2,1,0:T(8,128)} %copy-done.9) | copy-start | bytes 9437188
  143.7 12.1 %copy-start.30 = (f32[3,128]{1,0:T(4,128)S(1)}, f32[3,128]{1,0:T(4,128)}, u32[]{:S(2)}) copy-start(f32[3,128]{1,0:T(4,128)} %copy-done.29) | copy-start | bytes 4612
  162.4 9.1 %copy-start.20 = (bf16[3,128,64]{1,2,0:T(8,128)(2,1)S(1)}, bf16[3,128,64]{1,2,0:T(8,128)(2,1)}, u32[]{:S(2)}) copy-start(bf16[3,128,64]{1,2,0:T(8,128)(2,1)} %gather_fusion) | copy-start | bytes 147460
  162.4 9.1 %copy-start.36 = (f32[3,128]{1,0:T(4,128)S(1)}, f32[3,128]{1,0:T(4,128)}, u32[]{:S(2)}) copy-start(f32[3,128]{1,0:T(4,128)} %copy-done.35) | copy-start | bytes 4612
  162.4 9.1 %copy-start.38 = (pred[3]{0:T(512)(128)(4,1)S(1)}, pred[3]{0:T(512)(128)(4,1)}, u32[]{:S(2)}) copy-start(pred[3]{0:T(512)(128)(4,1)} %compare_and_fusion) | copy-start | bytes 13
  171.4 307.2 %reduce-scatter.14.cloned.1.call-start = ((), (), s32[]{:S(2)}) async-start(), calls=%async_computation.7 | async-start | bytes 1114112
  177.3 5.5 copy-start.1
  177.3 5.5 copy-start.3
  182.4 491.4 %all-reduce.2.cloned.1.call-start = ((), (), s32[]{:S(2)}) async-start(), calls=%async_computation.3 | async-start | bytes 1179648 | tf_op jit(solution)/shard_map/psum | solution.py:150
  182.8 267.6 %copy-start.31 = (f32[3,128]{1,0:T(4,128)S(1)}, f32[3,128]{1,0:T(4,128)}, u32[]{:S(2)}) copy-start(f32[3,128]{1,0:T(4,128)} %copy-done.29) | copy-start | bytes 4612
  182.8 267.6 %copy-start.37 = (f32[3,128]{1,0:T(4,128)S(1)}, f32[3,128]{1,0:T(4,128)}, u32[]{:S(2)}) copy-start(f32[3,128]{1,0:T(4,128)} %copy-done.35) | copy-start | bytes 4612
  182.8 267.6 %copy-start.40 = (f32[3,128]{1,0:T(4,128)S(1)}, f32[3,128]{1,0:T(4,128)}, u32[]{:S(2)}) copy-start(f32[3,128]{1,0:T(4,128)} %copy-done.39) | copy-start | bytes 4612
  485.2 7.3 %copy-start.8 = (bf16[1,768,2048]{2,1,0:T(8,128)(2,1)S(1)}, bf16[1,768,2048]{2,1,0:T(8,128)(2,1)}, u32[]{:S(2)}) copy-start(bf16[1,768,2048]{2,1,0:T(8,128)(2,1)} %all-gather.5.cloned.1.call-done) | copy-start | bytes 9437188
  494.6 222.8 %reduce-scatter.10.cloned.1.call-start = ((), (), s32[]{:S(2)}) async-start(), calls=%async_computation.5 | async-start | bytes 3932160
  (19 other events, 50.1 us)
Sparse Core Ops, SparseCore 0:
  9.8 45.8 all-gather.4
  171.6 52.7 reduce-scatter.11
  227.0 55.9 reduce-scatter.13
  494.7 179.1 all-reduce.1
  676.2 41.0 reduce-scatter.9
where the time goes:
time: 736 us; the launch traced here: 727 us
  matrix products  312 us (42%)
  waiting for transfers between devices  216 us (29%)
  local copies, waits for them, and re-layouts  93.2 us (13%)
  other arithmetic  43.1 us (6%)
  blocking collectives  40.6 us (6%)
  between operations  15.2 us (2%)
    psum x1, waiting for transfers between devices, shards(): weight_grad = lax.psum(weight_part, ('seq', 'dp')) * grad_scale  174 us
    dot_general x5, matrix products, attend_back(): jnp.einsum('hqk,hke->hqe', grad_score, k_rows, preferred_element_type=jnp...  90.4 us
    dot_general x5, matrix products, attend_back(): jnp.einsum('hqk,hqe->hke', grad_score, q_rows, preferred_element_type=jnp...  88.1 us
    unnamed x8, waiting for transfers between devices  42.4 us
    sub x4, matrix products, attend(): expo_terms = jnp.exp(scores - row_top)  36.5 us
    dot_general x5, matrix products, attend_back(): jnp.einsum('hqe,hke->hqk', grad_bf, v_rows, preferred_element_type=jnp.fl...  32.8 us
    dot_general x5, matrix products, attend_back(): jnp.einsum('hqk,hqe->hke', weights, grad_bf, preferred_element_type=jnp.f...  30.4 us
    unnamed x95, local copies, waits for them, and re-layouts  29.8 us
  transfers between devices with their start and end apart: 5, of which 2 were waited for; matrix products, arithmetic and copies ran while one was open for 53% of the time, Pallas kernels for 0%

commit v1 on v0

v1 whole, which is shorter than its diff:
```python
import math

import jax
import jax.numpy as jnp
from jax import lax
from jax.experimental import pallas as pl
from jax.experimental.pallas import tpu as pltpu
from jax.sharding import PartitionSpec as P

SEL = 2048
HD = 64
NEGATIVE = -1e30
BF = jnp.bfloat16
F32 = jnp.float32
QB = 512
VMEM_BYTES = 60 * 2**20


def dot(a, b, ca, cb):
    return lax.dot_general(a, b, (((ca,), (cb,)), ((), ())), preferred_element_type=F32)


def split2(x):
    hi = x.astype(BF)
    return hi, (x - hi.astype(F32)).astype(BF)


def split3(x):
    hi = x.astype(BF)
    rest = x - hi.astype(F32)
    mid = rest.astype(BF)
    return hi, mid, (rest - mid.astype(F32)).astype(BF)


def call(kern, name, grid, in_specs, out_specs, out_shape, scratch=(), flops=0, nbytes=0):
    return pl.pallas_call(
        kern,
        name=name,
        grid=grid,
        in_specs=in_specs,
        out_specs=out_specs,
        out_shape=out_shape,
        scratch_shapes=list(scratch),
        compiler_params=pltpu.CompilerParams(vmem_limit_bytes=VMEM_BYTES),
        cost_estimate=pl.CostEstimate(flops=flops, bytes_accessed=nbytes, transcendentals=0),
    )


SMEM = pl.BlockSpec(memory_space=pltpu.SMEM)
WHOLE = pl.BlockSpec(memory_space=pltpu.VMEM)


def sel_matrix(off, rate, rows, cols):
    pos = lax.broadcasted_iota(jnp.int32, (rows, cols), 0)
    num = lax.broadcasted_iota(jnp.int32, (rows, cols), 1)
    return jnp.where(pos == num * rate + off, 1.0, 0.0).astype(BF)


def place_matrix(off, rate, start, rows, cols):
    num = lax.broadcasted_iota(jnp.int32, (rows, cols), 0)
    pos = lax.broadcasted_iota(jnp.int32, (rows, cols), 1) + start
    return jnp.where(pos == num * rate + off, 1.0, 0.0).astype(BF)


def pick_kernel(rate, offs, q, k, v, qp, kvp):
    heads = q.shape[0] // HD
    picks = qp.shape[1]
    for h in range(heads):
        rows = slice(h * HD, (h + 1) * HD)
        sel = sel_matrix(offs[h], rate, q.shape[1], picks)
        got = dot(jnp.concatenate([q[rows, :], k[rows, :], v[rows, :]], axis=0), sel, 1, 0)
        got = got.astype(BF)
        qp[rows, :] = got[:HD]
        kvp[rows, :] = got[HD : 2 * HD]
        kvp[heads * HD + h * HD : heads * HD + (h + 1) * HD, :] = got[2 * HD :]


def stack_rows(count, parts):
    row = lax.broadcasted_iota(jnp.int32, (count, parts[0].shape[1]), 0)
    out = jnp.zeros(row.shape, F32)
    for i, part in enumerate(parts):
        out = jnp.where(row == i, part.astype(F32), out)
    return out.astype(BF)


def fwd_kernel(info, q, k, v, e_out, out, stats, kt, s_buf):
    tok = k.shape[1]
    qb = q.shape[1]

    @pl.when(pl.program_id(1) == 0)
    def _():
        pos = lax.broadcasted_iota(jnp.int32, (HD, tok), 1) + info[1]
        row = lax.broadcasted_iota(jnp.int32, (HD, tok), 0)
        bias = jnp.where((row == 0) & (pos >= info[0]), NEGATIVE, 0.0).astype(BF)
        kt[...] = jnp.concatenate([k[...], bias], axis=0).T

    one = jnp.where(lax.broadcasted_iota(jnp.int32, (HD, qb), 0) == 0, 1.0, 0.0).astype(BF)
    qa = jnp.concatenate([q[...] * jnp.asarray(0.125, BF), one], axis=0)
    row16 = lax.broadcasted_iota(jnp.int32, (16, tok), 0)
    va = jnp.concatenate([v[...], jnp.where(row16 == 0, 1.0, 0.0).astype(BF)], axis=0)
    ck = 256
    half = 256
    for c0 in range(0, qb, half):
        cols = slice(c0, c0 + half)
        top = None
        for i in range(0, tok, ck):
            s = dot(kt[i : i + ck, :], qa[:, cols], 1, 0)
            s_buf[i : i + ck, cols] = s
            part = jnp.max(s.reshape(ck // 8, 8, half), axis=0)
            top = part if top is None else jnp.maximum(top, part)
        m = jnp.max(top, axis=0, keepdims=True)
        acc = None
        for i in range(0, tok, ck):
            e = jnp.exp(s_buf[i : i + ck, cols] - m).astype(BF)
            e_out[0, i : i + ck, cols] = e
            part = dot(va[:, i : i + ck], e, 1, 0)
            acc = part if acc is None else acc + part
        t = acc[HD : HD + 1]
        rt = 1.0 / t
        out[:, cols] = acc[:HD] * rt
        stats[0, :, cols] = jnp.concatenate(
            [m + jnp.log(t), rt, jnp.zeros((6, half), F32)], axis=0
        )


def mida_kernel(rate, info, offs, qp, kvf, out_a, stats, w, terms, attn, shares, out_b, pf):
    heads = stats.shape[0]
    tok = out_a.shape[1]
    picks = qp.shape[1]
    ranks = kvf.shape[0]
    width = heads * HD
    length, start = info[0], info[1]
    pos = lax.broadcasted_iota(jnp.int32, (1, tok), 1) + start
    keep = jnp.where(pos < length, 1.0, 0.0)
    key_pos = lax.broadcasted_iota(jnp.int32, (ranks * picks, 1), 0) * rate
    for h in range(heads):
        rows = slice(h * HD, (h + 1) * HD)
        off = offs[h]
        kf = jnp.concatenate([kvf[r, rows, :] for r in range(ranks)], axis=1)
        vf = jnp.concatenate(
            [kvf[r, width + h * HD : width + (h + 1) * HD, :] for r in range(ranks)], axis=1
        )
        s = dot(kf, qp[rows, :] * jnp.asarray(0.125, BF), 0, 0)
        s = jnp.where(key_pos + off < length, s, NEGATIVE)
        m = jnp.max(s, axis=0, keepdims=True)
        e = jnp.exp(s - m)
        t = jnp.sum(e, axis=0, keepdims=True)
        p = (e * (1.0 / t)).astype(BF)
        pf[h] = p
        ob = dot(vf, p, 1, 0)
        out_b[rows, :] = ob
        lse_b = m + jnp.log(t)
        place = place_matrix(off, rate, 0, picks, tok)
        l_hi, l_mid, l_lo = split3(lse_b)
        o_hi, o_lo = split2(ob)
        stack = jnp.concatenate([o_hi, o_lo, stack_rows(16, [l_hi, l_mid, l_lo])], axis=0)
        spread = dot(stack, place, 1, 0)
        of = spread[:HD] + spread[HD : 2 * HD]
        lf = spread[128:129] + spread[129:130] + spread[130:131]
        here = lax.broadcasted_iota(jnp.int32, (1, tok), 1)
        chosen = (here % rate) == off
        lf = jnp.where(chosen, lf, NEGATIVE)
        gap = stats[h, 0:1, :] - lf
        sa = 1.0 / (1.0 + jnp.exp(-gap))
        sb = 1.0 / (1.0 + jnp.exp(gap))
        shares[h] = jnp.concatenate([sa, sb, jnp.zeros((6, tok), F32)], axis=0)
        attn[rows, :] = ((sa * out_a[rows, :] + sb * of) * keep).astype(BF)
    terms[...] = dot(w[...], attn[...], 0, 0).astype(BF)


def midb_kernel(
    rate, info, offs, cot, w, attn, shares, out_a, stats, out_b, pf, qp, kvf,
    dob, dkv, dqf, wpart,
):
    heads = stats.shape[0]
    tok = out_a.shape[1]
    picks = qp.shape[1]
    ranks = kvf.shape[0]
    width = heads * HD
    length, start = info[0], info[1]
    pos = lax.broadcasted_iota(jnp.int32, (1, tok), 1) + start
    keep = jnp.where(pos < length, 1.0, 0.0).astype(BF)
    wpart[...] = dot(attn[...], cot[...], 1, 1)
    for h in range(heads):
        rows = slice(h * HD, (h + 1) * HD)
        off = offs[h]
        g_bf = dot(w[rows, :], cot[...], 1, 0).astype(BF) * keep
        g = g_bf.astype(F32)
        place = place_matrix(off, rate, 0, picks, tok)
        sel = sel_matrix(off, rate, tok, picks)
        ob = out_b[rows, :]
        o_hi, o_lo = split2(ob)
        spread = dot(jnp.concatenate([o_hi, o_lo], axis=0), place, 1, 0)
        of = spread[:HD] + spread[HD:]
        sa, sb = shares[h, 0:1, :], shares[h, 1:2, :]
        oa = out_a[rows, :]
        dlse = sa * sb * jnp.sum(g * (oa - of), axis=0, keepdims=True)
        rt = stats[h, 1:2, :]
        dout = sa * g
        delta = jnp.sum(dout.astype(BF).astype(F32) * oa, axis=0, keepdims=True)
        c_hi, c_lo = split2((dlse - delta) * rt)
        dob[h] = jnp.concatenate(
            [(dout * rt).astype(BF), stack_rows(HD, [c_hi, c_lo])], axis=0
        )
        s_hi, s_lo = split2(sb)
        l_hi, l_lo = split2(dlse)
        picked = dot(
            jnp.concatenate([g_bf, stack_rows(16, [s_hi, s_lo, l_hi, l_lo])], axis=0), sel, 1, 0
        )
        sb_p = picked[64:65] + picked[65:66]
        dlse_p = -(picked[66:67] + picked[67:68])
        do_b = (sb_p * picked[:HD]).astype(BF)
        delta_b = jnp.sum(do_b.astype(F32) * ob, axis=0, keepdims=True)
        kf = jnp.concatenate([kvf[r, rows, :] for r in range(ranks)], axis=1)
        vf = jnp.concatenate(
            [kvf[r, width + h * HD : width + (h + 1) * HD, :] for r in range(ranks)], axis=1
        )
        dp = dot(vf, do_b, 0, 0) + (dlse_p - delta_b)
        p = pf[h]
        ds = (p.astype(F32) * dp * 0.125).astype(BF)
        dqf[rows, :] = dot(kf, ds, 1, 0)
        dk = dot(qp[rows, :], ds, 1, 1).astype(BF)
        dv = dot(do_b, p, 1, 1).astype(BF)
        for r in range(ranks):
            cols = slice(r * picks, (r + 1) * picks)
            dkv[r, rows, :] = dk[:, cols]
            dkv[r, width + h * HD : width + (h + 1) * HD, :] = dv[:, cols]


def bwd_kernel(rate, offs, e, dob, q, k, v, dqf, dq, dk, dv, vt):
    tok = k.shape[1]
    qb = q.shape[1]
    step = pl.program_id(1)

    @pl.when(step == 0)
    def _():
        row = lax.broadcasted_iota(jnp.int32, (HD, tok), 0)
        ones = jnp.where(row < 2, 1.0, 0.0).astype(BF)
        vt[...] = jnp.concatenate([v[...], ones], axis=0).T
        dk[...] = jnp.zeros_like(dk)
        dv[...] = jnp.zeros_like(dv)

    ck = 256
    do = dob[0, :HD, :]
    acc = None
    for i in range(0, tok, ck):
        dp = dot(vt[i : i + ck, :], dob[0], 1, 0)
        ei = e[0, i : i + ck, :]
        ds = (ei.astype(F32) * dp).astype(BF)
        part = dot(k[:, i : i + ck], ds, 1, 0)
        acc = part if acc is None else acc + part
        dk[:, i : i + ck] += dot(q[...], ds, 1, 1)
        dv[:, i : i + ck] += dot(do, ei, 1, 1)
    place = place_matrix(offs[pl.program_id(0)], rate, step * qb, dqf.shape[1], qb)
    d_hi, d_lo = split2(dqf[...])
    spread = dot(jnp.concatenate([d_hi, d_lo], axis=0), place, 1, 0)
    dq[...] = (acc * 0.125 + spread[:HD] + spread[HD:]).astype(BF)


def merge_kernel(rate, offs, dk, dv, far, kg, vg):
    heads = dk.shape[0] // HD
    width = heads * HD
    tok = dk.shape[1]
    picks = far.shape[2]
    total = far[0].astype(F32)
    for r in range(1, far.shape[0]):
        total = total + far[r].astype(F32)
    for h in range(heads):
        rows = slice(h * HD, (h + 1) * HD)
        place = place_matrix(offs[h], rate, 0, picks, tok)
        both = jnp.concatenate(
            [total[rows], total[width + h * HD : width + (h + 1) * HD]], axis=0
        )
        hi, lo = split2(both)
        spread = dot(jnp.concatenate([hi, lo], axis=0), place, 1, 0)
        near_k = dk[rows, :] * 0.125
        kg[rows, :] = (near_k + spread[:HD] + spread[2 * HD : 3 * HD]).astype(BF)
        vg[rows, :] = (dv[rows, :] + spread[HD : 2 * HD] + spread[3 * HD :]).astype(BF)


SDS = jax.ShapeDtypeStruct


def pick(rate, offs, q, k, v, picks):
    rows, tok = q.shape
    return call(
        lambda *r: pick_kernel(rate, *r), "pick", (), [SMEM, WHOLE, WHOLE, WHOLE], [WHOLE, WHOLE],
        [SDS((rows, picks), BF), SDS((2 * rows, picks), BF)],
        flops=6 * rows * tok * picks, nbytes=6 * rows * tok,
    )(offs, q, k, v)


def forward(info, q, k, v):
    rows, tok = q.shape
    heads = rows // HD
    qb = min(QB, tok)
    by_q = pl.BlockSpec((HD, qb), lambda h, j: (h, j))
    whole = pl.BlockSpec((HD, tok), lambda h, j: (h, 0))
    return call(
        fwd_kernel, "fwd", (heads, tok // qb), [SMEM, by_q, whole, whole],
        [
            pl.BlockSpec((1, tok, qb), lambda h, j: (h, 0, j)),
            by_q,
            pl.BlockSpec((1, 8, qb), lambda h, j: (h, 0, j)),
        ],
        [SDS((heads, tok, tok), BF), SDS((rows, tok), F32), SDS((heads, 8, tok), F32)],
        scratch=[pltpu.VMEM((tok, 2 * HD), BF), pltpu.VMEM((tok, qb), F32)],
        flops=4 * rows * tok * tok, nbytes=2 * heads * tok * tok,
    )(info, q, k, v)


def mid_a(rate, info, offs, qp, kvf, out_a, stats, w):
    rows, tok = out_a.shape
    heads = rows // HD
    picks = qp.shape[1]
    return call(
        lambda *r: mida_kernel(rate, *r), "mida", (), [SMEM, SMEM] + [WHOLE] * 5, [WHOLE] * 5,
        [
            SDS((w.shape[1], tok), BF), SDS((rows, tok), BF), SDS((heads, 8, tok), F32),
            SDS((rows, picks), F32), SDS((heads, kvf.shape[0] * picks, picks), BF),
        ],
        flops=2 * rows * tok * w.shape[1], nbytes=2 * tok * w.shape[1],
    )(info, offs, qp, kvf, out_a, stats, w)


def mid_b(rate, info, offs, cot, w, attn, shares, out_a, stats, out_b, pf, qp, kvf):
    rows, tok = out_a.shape
    heads = rows // HD
    picks = qp.shape[1]
    return call(
        lambda *r: midb_kernel(rate, *r), "midb", (), [SMEM, SMEM] + [WHOLE] * 10, [WHOLE] * 4,
        [
            SDS((heads, 2 * HD, tok), BF), SDS(kvf.shape, BF), SDS((rows, picks), F32),
            SDS(w.shape, F32),
        ],
        flops=4 * rows * tok * w.shape[1], nbytes=2 * tok * w.shape[1],
    )(info, offs, cot, w, attn, shares, out_a, stats, out_b, pf, qp, kvf)


def backward(rate, offs, e, dob, q, k, v, dqf):
    rows, tok = q.shape
    heads = rows // HD
    qb = min(QB, tok)
    by_q = pl.BlockSpec((HD, qb), lambda h, j: (h, j))
    whole = pl.BlockSpec((HD, tok), lambda h, j: (h, 0))
    return call(
        lambda *r: bwd_kernel(rate, *r), "bwd", (heads, tok // qb),
        [
            SMEM, pl.BlockSpec((1, tok, qb), lambda h, j: (h, 0, j)),
            pl.BlockSpec((1, 2 * HD, qb), lambda h, j: (h, 0, j)),
            by_q, whole, whole, pl.BlockSpec((HD, dqf.shape[1]), lambda h, j: (h, 0)),
        ],
        [by_q, whole, whole],
        [SDS((rows, tok), BF), SDS((rows, tok), F32), SDS((rows, tok), F32)],
        scratch=[pltpu.VMEM((tok, 2 * HD), BF)],
        flops=8 * rows * tok * tok, nbytes=2 * heads * tok * tok,
    )(offs, e, dob, q, k, v, dqf)


def merge(rate, offs, dk, dv, far):
    rows, tok = dk.shape
    return call(
        lambda *r: merge_kernel(rate, *r), "merge", (), [SMEM] + [WHOLE] * 3, [WHOLE] * 2,
        [SDS((rows, tok), BF)] * 2,
        flops=8 * rows * tok * far.shape[2], nbytes=12 * rows * tok,
    )(offs, dk, dv, far)


def shards(queries, keys, values, cotangent, w_out, lengths, offsets):
    rows, tok = queries.shape[1:]
    seq_count = lax.axis_size("seq")
    rate = tok * seq_count // SEL
    picks = tok // rate
    info = jnp.stack([lengths[0], lax.axis_index("seq").astype(jnp.int32) * tok])
    q, k, v = queries[0], keys[0], values[0]
    cot = lax.all_gather(cotangent[0], "head", axis=0, tiled=True)
    qp, kvp = pick(rate, offsets, q, k, v, picks)
    kvf = lax.all_gather(kvp, "seq")
    e, out_a, stats = forward(info, q, k, v)
    terms, attn, shares, out_b, pf = mid_a(rate, info, offsets, qp, kvf, out_a, stats, w_out)
    mixed = lax.psum_scatter(terms, "head", scatter_dimension=0, tiled=True)
    dob, dkv, dqf, wpart = mid_b(
        rate, info, offsets, cot, w_out, attn, shares, out_a, stats, out_b, pf, qp, kvf
    )
    far = lax.all_to_all(dkv, "seq", 0, 0)
    grad_scale = 1.0 / math.sqrt(tok * seq_count * lax.axis_size("dp"))
    pieces = wpart.astype(BF).reshape(seq_count, rows // seq_count, w_out.shape[1])
    mine = jnp.sum(lax.all_to_all(pieces, "seq", 0, 0).astype(F32), axis=0)
    mine = lax.psum(mine, "dp") * grad_scale
    weight_grad = lax.all_gather(mine, "seq", axis=0, tiled=True)
    dq, dk, dv = backward(rate, offsets, e, dob, q, k, v, dqf)
    kg, vg = merge(rate, offsets, dk, dv, far)
    return (mixed[None], dq[None], kg[None], vg[None], weight_grad)


def solution(mesh):
    full = P("dp", "head", "seq")
    return jax.shard_map(
        shards,
        mesh=mesh,
        in_specs=(full, full, full, full, P("head", None), P("dp"), P("head")),
        out_specs=(full, full, full, full, P("head", None)),
        check_vma=False,
    )
```

time: 736 us -> 224 us (0.30); the launches traced: 727 us -> 224 us
  matrix products: 312 us -> 0 us
  waiting for transfers between devices: 216 us -> 45.8 us
  Pallas kernels: 0 us -> 97.8 us
  local copies, waits for them, and re-layouts: 93.2 us -> 2.09 us
  other arithmetic: 43.1 us -> 1.76 us
  blocking collectives: 40.6 us -> 57.8 us
    dot_general x33 -> x0, matrix products: 276 us -> none  [the longest x5 90.4 us: attend_back(): jnp.einsum('hqk,hke->hqe', grad_score, k_rows, preferred_element_type=jnp...]
    psum x1 -> x0, waiting for transfers between devices: 174 us -> none  [shards(): weight_grad = lax.psum(weight_part, ('seq', 'dp')) * grad_scale]
    pallas_call x0 -> x6, Pallas kernels: none -> 97.8 us  [the longest x1 39.7 us: backward(): call(lambda *r: bwd_kernel(rate, *r), 'bwd', (heads, tok // qb), [SMEM, p...]
    all_gather x1 -> x2, waiting for transfers between devices: 0.01 us -> 45 us  [the longest x1 33.5 us: shards(): cot = lax.all_gather(cotangent[0], 'head', axis=0, tiled=True)]
    unnamed x8 -> x3, waiting for transfers between devices: 42.4 us -> 0.73 us
    sub x4 -> x0, matrix products: 36.5 us -> none  [attend(): expo_terms = jnp.exp(scores - row_top)]
    unnamed x95 -> x3, local copies, waits for them, and re-layouts: 29.8 us -> 2.03 us
    reduce_sum x8 -> x1, other arithmetic: 22.2 us -> 0.07 us  [shards(): mine = jnp.sum(lax.all_to_all(pieces, 'seq', 0, 0).astype(F32), axis=0)]
  transfers between devices with their start and end apart: 5 -> 4, of which waited for: 2 -> 2; matrix products, arithmetic and copies ran while one was open for 53% -> 1% of each run, Pallas kernels for 0% -> 42%
where the time goes in v1:
time: 224 us
  Pallas kernels  97.8 us (44%)
  blocking collectives  57.8 us (26%)
  waiting for transfers between devices  45.8 us (20%)
  between operations  14.4 us (6%)
  starting transfers between devices  3.95 us (2%)
    pallas_call x1, Pallas kernels, backward(): call(lambda *r: bwd_kernel(rate, *r), 'bwd', (heads, tok // qb), [SMEM, p...  39.7 us
    all_gather x1, waiting for transfers between devices, shards(): cot = lax.all_gather(cotangent[0], 'head', axis=0, tiled=True)  33.5 us
    pallas_call x1, Pallas kernels, forward(): call(fwd_kernel, 'fwd', (heads, tok // qb), [SMEM, by_q, whole, whole], [...  30 us
    all_gather x1, blocking collectives, shards(): weight_grad = lax.all_gather(mine, 'seq', axis=0, tiled=True)  22.1 us
    all_to_all x1, blocking collectives, shards(): mine = jnp.sum(lax.all_to_all(pieces, 'seq', 0, 0).astype(F32), axis=0)  22 us
    psum x1, blocking collectives, shards(): mine = lax.psum(mine, 'dp') * grad_scale  13.6 us
    pallas_call x1, Pallas kernels, mid_b(): call(lambda *r: midb_kernel(rate, *r), 'midb', (), [SMEM, SMEM] + [WHOLE]...  11.9 us
    all_gather x1, waiting for transfers between devices, shards(): kvf = lax.all_gather(kvp, 'seq')  11.6 us
  transfers between devices with their start and end apart: 4, of which 2 were waited for; matrix products, arithmetic and copies ran while one was open for 1% of the time, Pallas kernels for 42%

profile of v1, /device:TPU:1, one launch (start us, length us, event | category | flops | bytes accessed | tf_op | source)
XLA Modules:
  0.0 223.6 jit_solution(16349228452747138950)
XLA Ops:
  7.2 0.0 all-gather.6.cloned.1.call-start
  7.2 3.1 %pick.1 = (bf16[192,128]{1,0:T(8,128)(2,1)}, bf16[384,128]{1,0:T(8,128)(2,1)}) custom-call(s32[3]{0:T(128)} %r_0_.5, bf16[192,2048]{1,0:T(8,128)(2,1)} %bitcast.15, bf16[192,2048]{1,0:T(8,128)(2,1)} %bitcast.18, bf16[192,2048]{1,0:T(8,128)(2,1)} %bitcast.21), custom_call_target="tpu_custom_call" | custom-call | flops 301989888 | bytes 2359296 | tf_op jit(solution)/shard_map/pick/pallas_call | solution.py:286
  10.3 0.0 all-gather.6.cloned.1.call-update
  10.3 0.0 all-gather.8.cloned.1.call-start
  10.3 0.7 all-gather.8.cloned.1.call-update
  11.0 0.0 reduce-scatter.2.cloned.1.call-start
  11.7 0.6 pad_add_fusion.info.r_0_
  12.3 30.0 %fwd.1 = (bf16[3,2048,2048]{2,1,0:T(8,128)(2,1)}, f32[192,2048]{1,0:T(8,128)}, f32[3,8,2048]{2,1,0:T(8,128)}) custom-call(s32[2]{0:T(128)} %pad_add_fusion.info.r_0_, bf16[192,2048]{1,0:T(8,128)(2,1)} %bitcast.16, bf16[192,2048]{1,0:T(8,128)(2,1)} %bitcast.19, bf16[192,2048]{1,0:T(8,128)(2,1)} %bitcast.22), custom_call_target="tpu_custom_call" | custom-call | flops 3221225472 | bytes 25165824 | tf_op jit(solution)/shard_map/fwd/pallas_call | solution.py:299
  42.3 11.6 %all-gather.6.cloned.1.call-done = bf16[6144,128]{1,0:T(8,128)(2,1)} async-done(((bf16[384,128]{1,0:T(8,128)(2,1)}), bf16[6144,128]{1,0:T(8,128)(2,1)}) %all-gather.6.cloned.1.call-update) | async-done | bytes 1572880 | tf_op jit(solution)/shard_map/all_gather | solution.py:378
  53.8 8.6 %mida.1 = (bf16[768,2048]{1,0:T(8,128)(2,1)}, bf16[192,2048]{1,0:T(8,128)(2,1)}, f32[3,8,2048]{2,1,0:T(8,128)}, f32[192,128]{1,0:T(8,128)}, bf16[3,2048,128]{2,1,0:T(8,128)(2,1)}) custom-call(s32[2]{0:T(128)} %pad_add_fusion.info.r_0_, s32[3]{0:T(128)} %r_0_.5, bf16[192,128]{1,0:T(8,128)(2,1)} %get-tuple-element.24.r_2_.r_10_, ...), custom_call_target="tpu_custom_call" | custom-call | flops 603979776 | bytes 3145728 | tf_op jit(solution)/shard_map/mida/pallas_call | solution.py:316
  62.5 0.0 reduce-scatter.2.cloned.1.call-update
  62.5 33.5 %all-gather.8.cloned.1.call-done = bf16[1,768,2048]{2,1,0:T(8,128)(2,1)} async-done(((bf16[1,192,2048]{2,1,0:T(8,128)(2,1)}), bf16[1,768,2048]{2,1,0:T(8,128)(2,1)}) %all-gather.8.cloned.1.call-update) | async-done | bytes 3145744 | tf_op jit(solution)/shard_map/all_gather | solution.py:376
  96.0 11.9 %midb.1 = (bf16[3,128,2048]{2,1,0:T(8,128)(2,1)}, bf16[16,384,128]{2,1,0:T(8,128)(2,1)}, f32[192,128]{1,0:T(8,128)}, f32[192,768]{1,0:T(8,128)}) custom-call(s32[2]{0:T(128)} %pad_add_fusion.info.r_0_, s32[3]{0:T(128)} %r_0_.5, bf16[768,2048]{1,0:T(8,128)(2,1)} %bitcast.14, bf16[192,768]{1,0:T(8,128)(2,1)} %r_3_.1, ...), custom_call_target="tpu_custom_call" | custom-call | flops 1207959552 | bytes 3145728 | tf_op jit(solution)/shard_map/midb/pallas_call | solution.py:330
  107.9 1.1 convert_element_type.6
  109.0 0.1 reshape.13
  109.1 22.0 %all_to_all.10 = bf16[16,12,768]{2,1,0:T(8,128)(2,1)S(1)} all-to-all(bf16[16,12,768]{2,1,0:T(8,128)(2,1)S(1)} %reshape.13), channel_id=1, replica_groups=mesh['seq'=16,'head'=4,'dp'=4] {'seq'}, dimensions={0} | all-to-all | bytes 589824 | tf_op jit(solution)/shard_map/all_to_all | solution.py:388
  131.1 3.8 %all-to-all-start = ((bf16[16,384,128]{2,1,0:T(8,128)(2,1)}), bf16[16,384,128]{2,1,0:T(8,128)(2,1)S(1)}, u32[]{:S(2)}, u32[]{:S(2)}) async-start(bf16[16,384,128]{2,1,0:T(8,128)(2,1)} %get-tuple-element.39), calls=%async_computation.1 | async-start | bytes 3145728 | tf_op jit(solution)/shard_map/all_to_all | solution.py:385
  134.9 39.7 %bwd.1 = (bf16[192,2048]{1,0:T(8,128)(2,1)}, f32[192,2048]{1,0:T(8,128)}, f32[192,2048]{1,0:T(8,128)}) custom-call(s32[3]{0:T(128)} %r_0_.5, bf16[3,2048,2048]{2,1,0:T(8,128)(2,1)} %get-tuple-element.29.r_1_, bf16[3,128,2048]{2,1,0:T(8,128)(2,1)} %get-tuple-element.34.r_2_, bf16[192,2048]{1,0:T(8,128)(2,1)} %bitcast.17, bf16[192,2048]{1,0:T(8,128)(2,1)} %bitcast.20, ...), custom_call_target="tpu_custom_call" | custom-call | flops 6442450944 | bytes 25165824 | tf_op jit(solution)/shard_map/bwd/pallas_call | solution.py:346
  174.6 0.1 convert_reduce_fusion
  174.7 13.6 %psum.7 = f32[12,768]{1,0:T(8,128)S(1)} all-reduce(f32[12,768]{1,0:T(8,128)S(1)} %convert_reduce_fusion), channel_id=1, replica_groups=mesh['seq'=16,'head'=4,'dp'=4] {'dp'}, use_global_device_ids=true, to_apply=%region_2.0 | all-reduce | flops 9216 | bytes 73728 | tf_op jit(solution)/shard_map/psum | solution.py:389
  188.4 22.1 %all-gather.2 = f32[16,12,768]{2,1,0:T(8,128)S(1)} all-gather(f32[1,12,768]{2,1,0:T(8,128)S(1)} %multiply_bitcast_fusion), channel_id=1, replica_groups=mesh['seq'=16,'head'=4,'dp'=4] {'seq'}, dimensions={0}, use_global_device_ids=true | all-gather | bytes 626688 | tf_op jit(solution)/shard_map/all_gather | solution.py:390
  210.5 0.9 reshape.17
  211.3 0.0 all-to-all-done.r_3_
  211.3 0.0 copy-start
  211.3 1.1 copy-done
  212.5 4.6 %merge.1 = (bf16[192,2048]{1,0:T(8,128)(2,1)}, bf16[192,2048]{1,0:T(8,128)(2,1)}) custom-call(s32[3]{0:T(128)} %r_0_.5, f32[192,2048]{1,0:T(8,128)} %get-tuple-element.37.r_1_, f32[192,2048]{1,0:T(8,128)} %get-tuple-element.38.r_2_, bf16[16,384,128]{2,1,0:T(8,128)(2,1)} %copy-done), custom_call_target="tpu_custom_call" | custom-call | flops 402653184 | bytes 4718592 | tf_op jit(solution)/shard_map/merge/pallas_call | solution.py:362
  217.1 0.0 reduce-scatter.2.cloned.1.call-done
  (1 shorter events, 0.0 us)
Async XLA Ops:
  7.2 46.7 %all-gather.6.cloned.1.call-start = ((), (), s32[]{:S(2)}) async-start(), calls=%async_computation.4 | async-start | bytes 1671168 | tf_op jit(solution)/shard_map/all_gather | solution.py:378
  10.3 85.7 %all-gather.8.cloned.1.call-start = ((), (), s32[]{:S(2)}) async-start(), calls=%async_computation.5 | async-start | bytes 3932160 | tf_op jit(solution)/shard_map/all_gather | solution.py:376
  11.0 206.0 %reduce-scatter.2.cloned.1.call-start = ((), (), s32[]{:S(2)}) async-start(), calls=%async_computation.3 | async-start | bytes 3932160 | tf_op jit(solution)/shard_map/reduce_scatter | solution.py:381
  131.1 80.2 %all-to-all-start = ((bf16[16,384,128]{2,1,0:T(8,128)(2,1)}), bf16[16,384,128]{2,1,0:T(8,128)(2,1)S(1)}, u32[]{:S(2)}, u32[]{:S(2)}) async-start(bf16[16,384,128]{2,1,0:T(8,128)(2,1)} %get-tuple-element.39), calls=%async_computation.1 | async-start | bytes 3145728 | tf_op jit(solution)/shard_map/all_to_all | solution.py:385
  211.3 1.1 copy-start
Sparse Core Ops, SparseCore 0:
  10.4 43.3 all-gather.5
  55.7 40.2 all-gather.7
  99.1 41.0 reduce-scatter.1

commit v2 on v1

v2 whole, which is shorter than its diff:
```python
import math

import jax
import jax.numpy as jnp
from jax import lax
from jax.experimental import pallas as pl
from jax.experimental.pallas import tpu as pltpu
from jax.sharding import PartitionSpec as P

SEL = 2048
HD = 64
NEGATIVE = -1e30
BF = jnp.bfloat16
F32 = jnp.float32
QB = 1024
CK = 512
SAFE = 2.0**40
VMEM_BYTES = 60 * 2**20


def dot(a, b, ca, cb):
    return lax.dot_general(a, b, (((ca,), (cb,)), ((), ())), preferred_element_type=F32)


def split2(x):
    hi = x.astype(BF)
    return hi, (x - hi.astype(F32)).astype(BF)


def split3(x):
    hi = x.astype(BF)
    rest = x - hi.astype(F32)
    mid = rest.astype(BF)
    return hi, mid, (rest - mid.astype(F32)).astype(BF)


def call(kern, name, grid, in_specs, out_specs, out_shape, scratch=(), us=1):
    return pl.pallas_call(
        kern,
        name=name,
        grid=grid,
        in_specs=in_specs,
        out_specs=out_specs,
        out_shape=out_shape,
        scratch_shapes=list(scratch),
        compiler_params=pltpu.CompilerParams(vmem_limit_bytes=VMEM_BYTES),
        cost_estimate=work(us),
    )


def work(us):
    return pl.CostEstimate(flops=int(us * 1.15e9), bytes_accessed=0, transcendentals=0)


SMEM = pl.BlockSpec(memory_space=pltpu.SMEM)
WHOLE = pl.BlockSpec(memory_space=pltpu.VMEM)


def sel_matrix(off, rate, rows, cols):
    pos = lax.broadcasted_iota(jnp.int32, (rows, cols), 0)
    num = lax.broadcasted_iota(jnp.int32, (rows, cols), 1)
    return jnp.where(pos == num * rate + off, 1.0, 0.0).astype(BF)


def place_matrix(off, rate, start, rows, cols):
    num = lax.broadcasted_iota(jnp.int32, (rows, cols), 0)
    pos = lax.broadcasted_iota(jnp.int32, (rows, cols), 1) + start
    return jnp.where(pos == num * rate + off, 1.0, 0.0).astype(BF)


def pick_kernel(rate, offs, q, k, v, qp, kvp):
    sel = sel_matrix(offs[pl.program_id(0)], rate, q.shape[1], qp.shape[1])
    got = dot(jnp.concatenate([q[...], k[...], v[...]], axis=0), sel, 1, 0).astype(BF)
    qp[...] = got[:HD]
    kvp[0] = got[HD : 2 * HD]
    kvp[1] = got[2 * HD :]


def stack_rows(count, parts):
    row = lax.broadcasted_iota(jnp.int32, (count, parts[0].shape[1]), 0)
    out = jnp.zeros(row.shape, F32)
    for i, part in enumerate(parts):
        out = jnp.where(row == i, part.astype(F32), out)
    return out.astype(BF)


def fwd_kernel(info, q, k, v, e_out, out, stats, kt, qa, va):
    tok = k.shape[1]
    qb = out.shape[1]
    step = pl.program_id(1)

    @pl.when(step == 0)
    def _():
        pos = lax.broadcasted_iota(jnp.int32, (HD, tok), 1) + info[1]
        row = lax.broadcasted_iota(jnp.int32, (HD, tok), 0)
        bias = jnp.where(
            row == 0, jnp.where(pos >= info[0], NEGATIVE, 0.0), jnp.where(row == 1, -1.0, 0.0)
        )
        kt[...] = jnp.concatenate([k[...], bias.astype(BF)], axis=0).T
        one = jnp.where(row == 0, 1.0, 0.0).astype(BF)
        qa[...] = jnp.concatenate([q[...] * jnp.asarray(0.125, BF), one], axis=0)
        first = dot(kt[:256, :], qa[...], 1, 0)
        top = jnp.max(jnp.max(first.reshape(32, 8, tok), axis=0), axis=0, keepdims=True)
        qa[HD:, :] = jnp.where(row == 0, 1.0, jnp.where(row == 1, top, 0.0)).astype(BF)
        row16 = lax.broadcasted_iota(jnp.int32, (16, tok), 0)
        va[...] = jnp.concatenate([v[...], jnp.where(row16 == 0, 1.0, 0.0).astype(BF)], axis=0)

    base = pl.multiple_of(step * qb, qb)

    def finish(cols, acc):
        rt = 1.0 / acc[HD : HD + 1]
        out[:, cols] = acc[:HD] * rt
        stats[0, :, cols] = jnp.broadcast_to(rt, (8, rt.shape[1]))

    qc = qa[:, pl.ds(base, qb)]
    for i in range(0, tok, CK):
        e_out[0, i : i + CK, :] = jnp.exp(dot(kt[i : i + CK, :], qc, 1, 0)).astype(BF)
    acc = dot(va[...], e_out[0], 1, 0)
    finish(slice(0, qb), acc)
    total = acc[HD : HD + 1]
    unsafe = jnp.max(jnp.where(total < SAFE, 0.0, 1.0)) > 0.0

    @pl.when(unsafe)
    def _():
        width = 128

        def redo(n, carry):
            c0 = pl.multiple_of(n * width, width)
            cols = pl.ds(c0, width)
            s = dot(kt[...], qa[:, pl.ds(pl.multiple_of(base + c0, width), width)], 1, 0)
            s = s - jnp.max(s, axis=0, keepdims=True)
            e_out[0, :, cols] = jnp.exp(s).astype(BF)
            finish(cols, dot(va[...], e_out[0, :, cols], 1, 0))
            return carry

        lax.fori_loop(0, qb // width, redo, 0)


def projg_kernel(rate, info, offs, c0, c1, c2, c3, w, out_a, stats, g_out, dob, cot):
    part, cols = c0.shape
    count = cot.shape[0] // part
    for s, block in enumerate((c0, c1, c2, c3)):
        owner = lax.rem(info[2] + (count - s), count)
        cot[pl.ds(pl.multiple_of(owner * part, part), part), :] = block[...]
    heads = stats.shape[0]
    here = lax.broadcasted_iota(jnp.int32, (1, cols), 1) + pl.program_id(0) * cols
    keep = jnp.where(here + info[1] < info[0], 1.0, 0.0)
    g_all = dot(w[...], cot[...], 1, 0).astype(BF).astype(F32) * keep
    g_out[...] = g_all.astype(BF)
    for h in range(heads):
        rows = slice(h * HD, (h + 1) * HD)
        g = jnp.where((here % rate) == offs[h], 0.0, g_all[rows])
        rt = stats[h, 0:1, :]
        delta = jnp.sum(g * out_a[rows, :], axis=0, keepdims=True)
        c_hi, c_lo = split2(-delta * rt)
        dob[h] = jnp.concatenate([(g * rt).astype(BF), stack_rows(HD, [c_hi, c_lo])], axis=0)


def softmax_rows(s):
    m = jnp.max(s, axis=1, keepdims=True)
    e = jnp.exp(s - m)
    t = jnp.sum(e, axis=1, keepdims=True)
    return (e * (1.0 / t)).astype(BF), m + jnp.log(t)


def far_parts(kv_own, kv_oth, rows):
    both = [ref.at[c] for ref in (kv_own, kv_oth) for c in range(ref.shape[0])]
    return tuple(jnp.concatenate([ref[n, rows, :] for ref in both], axis=1) for n in range(2))


def mida_kernel(
    rate, info, offs, qp, kv_own, kv_oth, k, v, out_a, w,
    t0, t1, t2, t3, attn, pa, pb, oa_p, ob_p, sh_p, wt,
):
    part = t0.shape[0]
    count = wt.shape[0] // part
    heads = pa.shape[0]
    tok = out_a.shape[1]
    picks = qp.shape[1]
    chips = kv_own.shape[0]
    length, start, core = info[0], info[1], info[3]
    here = lax.broadcasted_iota(jnp.int32, (1, tok), 1)
    keep = jnp.where(here + start < length, 1.0, 0.0)
    num = lax.broadcasted_iota(jnp.int32, (1, 2 * chips * picks), 1)
    chunk = num // picks
    rank = 2 * (chunk % chips) + jnp.where(chunk < chips, core, 1 - core)
    far_pos = (rank * picks + num % picks) * rate
    pick_pos = lax.broadcasted_iota(jnp.int32, (picks, 1), 0) * rate + start
    wt[...] = w[...].T
    for h in range(heads):
        rows = slice(h * HD, (h + 1) * HD)
        off = offs[h]
        kf, vf = far_parts(kv_own, kv_oth, rows)
        qs = qp[rows, :] * jnp.asarray(0.125, BF)
        p_b, lse_b = softmax_rows(
            jnp.where(far_pos + off < length, dot(qs, kf, 0, 0), NEGATIVE)
        )
        p_a, lse_a = softmax_rows(
            jnp.where(here + start < length, dot(qs, k[rows, :], 0, 0), NEGATIVE)
        )
        pa[h] = p_a
        pb[h] = p_b
        o_b = dot(p_b, vf, 1, 1)
        o_a = dot(p_a, v[rows, :], 1, 1)
        oa_p[h] = o_a
        ob_p[h] = o_b
        gap = lse_a - lse_b
        near = 1.0 / (1.0 + jnp.exp(-gap))
        far = 1.0 / (1.0 + jnp.exp(gap))
        sh_p[h] = jnp.concatenate(
            [jnp.broadcast_to(near, (picks, HD)), jnp.broadcast_to(far, (picks, HD))], axis=1
        )
        live = jnp.where(pick_pos + off < length, 1.0, 0.0)
        mixed_p = ((near * o_a + far * o_b) * live).astype(BF)
        spread = dot(mixed_p, place_matrix(off, rate, 0, picks, tok), 0, 0)
        attn[rows, :] = jnp.where((here % rate) == off, spread, out_a[rows, :] * keep).astype(BF)
    for s, term in enumerate((t0, t1, t2, t3)):
        owner = lax.rem(info[2] + s, count)
        out_rows = pl.ds(pl.multiple_of(owner * part, part), part)
        term[...] = dot(wt[out_rows, :], attn[...], 1, 0).astype(BF)


def midb_kernel(
    rate, info, offs, g_in, sh_p, oa_p, ob_p, pa, pb, qp, kv_own, kv_oth, k, v, attn,
    c0, c1, c2, c3, kept, sent, dqp, dkp, dvp, cot, sems,
):
    part = c0.shape[0]
    count = cot.shape[0] // part
    copies = []
    for s, block in enumerate((c0, c1, c2, c3)):
        owner = lax.rem(info[2] + (count - s), count)
        there = cot.at[pl.ds(pl.multiple_of(owner * part, part), part), :]
        copies.append(pltpu.make_async_copy(block, there, sems.at[s]))
        copies[-1].start()
    heads = pa.shape[0]
    tok = g_in.shape[1]
    picks = qp.shape[1]
    chips = kept.shape[0]
    width = heads * HD
    for h in range(heads):
        rows = slice(h * HD, (h + 1) * HD)
        g = dot(sel_matrix(offs[h], rate, tok, picks), g_in[rows, :], 0, 1)
        near, far = sh_p[h, :, :HD], sh_p[h, :, HD:]
        o_a, o_b = oa_p[h], ob_p[h]
        dlse = (near * far)[:, :1] * jnp.sum(g * (o_a - o_b), axis=1, keepdims=True)
        kf, vf = far_parts(kv_own, kv_oth, rows)
        q = qp[rows, :]

        def back(k_all, v_all, p, do, out, dl):
            delta = jnp.sum(do.astype(F32) * out, axis=1, keepdims=True)
            dp = dot(do, v_all, 1, 0) + (dl - delta)
            ds = (p.astype(F32) * dp * 0.125).astype(BF)
            return dot(ds, k_all, 1, 1), dot(q, ds, 1, 0), dot(do, p, 0, 0)

        dq_a, dk_a, dv_a = back(k[rows, :], v[rows, :], pa[h], (near * g).astype(BF), o_a, dlse)
        dq_b, dk_b, dv_b = back(kf, vf, pb[h], (far * g).astype(BF), o_b, -dlse)
        dqp[h] = (dq_a + dq_b).astype(BF)
        dkp[rows, :] = dk_a.astype(BF)
        dvp[rows, :] = dv_a.astype(BF)
        for n, grad in enumerate((dk_b.astype(BF), dv_b.astype(BF))):
            first = n * width + h * HD
            for i, ref in enumerate((kept, sent)):
                for c in range(chips):
                    cols = slice((i * chips + c) * picks, (i * chips + c + 1) * picks)
                    ref[c, first : first + HD, :] = grad[:, cols]
    for copy in copies:
        copy.wait()
    grad = dot(attn[...], cot[...], 1, 1)
    size = grad.shape[0] // (2 * chips)
    blank = jnp.zeros((16 - size, grad.shape[1]), F32)
    for side in range(2):

        @pl.when(info[3] == side)
        def _():
            for ref, core in ((kept, side), (sent, 1 - side)):
                for c in range(chips):
                    r = 2 * c + core
                    piece = jnp.concatenate([grad[r * size : (r + 1) * size], blank], axis=0)
                    piece = piece.astype(BF)
                    for n in range(grad.shape[1] // picks):
                        first = 2 * width + 16 * n
                        ref[c, first : first + 16, :] = piece[:, n * picks : (n + 1) * picks]


def bwd_kernel(e, dob, q, k, v, *rest):
    dq, dk, dv, vt = rest[-4:]
    tok = k.shape[1]
    qb = q.shape[1]
    step = pl.program_id(1)

    @pl.when(step == 0)
    def _():
        row = lax.broadcasted_iota(jnp.int32, (HD, tok), 0)
        ones = jnp.where(row < 2, 1.0, 0.0).astype(BF)
        vt[...] = jnp.concatenate([v[...], ones], axis=0).T
        dk[...] = jnp.zeros_like(dk)
        dv[...] = jnp.zeros_like(dv)

    ck = CK
    do = dob[0, :HD, :]
    acc = None
    for i in range(0, tok, ck):
        dp = dot(vt[i : i + ck, :], dob[0], 1, 0)
        ei = e[0, i : i + ck, :]
        ds = (ei.astype(F32) * dp).astype(BF)
        part = dot(k[:, i : i + ck], ds, 1, 0)
        acc = part if acc is None else acc + part
        dk[:, i : i + ck] += dot(q[...], ds, 1, 1)
        dv[:, i : i + ck] += dot(do, ei, 1, 1)
    dq[...] = (acc * 0.125).astype(BF)


def merge_kernel(rate, offs, dq, dk, dv, dqp, dkp, dvp, far_k, far_v, qg, kg, vg):
    place = place_matrix(offs[pl.program_id(0)], rate, 0, far_k.shape[2], dk.shape[1])
    sums = []
    for parts in (far_k, far_v):
        total = parts[0].astype(F32)
        for r in range(1, parts.shape[0]):
            total = total + parts[r].astype(F32)
        sums.append(total.astype(BF))
    spread = dot(jnp.concatenate(sums + [dqp[0].T], axis=0), place, 1, 0)
    near_k = dk[...] * 0.125 + dkp[...].astype(F32)
    near_v = dv[...] + dvp[...].astype(F32)
    kg[...] = (near_k + spread[:HD]).astype(BF)
    vg[...] = (near_v + spread[HD : 2 * HD]).astype(BF)
    qg[...] = (dq[...].astype(F32) + spread[2 * HD :]).astype(BF)


SDS = jax.ShapeDtypeStruct


def pick(rate, offs, q, k, v, picks):
    rows, tok = q.shape
    by_head = pl.BlockSpec((HD, tok), lambda h: (h, 0))
    return call(
        lambda *r: pick_kernel(rate, *r), "pick", (rows // HD,),
        [SMEM, by_head, by_head, by_head],
        [
            pl.BlockSpec((HD, picks), lambda h: (h, 0)),
            pl.BlockSpec((2, HD, picks), lambda h: (0, h, 0)),
        ],
        [SDS((rows, picks), BF), SDS((2, rows, picks), BF)],
        us=2,
    )(offs, q, k, v)


def forward(info, q, k, v):
    rows, tok = q.shape
    heads = rows // HD
    qb = min(QB, tok)
    by_q = pl.BlockSpec((HD, qb), lambda h, j: (h, j))
    whole = pl.BlockSpec((HD, tok), lambda h, j: (h, 0))
    return call(
        fwd_kernel, "fwd", (heads, tok // qb), [SMEM, whole, whole, whole],
        [
            pl.BlockSpec((1, tok, qb), lambda h, j: (h, 0, j)),
            by_q,
            pl.BlockSpec((1, 8, qb), lambda h, j: (h, 0, j)),
        ],
        [SDS((heads, tok, tok), BF), SDS((rows, tok), F32), SDS((heads, 8, tok), F32)],
        scratch=[
            pltpu.VMEM((tok, 2 * HD), BF), pltpu.VMEM((2 * HD, tok), BF),
            pltpu.VMEM((HD + 16, tok), BF),
        ],
        us=18,
    )(info, q, k, v)


def project(rate, info, offs, blocks, w, out_a, stats):
    rows, tok = out_a.shape
    heads = rows // HD
    cols = tok // 4
    by_p = pl.BlockSpec((rows, cols), lambda j: (0, j))
    by_h = lambda n: pl.BlockSpec((heads, n, cols), lambda j: (0, 0, j))
    return call(
        lambda *r: projg_kernel(rate, *r), "projg", (tok // cols,),
        [SMEM, SMEM] + [by_p] * 4 + [WHOLE, by_p, by_h(8)],
        [by_p, by_h(2 * HD)],
        [SDS((rows, tok), BF), SDS((heads, 2 * HD, tok), BF)],
        scratch=[pltpu.VMEM((w.shape[1], cols), BF)],
        us=4,
    )(info, offs, *blocks, w, out_a, stats)


def mid_a(rate, info, offs, qp, kv_own, kv_oth, k, v, out_a, w):
    rows, tok = out_a.shape
    heads = rows // HD
    picks = qp.shape[1]
    far = 2 * kv_own.shape[0] * picks
    return call(
        lambda *r: mida_kernel(rate, *r), "mida", (), [SMEM, SMEM] + [WHOLE] * 7, [WHOLE] * 10,
        [SDS((rows, tok), BF)] * 5
        + [
            SDS((heads, picks, tok), BF), SDS((heads, picks, far), BF),
            SDS((heads, picks, HD), F32), SDS((heads, picks, HD), F32),
            SDS((heads, picks, 2 * HD), F32),
        ],
        scratch=[pltpu.VMEM((w.shape[1], rows), BF)],
        us=10,
    )(info, offs, qp, kv_own, kv_oth, k, v, out_a, w)


def mid_b(rate, info, offs, g, sh_p, oa_p, ob_p, pa, pb, qp, kv_own, kv_oth, k, v, attn, blocks):
    rows, tok = g.shape
    heads = rows // HD
    picks = qp.shape[1]
    count = len(blocks)
    chips = kv_own.shape[0]
    anywhere = pl.BlockSpec(memory_space=pl.ANY)
    half = SDS((chips, 2 * rows + 16 * (count * rows // picks), picks), BF)
    return call(
        lambda *r: midb_kernel(rate, *r), "midb", (),
        [SMEM, SMEM] + [WHOLE] * 12 + [anywhere] * 4, [WHOLE] * 5,
        [half, half, SDS((heads, picks, HD), BF), SDS((rows, tok), BF), SDS((rows, tok), BF)],
        scratch=[pltpu.VMEM((count * rows, tok), BF), pltpu.SemaphoreType.DMA((count,))],
        us=10,
    )(info, offs, g, sh_p, oa_p, ob_p, pa, pb, qp, kv_own, kv_oth, k, v, attn, *blocks)


def hold(x, after):
    anywhere = pl.BlockSpec(memory_space=pl.ANY)
    return pl.pallas_call(
        lambda *refs: None, name="hold", in_specs=[anywhere] * 2, out_specs=anywhere,
        out_shape=SDS(x.shape, x.dtype), input_output_aliases={0: 0},
    )(x, after)


def total_kernel(parts, after, out):
    total = parts[0].astype(F32)
    for r in range(1, parts.shape[0]):
        total = total + parts[r].astype(F32)
    out[...] = total


def total(parts, first, after):
    count, rows, cols = parts.shape
    rows -= first
    return call(
        total_kernel, "total", (1,),
        [
            pl.BlockSpec((count, rows, cols), lambda i: (0, first // rows, 0)),
            pl.BlockSpec(memory_space=pl.ANY),
        ],
        pl.BlockSpec((rows, cols), lambda i: (0, 0)),
        SDS((rows, cols), F32), us=1,
    )(parts, after)


def backward(first, heads, e, dob, q, k, v, earlier, after):
    rows, tok = q.shape
    qb = min(QB, tok)
    by_q = pl.BlockSpec((HD, qb), lambda h, j: (first + h, j))
    whole = pl.BlockSpec((HD, tok), lambda h, j: (first + h, 0))
    anywhere = pl.BlockSpec(memory_space=pl.ANY)
    n_in = 5 + len(after)
    return pl.pallas_call(
        bwd_kernel,
        name="bwd%d" % first,
        grid=(heads, tok // qb),
        in_specs=[
            pl.BlockSpec((1, tok, qb), lambda h, j: (first + h, 0, j)),
            pl.BlockSpec((1, 2 * HD, qb), lambda h, j: (first + h, 0, j)),
            by_q, whole, whole,
        ]
        + [anywhere] * (len(after) + len(earlier)),
        out_specs=[by_q, whole, whole],
        out_shape=[SDS((rows, tok), BF), SDS((rows, tok), F32), SDS((rows, tok), F32)],
        scratch_shapes=[pltpu.VMEM((tok, 2 * HD), BF)],
        input_output_aliases={n_in + i: i for i in range(len(earlier))},
        compiler_params=pltpu.CompilerParams(vmem_limit_bytes=VMEM_BYTES),
        cost_estimate=work(12 * heads),
    )(e, dob, q, k, v, *after, *earlier)


def merge(rate, offs, dq, dk, dv, dqp, dkp, dvp, far):
    rows, tok = dk.shape
    heads = rows // HD
    chips, _, picks = far.shape
    by_head = pl.BlockSpec((HD, tok), lambda h: (h, 0))
    return call(
        lambda *r: merge_kernel(rate, *r), "merge", (heads,),
        [SMEM] + [by_head] * 3 + [pl.BlockSpec((1, picks, HD), lambda h: (h, 0, 0))]
        + [by_head] * 2
        + [
            pl.BlockSpec((chips, HD, picks), lambda h: (0, h, 0)),
            pl.BlockSpec((chips, HD, picks), lambda h: (0, heads + h, 0)),
        ],
        [by_head] * 3,
        [SDS((rows, tok), BF)] * 3,
        us=5,
    )(offs, dq, dk, dv, dqp, dkp, dvp, far, far)


def shift(x, axis, by):
    count = lax.axis_size(axis)
    return lax.ppermute(x, axis, [(i, (i + by) % count) for i in range(count)])


def shards(queries, keys, values, cotangent, w_out, lengths, offsets):
    rows, tok = queries.shape[1:]
    seq_count = lax.axis_size("seq")
    rate = tok * seq_count // SEL
    picks = tok // rate
    place = lax.axis_index("seq").astype(jnp.int32)
    info = jnp.stack(
        [
            lengths[0], place * tok, lax.axis_index("head").astype(jnp.int32), place % 2,
            place // 2,
        ]
    )
    q, k, v = queries[0], keys[0], values[0]
    groups = [list(range(c, seq_count, 2)) for c in range(2)]
    chips = seq_count // 2
    swap = [(i, i ^ 1) for i in range(seq_count)]
    qp, kvp = pick(rate, offsets, q, k, v, picks)
    kv_own = lax.all_to_all(
        jnp.broadcast_to(kvp[None], (chips,) + kvp.shape), "seq", 0, 0, axis_index_groups=groups
    )
    own = cotangent[0]
    blocks = [own] + [shift(own, "head", s) for s in (1, 2, 3)]
    e, out_a, stats = forward(info, q, k, v)
    kv_own = hold(kv_own, stats)
    kv_oth = lax.ppermute(kv_own, "seq", swap)
    *terms, attn, pa, pb, oa_p, ob_p, sh_p = mid_a(
        rate, info, offsets, qp, kv_own, kv_oth, k, v, out_a, w_out
    )
    sent_terms = [shift(terms[s], "head", s) for s in (1, 2, 3)]
    g, dob = project(rate, info, offsets, blocks, w_out, out_a, stats)
    kept, sent, dqp, dkp, dvp = mid_b(
        rate, info, offsets, g, sh_p, oa_p, ob_p, pa, pb, qp, kv_own, kv_oth, k, v, attn, blocks
    )
    got = lax.ppermute(sent, "seq", swap)
    pair = (kept.astype(F32) + got.astype(F32)).astype(BF)
    far = lax.all_to_all(pair, "seq", 0, 0, axis_index_groups=groups)
    grads = backward(0, 2, e, dob, q, k, v, (), (pair,))
    mine = total(far, 2 * rows, grads[0]).reshape(-1, 16, picks)[:, : rows // seq_count]
    mine = mine.transpose(1, 0, 2).reshape(rows // seq_count, -1)
    grad_scale = 1.0 / math.sqrt(tok * seq_count * lax.axis_size("dp"))
    mine = (mine + sum(shift(mine, "dp", s) for s in (1, 2, 3))) * grad_scale
    weight_grad = lax.all_to_all(
        jnp.broadcast_to(mine[None], (seq_count,) + mine.shape), "seq", 0, 0
    ).reshape(w_out.shape)
    dq, dk, dv = backward(2, 1, e, dob, q, k, v, grads, sent_terms)
    mixed = sum(t.astype(F32) for t in [terms[0]] + sent_terms).astype(BF)
    qg, kg, vg = merge(rate, offsets, dq, dk, dv, dqp, dkp, dvp, far)
    return (mixed[None], qg[None], kg[None], vg[None], weight_grad)


def solution(mesh):
    full = P("dp", "head", "seq")
    return jax.shard_map(
        shards,
        mesh=mesh,
        in_specs=(full, full, full, full, P("head", None), P("dp"), P("head")),
        out_specs=(full, full, full, full, P("head", None)),
        check_vma=False,
    )
```

time: 224 us -> 195 us (0.87)
  blocking collectives: 57.8 us -> 0 us
  Pallas kernels: 97.8 us -> 131 us
  waiting for transfers between devices: 45.8 us -> 12.6 us
  starting transfers between devices: 3.95 us -> 34.8 us
  between operations: 14.4 us -> 1.41 us
  local copies, waits for them, and re-layouts: 2.09 us -> 9.39 us
  other arithmetic: 1.76 us -> 5.22 us
    all_gather x2 -> x0, waiting for transfers between devices: 45 us -> none  [the longest x1 33.5 us: shards(): cot = lax.all_gather(cotangent[0], 'head', axis=0, tiled=True)]
    pallas_call x4 -> x8, Pallas kernels: 77.3 us -> 110 us  [the longest x1 60.4 us: forward(): call(fwd_kernel, 'fwd', (heads, tok // qb), [SMEM, whole, whole, whole],...]
    all_gather x1 -> x0, blocking collectives: 22.1 us -> none  [shards(): weight_grad = lax.all_gather(mine, 'seq', axis=0, tiled=True)]
    all_to_all x1 -> x0, blocking collectives: 22 us -> none  [shards(): mine = jnp.sum(lax.all_to_all(pieces, 'seq', 0, 0).astype(F32), axis=0)]
    all_to_all x1 -> x3, starting transfers between devices: 3.83 us -> 20.4 us  [the longest x1 8.19 us: shards(): lax.all_to_all(jnp.broadcast_to(kvp[None], (chips,) + kvp.shape), 'seq',...]
    ppermute x0 -> x11, starting transfers between devices: none -> 14.4 us  [the longest x9 12.5 us: shift(): return lax.ppermute(x, axis, [(i, (i + by) % count) for i in range(count)])]
    psum x1 -> x0, blocking collectives: 13.6 us -> none  [shards(): mine = lax.psum(mine, 'dp') * grad_scale]
    all_to_all x1 -> x3, waiting for transfers between devices: 0.01 us -> 11.5 us  [the longest x1 6.39 us: shards(): far = lax.all_to_all(pair, 'seq', 0, 0, axis_index_groups=groups)]
  transfers between devices with their start and end apart: 4 -> 14, of which waited for: 2 -> 4; matrix products, arithmetic and copies ran while one was open for 1% -> 4% of each run, Pallas kernels for 42% -> 57%
where the time goes in v2:
time: 195 us; the launch traced here: 194 us
  Pallas kernels  131 us (67%)
  starting transfers between devices  34.8 us (18%)
  waiting for transfers between devices  12.6 us (6%)
  local copies, waits for them, and re-layouts  9.39 us (5%)
  other arithmetic  5.22 us (3%)
    pallas_call x1, Pallas kernels, forward(): call(fwd_kernel, 'fwd', (heads, tok // qb), [SMEM, whole, whole, whole],...  60.4 us
    pallas_call x2, Pallas kernels, backward(): pl.pallas_call(bwd_kernel, name='bwd%d' % first, grid=(heads, tok // qb),...  33.8 us
    ppermute x9, starting transfers between devices, shift(): return lax.ppermute(x, axis, [(i, (i + by) % count) for i in range(count)])  12.5 us
    pallas_call x1, Pallas kernels, mid_b(): call(lambda *r: midb_kernel(rate, *r), 'midb', (), [SMEM, SMEM] + [WHOLE]...  11 us
    pallas_call x1, Pallas kernels, mid_a(): call(lambda *r: mida_kernel(rate, *r), 'mida', (), [SMEM, SMEM] + [WHOLE]...  9.44 us
    all_to_all x1, starting transfers between devices, shards(): lax.all_to_all(jnp.broadcast_to(kvp[None], (chips,) + kvp.shape), 'seq',...  8.19 us
    all_to_all x1, starting transfers between devices, shards(): far = lax.all_to_all(pair, 'seq', 0, 0, axis_index_groups=groups)  6.92 us
    all_to_all x1, waiting for transfers between devices, shards(): far = lax.all_to_all(pair, 'seq', 0, 0, axis_index_groups=groups)  6.39 us
  transfers between devices with their start and end apart: 14, of which 4 were waited for; matrix products, arithmetic and copies ran while one was open for 4% of the time, Pallas kernels for 57%

profile of v2, /device:TPU:1, one launch (start us, length us, event | category | flops | bytes accessed | tf_op | source)
XLA Modules:
  0.0 194.3 jit_solution(16397006106748669232)
XLA Ops:
  0.6 3.4 %collective-permute-start.6 = (bf16[192,2048]{1,0:T(8,128)(2,1)}, bf16[192,2048]{1,0:T(8,128)(2,1)S(1)}, u32[]{:S(2)}, u32[]{:S(2)}) collective-permute-start(bf16[192,2048]{1,0:T(8,128)(2,1)} %bitcast.28), channel_id=1, source_target_pairs={{0,12},{4,0},{8,4},{12,8},{1,13},{5,1},{9,5},{13,9},{2,14},{6,2},{... | collective-permute-start | bytes 2359304 | tf_op jit(solution)/shard_map/ppermute | solution.py:496
  5.1 3.6 %pick.1 = (bf16[192,128]{1,0:T(8,128)(2,1)}, bf16[2,192,128]{2,1,0:T(8,128)(2,1)}) custom-call(s32[3]{0:T(128)} %r_0_.3, bf16[192,2048]{1,0:T(8,128)(2,1)} %bitcast.33, bf16[192,2048]{1,0:T(8,128)(2,1)} %bitcast.37, bf16[192,2048]{1,0:T(8,128)(2,1)} %bitcast.43), custom_call_target="tpu_custom_call" | custom-call | flops 2300000000 | tf_op jit(solution)/shard_map/pick/pallas_call | solution.py:335
  8.7 1.9 broadcast_in_dim.24
  10.7 8.2 %all-to-all-start = ((bf16[8,2,192,128]{3,2,1,0:T(8,128)(2,1)}), bf16[8,2,192,128]{3,2,1,0:T(8,128)(2,1)S(1)}, u32[]{:S(2)}, u32[]{:S(2)}) async-start(bf16[8,2,192,128]{3,2,1,0:T(8,128)(2,1)} %broadcast_in_dim.24), calls=%async_computation | async-start | bytes 1572864 | tf_op jit(solution)/shard_map/all_to_all | solution.py:516
  19.5 0.7 stack.19.info.r_0_
  20.2 60.4 %fwd.1 = (bf16[3,2048,2048]{2,1,0:T(8,128)(2,1)}, f32[192,2048]{1,0:T(8,128)}, f32[3,8,2048]{2,1,0:T(8,128)}) custom-call(s32[5]{0:T(128)} %stack.19.info.r_0_, bf16[192,2048]{1,0:T(8,128)(2,1)} %bitcast.34, bf16[192,2048]{1,0:T(8,128)(2,1)} %bitcast.38, bf16[192,2048]{1,0:T(8,128)(2,1)} %bitcast.44), custom_call_target="tpu_custom_call" | custom-call | flops 20700000256 | tf_op jit(solution)/shard_map/fwd/pallas_call | solution.py:353
  80.6 0.9 copy-done
  81.5 1.8 collective-permute-start
  83.4 0.9 copy-done.5
  84.8 5.7 %projg.1 = (bf16[192,2048]{1,0:T(8,128)(2,1)}, bf16[3,128,2048]{2,1,0:T(8,128)(2,1)}) custom-call(s32[5]{0:T(128)} %stack.19.info.r_0_, s32[3]{0:T(128)} %r_0_.3, bf16[192,2048]{1,0:T(8,128)(2,1)} %bitcast.31, bf16[192,2048]{1,0:T(8,128)(2,1)} %copy-done.7, bf16[192,2048]{1,0:T(8,128)(2,1)} %copy-done.6, bf16[192,2048]{1,0:T(8,128)(2,1)} %copy-done.5, ...), custom_call_target="tpu_custom_call" | custom-call | flops 4600000000 | tf_op jit(solution)/shard_map/projg/pallas_call | solution.py:375
  90.5 0.9 copy-done.8
  91.4 9.4 %mida.1 = (bf16[192,2048]{1,0:T(8,128)(2,1)}, bf16[192,2048]{1,0:T(8,128)(2,1)}, bf16[192,2048]{1,0:T(8,128)(2,1)}, bf16[192,2048]{1,0:T(8,128)(2,1)}, bf16[192,...) custom-call(s32[5]{0:T(128)} %stack.19.info.r_0_, ...), custom_call_target="tpu_custom_call" | custom-call | flops 11500000256 | tf_op jit(solution)/shard_map/mida/pallas_call | solution.py:390
  100.8 11.0 %midb.1 = (bf16[8,480,128]{2,1,0:T(8,128)(2,1)}, bf16[8,480,128]{2,1,0:T(8,128)(2,1)}, bf16[3,128,64]{2,1,0:T(8,128)(2,1)}, bf16[192,2048]{1,0:T(8,128)(2,1)}, bf16[192,2048]{1,0:T(8,128)(2,1)}) custom-call(s32[5]{0:T(128)} %stack.19.info.r_0_, s32[3]{0:T(128)} %r_0_.3, bf16[192,2048]{1,0:T(8,128)(2,1)} %get-tuple-element.46.r_2_, ...), custom_call_target="tpu_custom_call" | custom-call | flops 11500000256 | tf_op jit(solution)/shard_map/midb/pallas_call | solution.py:411
  112.0 1.6 collective-permute-start.1
  113.6 1.7 collective-permute-start.2
  115.3 0.8 collective-permute-start.3
  116.1 2.4 %add_convert_fusion.rest_0_ = bf16[8,480,128]{2,1,0:T(8,128)(2,1)} fusion(bf16[8,480,128]{2,1,0:T(8,128)(2,1)S(1)} %collective-permute-done.7, bf16[8,480,128]{2,1,0:T(8,128)(2,1)} %get-tuple-element.53), kind=kLoop, calls=%fused_computation | loop fusion | flops 1966080 | bytes 2949120 | tf_op jit(solution)/shard_map/convert_element_type | solution.py:533
  118.5 6.9 %all-to-all-start.1 = ((bf16[8,480,128]{2,1,0:T(8,128)(2,1)}), bf16[8,480,128]{2,1,0:T(8,128)(2,1)S(1)}, u32[]{:S(2)}, u32[]{:S(2)}) async-start(bf16[8,480,128]{2,1,0:T(8,128)(2,1)} %add_convert_fusion.rest_0_), calls=%async_computation.1 | async-start | bytes 1966080 | tf_op jit(solution)/shard_map/all_to_all | solution.py:534
  125.4 21.4 %bwd0.1 = (bf16[192,2048]{1,0:T(8,128)(2,1)}, f32[192,2048]{1,0:T(8,128)}, f32[192,2048]{1,0:T(8,128)}) custom-call(bf16[3,2048,2048]{2,1,0:T(8,128)(2,1)} %get-tuple-element.44.e, bf16[3,128,2048]{2,1,0:T(8,128)(2,1)} %get-tuple-element.45.dob, bf16[192,2048]{1,0:T(8,128)(2,1)} %bitcast.35, bf16[192,2048]{1,0:T(8,128)(2,1)} %bitcast.41, ...), custom_call_target="tpu_custom_call" | custom-call | flops 27599998976 | tf_op jit(solution)/shard_map/bwd0/pallas_call | solution.py:456
  146.8 6.4 %all-to-all-done.1.r_7_.r_8_.parts = bf16[8,480,128]{2,1,0:T(8,128)(2,1)S(1)} async-done(((bf16[8,480,128]{2,1,0:T(8,128)(2,1)}), bf16[8,480,128]{2,1,0:T(8,128)(2,1)S(1)}, u32[]{:S(2)}, u32[]{:S(2)}) %all-to-all-start.1) | async-done | bytes 983072 | tf_op jit(solution)/shard_map/all_to_all | solution.py:534
  153.2 0.9 copy-done.1
  154.2 1.6 total.1
  155.8 0.8 copy.20
  156.7 2.8 %collective-permute-start.10 = (f32[12,768]{1,0:T(8,128)S(1)}, f32[12,768]{1,0:T(8,128)S(1)}, u32[]{:S(2)}, u32[]{:S(2)}) collective-permute-start(f32[12,768]{1,0:T(8,128)S(1)} %bitcast.23), channel_id=1, source_target_pairs={{0,3},{1,0},{2,1},{3,2},{4,7},{5,4},{6,5},{7,6},{8,11},{9,8},{10,9... | collective-permute-start | bytes 110600 | tf_op jit(solution)/shard_map/ppermute | solution.py:496
  159.8 0.7 collective-permute-start.8
  160.5 2.8 %fusion = bf16[1,192,2048]{2,1,0:T(8,128)(2,1)} fusion(bf16[192,2048]{1,0:T(8,128)(2,1)} %collective-permute-done.3.rest_2_, bf16[192,2048]{1,0:T(8,128)(2,1)S(1)} %collective-permute-done.2.rest_1_, bf16[192,2048]{1,0:T(8,128)(2,1)S(1)} %collective-permute-done.1.rest_0_, bf16[192,2048]{1,0:T(8,128)(2,1)S(1)} %copy-done.2), kind=kLoop, calls=%fused_computation.2 | loop fusion | flops 3145728 | bytes 3932160 | tf_op jit(solution)/shard_map/broadcast_in_dim | solution.py:546
  164.5 1.0 broadcast_in_dim.29
  165.4 5.3 %all-to-all-start.2 = ((f32[16,12,768]{2,1,0:T(8,128)}), f32[16,12,768]{2,1,0:T(8,128)S(1)}, u32[]{:S(2)}, u32[]{:S(2)}) async-start(f32[16,12,768]{2,1,0:T(8,128)} %broadcast_in_dim.29), calls=%async_computation.2 | async-start | bytes 1572864 | tf_op jit(solution)/shard_map/all_to_all | solution.py:540
  170.7 12.4 %bwd2.1 = (bf16[192,2048]{1,0:T(8,128)(2,1)}, f32[192,2048]{1,0:T(8,128)}, f32[192,2048]{1,0:T(8,128)}) custom-call(bf16[3,2048,2048]{2,1,0:T(8,128)(2,1)} %get-tuple-element.44.e, bf16[3,128,2048]{2,1,0:T(8,128)(2,1)} %get-tuple-element.45.dob, bf16[192,2048]{1,0:T(8,128)(2,1)} %bitcast.36, ...), custom_call_target="tpu_custom_call", output_to_operand_aliasing={{0}: (8, {}), {1}: (9, {}), {2}: (10, {})} | custom-call | flops 13799999488 | tf_op jit(solution)/shard_map/bwd2/pallas_call | solution.py:456
  183.1 5.2 %merge.1 = (bf16[192,2048]{1,0:T(8,128)(2,1)}, bf16[192,2048]{1,0:T(8,128)(2,1)}, bf16[192,2048]{1,0:T(8,128)(2,1)}) custom-call(s32[3]{0:T(128)} %r_0_.3, bf16[192,2048]{1,0:T(8,128)(2,1)} %get-tuple-element.58.r_1_, f32[192,2048]{1,0:T(8,128)} %get-tuple-element.59.r_2_, f32[192,2048]{1,0:T(8,128)} %get-tuple-element.60.r_3_, ...), custom_call_target="tpu_custom_call" | custom-call | flops 5750000128 | tf_op jit(solution)/shard_map/merge/pallas_call | solution.py:480
  188.4 5.1 %all-to-all-done.2 = f32[16,12,768]{2,1,0:T(8,128)S(1)} async-done(((f32[16,12,768]{2,1,0:T(8,128)}), f32[16,12,768]{2,1,0:T(8,128)S(1)}, u32[]{:S(2)}, u32[]{:S(2)}) %all-to-all-start.2) | async-done | bytes 589856 | tf_op jit(solution)/shard_map/all_to_all | solution.py:540
  193.4 0.9 reshape.23
  (34 shorter events, 3.3 us)
Async XLA Ops:
  0.6 82.7 %collective-permute-start.6 = (bf16[192,2048]{1,0:T(8,128)(2,1)}, bf16[192,2048]{1,0:T(8,128)(2,1)S(1)}, u32[]{:S(2)}, u32[]{:S(2)}) collective-permute-start(bf16[192,2048]{1,0:T(8,128)(2,1)} %bitcast.28), channel_id=1, source_target_pairs={{0,12},{4,0},{8,4},{12,8},{1,13},{5,1},{9,5},{13,9},{2,14},{6,2},{... | collective-permute-start | bytes 2359304 | tf_op jit(solution)/shard_map/ppermute | solution.py:496
  4.0 79.3 %collective-permute-start.5 = (bf16[192,2048]{1,0:T(8,128)(2,1)}, bf16[192,2048]{1,0:T(8,128)(2,1)S(1)}, u32[]{:S(2)}, u32[]{:S(2)}) collective-permute-start(bf16[192,2048]{1,0:T(8,128)(2,1)} %bitcast.29), channel_id=1, source_target_pairs={{0,8},{4,12},{8,0},{12,4},{1,9},{5,13},{9,1},{13,5},{2,10},{6,14},... | collective-permute-start | bytes 2359304 | tf_op jit(solution)/shard_map/ppermute | solution.py:496
  4.5 78.8 %collective-permute-start.4 = (bf16[192,2048]{1,0:T(8,128)(2,1)}, bf16[192,2048]{1,0:T(8,128)(2,1)S(1)}, u32[]{:S(2)}, u32[]{:S(2)}) collective-permute-start(bf16[192,2048]{1,0:T(8,128)(2,1)} %bitcast.30), channel_id=1, source_target_pairs={{0,4},{4,8},{8,12},{12,0},{1,5},{5,9},{9,13},{13,1},{2,6},{6,10},{... | collective-permute-start | bytes 2359304 | tf_op jit(solution)/shard_map/ppermute | solution.py:496
  10.7 70.0 %all-to-all-start = ((bf16[8,2,192,128]{3,2,1,0:T(8,128)(2,1)}), bf16[8,2,192,128]{3,2,1,0:T(8,128)(2,1)S(1)}, u32[]{:S(2)}, u32[]{:S(2)}) async-start(bf16[8,2,192,128]{3,2,1,0:T(8,128)(2,1)} %broadcast_in_dim.24), calls=%async_computation | async-start | bytes 1572864 | tf_op jit(solution)/shard_map/all_to_all | solution.py:516
  80.6 0.9 copy-start
  81.5 9.0 %collective-permute-start = (bf16[8,2,192,128]{3,2,1,0:T(8,128)(2,1)}, bf16[8,2,192,128]{3,2,1,0:T(8,128)(2,1)S(1)}, u32[]{:S(2)}, u32[]{:S(2)}) collective-permute-start(bf16[8,2,192,128]{3,2,1,0:T(8,128)(2,1)} %hold.1.r_3_.r_9_), channel_id=1, source_target_pairs={{0,16},{16,0},{32,48},{48,32},{64,80},{80,64},{96,112},{112,96},{1... | collective-permute-start | bytes 2359304 | tf_op jit(solution)/shard_map/ppermute | solution.py:523
  83.3 0.9 copy-start.5
  83.3 1.2 copy-start.6
  83.3 1.4 copy-start.7
  90.5 0.9 copy-start.8
  111.9 4.2 %collective-permute-start.7 = (bf16[8,480,128]{2,1,0:T(8,128)(2,1)}, bf16[8,480,128]{2,1,0:T(8,128)(2,1)S(1)}, u32[]{:S(2)}, u32[]{:S(2)}) collective-permute-start(bf16[8,480,128]{2,1,0:T(8,128)(2,1)} %get-tuple-element.54), channel_id=1, source_target_pairs={{0,16},{16,0},{32,48},{48,32},{64,80},{80,64},{96,112},{112,96},{1... | collective-permute-start | bytes 2949128 | tf_op jit(solution)/shard_map/ppermute | solution.py:532
  112.0 47.8 %collective-permute-start.1 = (bf16[192,2048]{1,0:T(8,128)(2,1)}, bf16[192,2048]{1,0:T(8,128)(2,1)S(1)}, u32[]{:S(2)}, u32[]{:S(2)}) collective-permute-start(bf16[192,2048]{1,0:T(8,128)(2,1)} %get-tuple-element.41), channel_id=1, source_target_pairs={{0,4},{4,8},{8,12},{12,0},{1,5},{5,9},{9,13},{13,1},{2,6},{6,10},{... | collective-permute-start | bytes 2359304 | tf_op jit(solution)/shard_map/ppermute | solution.py:496
  113.6 46.9 %collective-permute-start.2 = (bf16[192,2048]{1,0:T(8,128)(2,1)}, bf16[192,2048]{1,0:T(8,128)(2,1)S(1)}, u32[]{:S(2)}, u32[]{:S(2)}) collective-permute-start(bf16[192,2048]{1,0:T(8,128)(2,1)} %get-tuple-element.42), channel_id=1, source_target_pairs={{0,8},{4,12},{8,0},{12,4},{1,9},{5,13},{9,1},{13,5},{2,10},{6,14},... | collective-permute-start | bytes 2359304 | tf_op jit(solution)/shard_map/ppermute | solution.py:496
  115.3 45.2 %collective-permute-start.3 = (bf16[192,2048]{1,0:T(8,128)(2,1)}, bf16[192,2048]{1,0:T(8,128)(2,1)}, u32[]{:S(2)}, u32[]{:S(2)}) collective-permute-start(bf16[192,2048]{1,0:T(8,128)(2,1)} %get-tuple-element.43), channel_id=1, source_target_pairs={{0,12},{4,0},{8,4},{12,8},{1,13},{5,1},{9,5},{13,9},{2,14},{6,2},{... | collective-permute-start | bytes 2359304 | tf_op jit(solution)/shard_map/ppermute | solution.py:496
  118.5 34.7 %all-to-all-start.1 = ((bf16[8,480,128]{2,1,0:T(8,128)(2,1)}), bf16[8,480,128]{2,1,0:T(8,128)(2,1)S(1)}, u32[]{:S(2)}, u32[]{:S(2)}) async-start(bf16[8,480,128]{2,1,0:T(8,128)(2,1)} %add_convert_fusion.rest_0_), calls=%async_computation.1 | async-start | bytes 1966080 | tf_op jit(solution)/shard_map/all_to_all | solution.py:534
  153.2 0.9 copy-start.1
  154.2 6.4 %copy-start.2 = (bf16[192,2048]{1,0:T(8,128)(2,1)S(1)}, bf16[192,2048]{1,0:T(8,128)(2,1)}, u32[]{:S(2)}) copy-start(bf16[192,2048]{1,0:T(8,128)(2,1)} %get-tuple-element.40) | copy-start | bytes 2359300
  156.7 6.7 %collective-permute-start.10 = (f32[12,768]{1,0:T(8,128)S(1)}, f32[12,768]{1,0:T(8,128)S(1)}, u32[]{:S(2)}, u32[]{:S(2)}) collective-permute-start(f32[12,768]{1,0:T(8,128)S(1)} %bitcast.23), channel_id=1, source_target_pairs={{0,3},{1,0},{2,1},{3,2},{4,7},{5,4},{6,5},{7,6},{8,11},{9,8},{10,9... | collective-permute-start | bytes 110600 | tf_op jit(solution)/shard_map/ppermute | solution.py:496
  159.5 4.5 %collective-permute-start.9 = (f32[12,768]{1,0:T(8,128)S(1)}, f32[12,768]{1,0:T(8,128)S(1)}, u32[]{:S(2)}, u32[]{:S(2)}) collective-permute-start(f32[12,768]{1,0:T(8,128)S(1)} %bitcast.24), channel_id=1, source_target_pairs={{0,2},{1,3},{2,0},{3,1},{4,6},{5,7},{6,4},{7,5},{8,10},{9,11},{10,... | collective-permute-start | bytes 110600 | tf_op jit(solution)/shard_map/ppermute | solution.py:496
  159.8 3.5 %copy-start.3 = (bf16[192,2048]{1,0:T(8,128)(2,1)}, bf16[192,2048]{1,0:T(8,128)(2,1)S(1)}, u32[]{:S(2)}) copy-start(bf16[192,2048]{1,0:T(8,128)(2,1)S(1)} %collective-permute-done.1.rest_0_) | copy-start | bytes 2359300
  159.8 4.6 %collective-permute-start.8 = (f32[12,768]{1,0:T(8,128)S(1)}, f32[12,768]{1,0:T(8,128)S(1)}, u32[]{:S(2)}, u32[]{:S(2)}) collective-permute-start(f32[12,768]{1,0:T(8,128)S(1)} %bitcast.25), channel_id=1, source_target_pairs={{0,1},{1,2},{2,3},{3,0},{4,5},{5,6},{6,7},{7,4},{8,9},{9,10},{10,1... | collective-permute-start | bytes 110600 | tf_op jit(solution)/shard_map/ppermute | solution.py:496
  160.5 2.8 %copy-start.4 = (bf16[192,2048]{1,0:T(8,128)(2,1)}, bf16[192,2048]{1,0:T(8,128)(2,1)S(1)}, u32[]{:S(2)}) copy-start(bf16[192,2048]{1,0:T(8,128)(2,1)S(1)} %collective-permute-done.2.rest_1_) | copy-start | bytes 2359300
  165.4 28.0 %all-to-all-start.2 = ((f32[16,12,768]{2,1,0:T(8,128)}), f32[16,12,768]{2,1,0:T(8,128)S(1)}, u32[]{:S(2)}, u32[]{:S(2)}) async-start(f32[16,12,768]{2,1,0:T(8,128)} %broadcast_in_dim.29), calls=%async_computation.2 | async-start | bytes 1572864 | tf_op jit(solution)/shard_map/all_to_all | solution.py:540

commit v3 on v2

v3 whole, which is shorter than its diff:
```python
import math

import jax
import jax.numpy as jnp
from jax import lax
from jax.experimental import pallas as pl
from jax.experimental.pallas import tpu as pltpu
from jax.sharding import PartitionSpec as P

SEL = 2048
HD = 64
NEGATIVE = -1e30
BF = jnp.bfloat16
F32 = jnp.float32
QB = 1024
CK = 512
SAFE = 2.0**40
VMEM_BYTES = 60 * 2**20


def dot(a, b, ca, cb):
    return lax.dot_general(a, b, (((ca,), (cb,)), ((), ())), preferred_element_type=F32)


def split2(x):
    hi = x.astype(BF)
    return hi, (x - hi.astype(F32)).astype(BF)


def split3(x):
    hi = x.astype(BF)
    rest = x - hi.astype(F32)
    mid = rest.astype(BF)
    return hi, mid, (rest - mid.astype(F32)).astype(BF)


def call(kern, name, grid, in_specs, out_specs, out_shape, scratch=(), us=1):
    return pl.pallas_call(
        kern,
        name=name,
        grid=grid,
        in_specs=in_specs,
        out_specs=out_specs,
        out_shape=out_shape,
        scratch_shapes=list(scratch),
        compiler_params=pltpu.CompilerParams(vmem_limit_bytes=VMEM_BYTES),
        cost_estimate=work(us),
    )


def work(us):
    return pl.CostEstimate(flops=int(us * 1.15e9), bytes_accessed=0, transcendentals=0)


SMEM = pl.BlockSpec(memory_space=pltpu.SMEM)
WHOLE = pl.BlockSpec(memory_space=pltpu.VMEM)


def sel_matrix(off, rate, rows, cols):
    pos = lax.broadcasted_iota(jnp.int32, (rows, cols), 0)
    num = lax.broadcasted_iota(jnp.int32, (rows, cols), 1)
    return jnp.where(pos == num * rate + off, 1.0, 0.0).astype(BF)


def place_matrix(off, rate, start, rows, cols):
    num = lax.broadcasted_iota(jnp.int32, (rows, cols), 0)
    pos = lax.broadcasted_iota(jnp.int32, (rows, cols), 1) + start
    return jnp.where(pos == num * rate + off, 1.0, 0.0).astype(BF)


def pick_kernel(rate, offs, q, k, v, qp, kvp):
    sel = sel_matrix(offs[pl.program_id(0)], rate, q.shape[1], qp.shape[1])
    got = dot(jnp.concatenate([q[...], k[...], v[...]], axis=0), sel, 1, 0).astype(BF)
    qp[...] = got[:HD]
    for c in range(kvp.shape[0]):
        kvp[c, 0] = got[HD : 2 * HD]
        kvp[c, 1] = got[2 * HD :]


def stack_rows(count, parts):
    row = lax.broadcasted_iota(jnp.int32, (count, parts[0].shape[1]), 0)
    out = jnp.zeros(row.shape, F32)
    for i, part in enumerate(parts):
        out = jnp.where(row == i, part.astype(F32), out)
    return out.astype(BF)


def fwd_kernel(info, q, k, v, qp, e_out, out, stats, pa, oa_p, lse_p, kt, qa, va):
    tok = k.shape[1]
    qb = out.shape[1]
    step = pl.program_id(1)

    @pl.when(step == 0)
    def _():
        pos = lax.broadcasted_iota(jnp.int32, (HD, tok), 1) + info[1]
        row = lax.broadcasted_iota(jnp.int32, (HD, tok), 0)
        bias = jnp.where(
            row == 0, jnp.where(pos >= info[0], NEGATIVE, 0.0), jnp.where(row == 1, -1.0, 0.0)
        )
        kt[...] = jnp.concatenate([k[...], bias.astype(BF)], axis=0).T
        one = jnp.where(row == 0, 1.0, 0.0).astype(BF)
        qa[...] = jnp.concatenate([q[...] * jnp.asarray(0.125, BF), one], axis=0)
        first = dot(kt[:256, :], qa[...], 1, 0)
        top = jnp.max(jnp.max(first.reshape(32, 8, tok), axis=0), axis=0, keepdims=True)
        qa[HD:, :] = jnp.where(row == 0, 1.0, jnp.where(row == 1, top, 0.0)).astype(BF)
        row16 = lax.broadcasted_iota(jnp.int32, (16, tok), 0)
        va[...] = jnp.concatenate([v[...], jnp.where(row16 == 0, 1.0, 0.0).astype(BF)], axis=0)

    base = pl.multiple_of(step * qb, qb)

    def finish(cols, acc):
        rt = 1.0 / acc[HD : HD + 1]
        out[:, cols] = acc[:HD] * rt
        stats[0, :, cols] = jnp.broadcast_to(rt, (8, rt.shape[1]))

    qc = qa[:, pl.ds(base, qb)]
    for i in range(0, tok, CK):
        e_out[0, i : i + CK, :] = jnp.exp(dot(kt[i : i + CK, :], qc, 1, 0)).astype(BF)
    acc = dot(va[...], e_out[0], 1, 0)
    finish(slice(0, qb), acc)
    total = acc[HD : HD + 1]
    unsafe = jnp.max(jnp.where(total < SAFE, 0.0, 1.0)) > 0.0

    @pl.when(step == pl.num_programs(1) - 1)
    def _():
        qs = qp[...] * jnp.asarray(0.125, BF)
        here = lax.broadcasted_iota(jnp.int32, (1, tok), 1)
        s = jnp.where(here + info[1] < info[0], dot(qs, k[...], 0, 0), NEGATIVE)
        p, lse = softmax_rows(s)
        pa[0] = p
        oa_p[0] = dot(p, v[...], 1, 1)
        lse_p[0] = jnp.broadcast_to(lse, lse_p.shape[1:])

    @pl.when(unsafe)
    def _():
        width = 128

        def redo(n, carry):
            c0 = pl.multiple_of(n * width, width)
            cols = pl.ds(c0, width)
            s = dot(kt[...], qa[:, pl.ds(pl.multiple_of(base + c0, width), width)], 1, 0)
            s = s - jnp.max(s, axis=0, keepdims=True)
            e_out[0, :, cols] = jnp.exp(s).astype(BF)
            finish(cols, dot(va[...], e_out[0, :, cols], 1, 0))
            return carry

        lax.fori_loop(0, qb // width, redo, 0)


def softmax_rows(s):
    m = jnp.max(s, axis=1, keepdims=True)
    e = jnp.exp(s - m)
    t = jnp.sum(e, axis=1, keepdims=True)
    return (e * (1.0 / t)).astype(BF), m + jnp.log(t)


def far_parts(kv_own, kv_oth, rows):
    both = [ref.at[c] for ref in (kv_own, kv_oth) for c in range(ref.shape[0])]
    return tuple(jnp.concatenate([ref[n, rows, :] for ref in both], axis=1) for n in range(2))


def mid_kernel(
    rate, info, offs, qp, kv_own, kv_oth, k, v, stats, w, pa, oa_p, lse_p, out_a, c0, c1, c2, c3,
    t0, t1, t2, t3, dob, kept, sent, dqp, dkp, dvp,
    wt, attn, pb, g_buf, oa, cot, t_buf, dob_buf, in_sems, out_sems,
):
    part = c0.shape[0]
    count = cot.shape[0] // part
    heads = pa.shape[0]
    tok = attn.shape[1]
    picks = qp.shape[1]
    chips = kv_own.shape[0]
    width = heads * HD
    length, start, core = info[0], info[1], info[3]
    oa_copy = pltpu.make_async_copy(out_a, oa, in_sems.at[count])
    oa_copy.start()
    copies = []
    for s, block in enumerate((c0, c1, c2, c3)):
        owner = lax.rem(info[2] + (count - s), count)
        there = cot.at[pl.ds(pl.multiple_of(owner * part, part), part), :]
        copies.append(pltpu.make_async_copy(block, there, in_sems.at[s]))
        copies[-1].start()

    here = lax.broadcasted_iota(jnp.int32, (1, tok), 1)
    keep = jnp.where(here + start < length, 1.0, 0.0)
    num = lax.broadcasted_iota(jnp.int32, (1, 2 * chips * picks), 1)
    chunk = num // picks
    rank = 2 * (chunk % chips) + jnp.where(chunk < chips, core, 1 - core)
    far_pos = (rank * picks + num % picks) * rate
    pick_pos = lax.broadcasted_iota(jnp.int32, (picks, 1), 0) * rate + start
    wt[...] = w[...].T
    kept_parts = []
    mixed_parts = []
    for h in range(heads):
        rows = slice(h * HD, (h + 1) * HD)
        off = offs[h]
        kf, vf = far_parts(kv_own, kv_oth, rows)
        qs = qp[rows, :] * jnp.asarray(0.125, BF)
        p_b, lse_b = softmax_rows(
            jnp.where(far_pos + off < length, dot(qs, kf, 0, 0), NEGATIVE)
        )
        pb[h] = p_b
        o_b = dot(p_b, vf, 1, 1)
        o_a, lse_a = oa_p[h], lse_p[h, :, :1]
        gap = lse_a - lse_b
        near = 1.0 / (1.0 + jnp.exp(-gap))
        far = 1.0 / (1.0 + jnp.exp(gap))
        kept_parts.append((o_a, o_b, near, far))
        live = jnp.where(pick_pos + off < length, 1.0, 0.0)
        mixed_parts.append(((near * o_a + far * o_b) * live).astype(BF))
    oa_copy.wait()
    for h in range(heads):
        rows = slice(h * HD, (h + 1) * HD)
        spread = dot(mixed_parts[h], place_matrix(offs[h], rate, 0, picks, tok), 0, 0)
        attn[rows, :] = jnp.where(
            (here % rate) == offs[h], spread, oa[rows, :] * keep
        ).astype(BF)
    sends = []
    for s, term in enumerate((t0, t1, t2, t3)):
        owner = lax.rem(info[2] + s, count)
        out_rows = pl.ds(pl.multiple_of(owner * part, part), part)
        t_buf[s] = dot(wt[out_rows, :], attn[...], 1, 0).astype(BF)
        sends.append(pltpu.make_async_copy(t_buf.at[s], term, out_sems.at[s]))
        sends[-1].start()

    for copy in copies:
        copy.wait()
    for h in range(heads):
        rows = slice(h * HD, (h + 1) * HD)
        g_all = dot(w[rows, :], cot[...], 1, 0).astype(BF).astype(F32) * keep
        g_buf[rows, :] = g_all.astype(BF)
        g = jnp.where((here % rate) == offs[h], 0.0, g_all)
        rt = stats[h, 0:1, :]
        delta = jnp.sum(g * oa[rows, :], axis=0, keepdims=True)
        c_hi, c_lo = split2(-delta * rt)
        dob_buf[h] = jnp.concatenate(
            [(g * rt).astype(BF), stack_rows(HD, [c_hi, c_lo])], axis=0
        )
    sends.append(pltpu.make_async_copy(dob_buf, dob, out_sems.at[count]))
    sends[-1].start()

    for h in range(heads):
        rows = slice(h * HD, (h + 1) * HD)
        g = dot(sel_matrix(offs[h], rate, tok, picks), g_buf[rows, :], 0, 1)
        o_a, o_b, near, far = kept_parts[h]
        dlse = near * far * jnp.sum(g * (o_a - o_b), axis=1, keepdims=True)
        kf, vf = far_parts(kv_own, kv_oth, rows)
        q = qp[rows, :]

        def back(k_all, v_all, p, do, out, dl):
            delta = jnp.sum(do.astype(F32) * out, axis=1, keepdims=True)
            dp = dot(do, v_all, 1, 0) + (dl - delta)
            ds = (p.astype(F32) * dp * 0.125).astype(BF)
            return dot(ds, k_all, 1, 1), dot(q, ds, 1, 0), dot(do, p, 0, 0)

        dq_a, dk_a, dv_a = back(k[rows, :], v[rows, :], pa[h], (near * g).astype(BF), o_a, dlse)
        dq_b, dk_b, dv_b = back(kf, vf, pb[h], (far * g).astype(BF), o_b, -dlse)
        dqp[h] = (dq_a + dq_b).astype(BF)
        dkp[rows, :] = dk_a.astype(BF)
        dvp[rows, :] = dv_a.astype(BF)
        for n, grad in enumerate((dk_b.astype(BF), dv_b.astype(BF))):
            first = n * width + h * HD
            for i, ref in enumerate((kept, sent)):
                for c in range(chips):
                    cols = slice((i * chips + c) * picks, (i * chips + c + 1) * picks)
                    ref[c, first : first + HD, :] = grad[:, cols]
    grad = dot(attn[...], cot[...], 1, 1)
    size = grad.shape[0] // chips
    half = grad.shape[1] // 2
    blank = jnp.zeros((32 - size, picks), F32)
    for side in range(2):

        @pl.when(core == side)
        def _():
            for ref, parity in ((kept, side), (sent, 1 - side)):
                for c in range(chips):
                    for n in range(half // picks):
                        left = parity * half + n * picks
                        piece = grad[c * size : (c + 1) * size, left : left + picks]
                        first = 2 * width + 32 * n
                        ref[c, first : first + 32, :] = jnp.concatenate(
                            [piece, blank], axis=0
                        ).astype(BF)
    for send in sends:
        send.wait()


def bwd_step(rate, off, e, dob, q, k, v, dqp, dkp, dvp, dq, dk, dv, vt):
    tok = k.shape[1]
    qb = q.shape[1]
    step = pl.program_id(1)

    @pl.when(step == 0)
    def _():
        row = lax.broadcasted_iota(jnp.int32, (HD, tok), 0)
        ones = jnp.where(row < 2, 1.0, 0.0).astype(BF)
        vt[...] = jnp.concatenate([v[...], ones], axis=0).T
        dk[...] = dkp[...].astype(F32) * 8.0
        dv[...] = dvp[...].astype(F32)

    do = dob[0, :HD, :]
    acc = None
    for i in range(0, tok, CK):
        dp = dot(vt[i : i + CK, :], dob[0], 1, 0)
        ei = e[0, i : i + CK, :]
        ds = (ei.astype(F32) * dp).astype(BF)
        part = dot(k[:, i : i + CK], ds, 1, 0)
        acc = part if acc is None else acc + part
        dk[:, i : i + CK] += dot(q[...], ds, 1, 1)
        dv[:, i : i + CK] += dot(do, ei, 1, 1)
    place = place_matrix(off, rate, step * qb, dqp.shape[1], qb)
    dq[...] = (acc * 0.125 + dot(dqp[0], place, 0, 0)).astype(BF)


def bwd_kernel(rate, offs, e, dob, q, k, v, dqp, dkp, dvp, dq, dk, dv, vt):
    off = offs[pl.program_id(0)]
    bwd_step(rate, off, e, dob, q, k, v, dqp, dkp, dvp, dq, dk, dv, vt)


def far_sum(rate, off, far_k, far_v, tok):
    sums = []
    for parts in (far_k, far_v):
        total = parts[0].astype(F32)
        for r in range(1, parts.shape[0]):
            total = total + parts[r].astype(F32)
        sums.append(total.astype(BF))
    place = place_matrix(off, rate, 0, far_k.shape[2], tok)
    return dot(jnp.concatenate(sums, axis=0), place, 1, 0)


def last_kernel(
    rate, last, offs, e, dob, q, k, v, dqp, dkp, dvp, far_k, far_v,
    dk_old, dv_old, old_k, old_v, t0, t1, t2, t3, dq_old,
    dq, kg, vg, mixed, dk, dv, k_buf, v_buf, vt, sems,
):
    tok = k.shape[1]
    step = pl.program_id(1)
    bwd_step(rate, offs[last], e, dob, q, k, v, dqp, dkp, dvp, dq, dk, dv, vt)

    def store(slot, head, near_k, near_v, spread):
        k_buf[slot] = (near_k * 0.125 + spread[:HD]).astype(BF)
        v_buf[slot] = (near_v + spread[HD:]).astype(BF)
        rows = pl.ds(pl.multiple_of(head * HD, HD), HD)
        for n, (buf, out) in enumerate(((k_buf, kg), (v_buf, vg))):
            pltpu.make_async_copy(buf.at[slot], out.at[rows, :], sems.at[slot, n]).start()

    def wait(slot):
        for n, (buf, out) in enumerate(((k_buf, kg), (v_buf, vg))):
            pltpu.make_async_copy(buf.at[slot], out.at[:HD, :], sems.at[slot, n]).wait()

    store(step, step, dk_old[...], dv_old[...], far_sum(rate, offs[step], old_k, old_v, tok))
    total = t0[...].astype(F32)
    for t in (t1, t2, t3):
        total = total + t[...].astype(F32)
    mixed[...] = total.astype(BF)

    @pl.when(step == last - 1)
    def _():
        store(last, last, dk[...], dv[...], far_sum(rate, offs[last], far_k, far_v, tok))
        for slot in range(last + 1):
            wait(slot)


SDS = jax.ShapeDtypeStruct


def pick(rate, offs, q, k, v, picks, copies):
    rows, tok = q.shape
    by_head = pl.BlockSpec((HD, tok), lambda h: (h, 0))
    return call(
        lambda *r: pick_kernel(rate, *r), "pick", (rows // HD,),
        [SMEM, by_head, by_head, by_head],
        [
            pl.BlockSpec((HD, picks), lambda h: (h, 0)),
            pl.BlockSpec((copies, 2, HD, picks), lambda h: (0, 0, h, 0)),
        ],
        [SDS((rows, picks), BF), SDS((copies, 2, rows, picks), BF)],
        us=2,
    )(offs, q, k, v)


def forward(info, q, k, v, qp):
    rows, tok = q.shape
    heads = rows // HD
    picks = qp.shape[1]
    qb = min(QB, tok)
    by_q = pl.BlockSpec((HD, qb), lambda h, j: (h, j))
    whole = pl.BlockSpec((HD, tok), lambda h, j: (h, 0))
    by_h = lambda n: pl.BlockSpec((1, picks, n), lambda h, j: (h, 0, 0))
    return call(
        fwd_kernel, "fwd", (heads, tok // qb),
        [SMEM, whole, whole, whole, pl.BlockSpec((HD, picks), lambda h, j: (h, 0))],
        [
            pl.BlockSpec((1, tok, qb), lambda h, j: (h, 0, j)),
            by_q,
            pl.BlockSpec((1, 8, qb), lambda h, j: (h, 0, j)),
            by_h(tok), by_h(HD), by_h(HD),
        ],
        [
            SDS((heads, tok, tok), BF), SDS((rows, tok), F32), SDS((heads, 8, tok), F32),
            SDS((heads, picks, tok), BF), SDS((heads, picks, HD), F32),
            SDS((heads, picks, HD), F32),
        ],
        scratch=[
            pltpu.VMEM((tok, 2 * HD), BF), pltpu.VMEM((2 * HD, tok), BF),
            pltpu.VMEM((HD + 16, tok), BF),
        ],
        us=18,
    )(info, q, k, v, qp)


def middle(rate, info, offs, qp, kv_own, kv_oth, k, v, stats, w, near, out_a, blocks):
    rows, tok = k.shape
    heads = rows // HD
    picks = qp.shape[1]
    count = len(blocks)
    chips = kv_own.shape[0]
    far = 2 * chips * picks
    anywhere = pl.BlockSpec(memory_space=pl.ANY)
    half = SDS((chips, 2 * rows + 16 * (count * rows // picks), picks), BF)
    dob = (heads, 2 * HD, tok)
    return call(
        lambda *r: mid_kernel(rate, *r), "mid", (),
        [SMEM, SMEM] + [WHOLE] * 10 + [anywhere] * 5,
        [anywhere] * 5 + [WHOLE] * 5,
        [SDS((rows, tok), BF)] * count
        + [
            SDS(dob, BF), half, half, SDS((heads, picks, HD), BF), SDS((rows, tok), BF),
            SDS((rows, tok), BF),
        ],
        scratch=[
            pltpu.VMEM((count * rows, rows), BF), pltpu.VMEM((rows, tok), BF),
            pltpu.VMEM((heads, picks, far), BF),
            pltpu.VMEM((rows, tok), BF), pltpu.VMEM((rows, tok), F32),
            pltpu.VMEM((count * rows, tok), BF), pltpu.VMEM((count, rows, tok), BF),
            pltpu.VMEM(dob, BF), pltpu.SemaphoreType.DMA((count + 1,)),
            pltpu.SemaphoreType.DMA((count + 1,)),
        ],
        us=20,
    )(info, offs, qp, kv_own, kv_oth, k, v, stats, w, *near, out_a, *blocks)


def hold_all(arrays, after):
    anywhere = pl.BlockSpec(memory_space=pl.ANY)
    count = len(arrays)
    return pl.pallas_call(
        lambda *refs: None, name="hold", in_specs=[anywhere] * (count + 1),
        out_specs=[anywhere] * count, out_shape=[SDS(x.shape, x.dtype) for x in arrays],
        input_output_aliases={i: i for i in range(count)},
    )(*arrays, after)


def hold(x, after):
    return hold_all([x], after)[0]


def total_kernel(parts, after, out):
    total = parts[0].astype(F32)
    for r in range(1, parts.shape[0]):
        total = total + parts[r].astype(F32)
    cols = total.shape[1]
    mine = jnp.concatenate(
        [total[r : r + out.shape[1]] for r in range(0, total.shape[0], 32)], axis=1
    )
    for r in range(out.shape[0]):
        out[r] = mine


def total(parts, first, size, copies, after):
    count, rows, cols = parts.shape
    rows -= first
    shape = (copies, size, rows // 32 * cols)
    return call(
        total_kernel, "total", (1,),
        [
            pl.BlockSpec((count, rows, cols), lambda i: (0, first // rows, 0)),
            pl.BlockSpec(memory_space=pl.ANY),
        ],
        pl.BlockSpec(shape, lambda i: (0, 0, 0)),
        SDS(shape, F32), us=1,
    )(parts, after)


def spread_kernel(scale, parts, out):
    mine = parts[0]
    for r in range(1, parts.shape[0]):
        mine = mine + parts[r]
    mine = mine * scale
    for r in range(out.shape[0]):
        out[r] = mine


def spread_sum(scale, parts, copies):
    return call(
        lambda *r: spread_kernel(scale, *r), "spread", (), [WHOLE], WHOLE,
        SDS((copies,) + parts.shape[1:], F32), us=1,
    )(parts)


def backward_specs(first, rows, tok, picks):
    qb = min(QB, tok)
    by_q = pl.BlockSpec((HD, qb), lambda h, j: (first + h, j))
    whole = pl.BlockSpec((HD, tok), lambda h, j: (first + h, 0))
    ins = [
        SMEM,
        pl.BlockSpec((1, tok, qb), lambda h, j: (first + h, 0, j)),
        pl.BlockSpec((1, 2 * HD, qb), lambda h, j: (first + h, 0, j)),
        by_q, whole, whole, pl.BlockSpec((1, picks, HD), lambda h, j: (first + h, 0, 0)),
        whole, whole,
    ]
    return qb, by_q, whole, ins


def backward(heads, rate, offs, e, dob, q, k, v, dqp, dkp, dvp, after):
    rows, tok = q.shape
    qb, by_q, whole, ins = backward_specs(0, rows, tok, dqp.shape[1])
    spare = [pl.BlockSpec(memory_space=pl.ANY)] * len(after)

    def kernel(*refs):
        bwd_kernel(rate, *refs[:9], *refs[9 + len(after) :])

    return call(
        kernel, "bwd", (heads, tok // qb), ins + spare, [by_q, whole, whole],
        [SDS((rows, tok), BF)] + [SDS((heads * HD, tok), F32)] * 2,
        scratch=[pltpu.VMEM((tok, 2 * HD), BF)],
        us=11 * heads,
    )(offs, e, dob, q, k, v, dqp, dkp, dvp, *after)


def backward_last(rate, offs, e, dob, q, k, v, dqp, dkp, dvp, far, dq_old, dk_old, dv_old, terms):
    rows, tok = q.shape
    heads = rows // HD
    last = heads - 1
    chips, _, picks = far.shape
    qb, by_q, whole, ins = backward_specs(last, rows, tok, picks)
    assert tok // qb == last
    anywhere = pl.BlockSpec(memory_space=pl.ANY)
    of = lambda at: pl.BlockSpec((chips, HD, picks), lambda h, j: (0, at(j), 0))
    old = pl.BlockSpec((HD, tok), lambda h, j: (j, 0))
    slab = pl.BlockSpec((rows // last, tok), lambda h, j: (j, 0))
    ins = ins + [of(lambda j: last), of(lambda j: heads + last), old, old]
    ins = ins + [of(lambda j: j), of(lambda j: heads + j)] + [slab] * len(terms) + [anywhere]
    buf = pltpu.VMEM((heads, HD, tok), BF)
    return pl.pallas_call(
        lambda *r: last_kernel(rate, last, *r),
        name="last",
        grid=(1, tok // qb),
        in_specs=ins,
        out_specs=[by_q, anywhere, anywhere, slab],
        out_shape=[SDS((rows, tok), BF)] * 4,
        scratch_shapes=[
            pltpu.VMEM((HD, tok), F32), pltpu.VMEM((HD, tok), F32), buf, buf,
            pltpu.VMEM((tok, 2 * HD), BF), pltpu.SemaphoreType.DMA((heads, 2)),
        ],
        input_output_aliases={len(ins) - 1: 0},
        compiler_params=pltpu.CompilerParams(vmem_limit_bytes=VMEM_BYTES),
        cost_estimate=work(13),
    )(offs, e, dob, q, k, v, dqp, dkp, dvp, far, far, dk_old, dv_old, far, far, *terms, dq_old)


def shift(x, axis, by):
    count = lax.axis_size(axis)
    return lax.ppermute(x, axis, [(i, (i + by) % count) for i in range(count)])


def shards(queries, keys, values, cotangent, w_out, lengths, offsets):
    rows, tok = queries.shape[1:]
    seq_count = lax.axis_size("seq")
    rate = tok * seq_count // SEL
    picks = tok // rate
    place = lax.axis_index("seq").astype(jnp.int32)
    info = jnp.stack(
        [
            lengths[0], place * tok, lax.axis_index("head").astype(jnp.int32), place % 2,
            place // 2,
        ]
    )
    q, k, v = queries[0], keys[0], values[0]
    groups = [list(range(c, seq_count, 2)) for c in range(2)]
    chips = seq_count // 2
    swap = [(i, i ^ 1) for i in range(seq_count)]
    qp, kvp = pick(rate, offsets, q, k, v, picks, chips)
    kv_own = lax.all_to_all(kvp, "seq", 0, 0, axis_index_groups=groups)
    own = cotangent[0]
    blocks = [own] + [shift(own, "head", s) for s in (1, 2, 3)]
    e, out_a, stats, *near = forward(info, q, k, v, qp)
    kv_own = hold(kv_own, stats)
    kv_oth = lax.ppermute(kv_own, "seq", swap)
    *terms, dob, kept, sent, dqp, dkp, dvp = middle(
        rate, info, offsets, qp, kv_own, kv_oth, k, v, stats, w_out, near, out_a, blocks
    )
    got = lax.ppermute(sent, "seq", swap)
    pair = (kept.astype(F32) + got.astype(F32)).astype(BF)
    far = lax.all_to_all(pair, "seq", 0, 0, axis_index_groups=groups)
    later = hold_all(terms[1:], pair)
    terms = terms[:1] + [shift(t, "head", s + 1) for s, t in enumerate(later)]
    dq, dk, dv = backward(2, rate, offsets, e, dob, q, k, v, dqp, dkp, dvp, (pair,))
    grad_scale = 1.0 / math.sqrt(tok * seq_count * lax.axis_size("dp"))
    mine = total(far, 2 * rows, rows // chips, lax.axis_size("dp"), dk)
    mine = lax.all_to_all(mine, "dp", 0, 0)
    spread = lax.all_to_all(spread_sum(grad_scale, mine, seq_count), "seq", 0, 0)
    spread = spread.reshape((chips, 2) + spread.shape[1:])
    weight_grad = spread.transpose(0, 2, 1, 3).reshape(w_out.shape)
    dq, kg, vg, mixed = backward_last(
        rate, offsets, e, dob, q, k, v, dqp, dkp, dvp, far, dq, dk, dv, terms
    )
    return (mixed[None], dq[None], kg[None], vg[None], weight_grad)


def solution(mesh):
    full = P("dp", "head", "seq")
    return jax.shard_map(
        shards,
        mesh=mesh,
        in_specs=(full, full, full, full, P("head", None), P("dp"), P("head")),
        out_specs=(full, full, full, full, P("head", None)),
        check_vma=False,
    )
```

time: 195 us -> 185 us (0.949)
  blocking collectives: 0 us -> 9.2 us
  Pallas kernels: 131 us -> 124 us
  waiting for transfers between devices: 12.6 us -> 7.77 us
  local copies, waits for them, and re-layouts: 9.39 us -> 5.91 us
  other arithmetic: 5.22 us -> 2.47 us
    all_to_all x0 -> x1, blocking collectives: none -> 9.2 us  [shards(): mine = lax.all_to_all(mine, 'dp', 0, 0)]
    pallas_call x8 -> x7, Pallas kernels: 126 us -> 119 us  [the longest x1 63.8 us: forward(): call(fwd_kernel, 'fwd', (heads, tok // qb), [SMEM, whole, whole, whole, p...]
    all_to_all x1, waiting for transfers between devices: 6.39 us -> 1.8 us  [shards(): far = lax.all_to_all(pair, 'seq', 0, 0, axis_index_groups=groups)]
    ppermute x9 -> x6, starting transfers between devices: 12.5 us -> 8.6 us  [shift(): return lax.ppermute(x, axis, [(i, (i + by) % count) for i in range(count)])]
    all_to_all x2, waiting for transfers between devices: 5.08 us -> 1.46 us  [the longest x1 1.46 us: shards(): lax.all_to_all(spread_sum(grad_scale, mine, seq_count), 'seq', 0, 0)]
    broadcast_in_dim x2 -> x0, local copies, waits for them, and re-layouts: 2.88 us -> none  [the longest x1 1.92 us: shards(): jnp.broadcast_to(kvp[None], (chips,) + kvp.shape)]
    broadcast_in_dim x1 -> x0, other arithmetic: 2.8 us -> none  [shards(): return (mixed[None], qg[None], kg[None], vg[None], weight_grad)]
    all_to_all x2, starting transfers between devices: 13.5 us -> 16.1 us  [the longest x1 8.19 us: shards(): kv_own = lax.all_to_all(kvp, 'seq', 0, 0, axis_index_groups=groups)]
  transfers between devices with their start and end apart: 14 -> 11, of which waited for: 4 -> 4; matrix products, arithmetic and copies ran while one was open for 4% -> 0% of each run, Pallas kernels for 57% -> 59%
where the time goes in v3:
time: 185 us
  Pallas kernels  124 us (67%)
  starting transfers between devices  33.9 us (18%)
  blocking collectives  9.2 us (5%)
  waiting for transfers between devices  7.77 us (4%)
  local copies, waits for them, and re-layouts  5.91 us (3%)
  other arithmetic  2.47 us (1%)
    pallas_call x1, Pallas kernels, forward(): call(fwd_kernel, 'fwd', (heads, tok // qb), [SMEM, whole, whole, whole, p...  63.8 us
    pallas_call x1, Pallas kernels, backward(): call(kernel, 'bwd', (heads, tok // qb), ins + spare, [by_q, whole, whole]...  21.9 us
    pallas_call x1, Pallas kernels, backward_last(): pl.pallas_call(lambda *r: last_kernel(rate, last, *r), name='last', grid=...  15.8 us
    pallas_call x1, Pallas kernels, middle(): call(lambda *r: mid_kernel(rate, *r), 'mid', (), [SMEM, SMEM] + [WHOLE] *...  15.4 us
    all_to_all x1, blocking collectives, shards(): mine = lax.all_to_all(mine, 'dp', 0, 0)  9.2 us
    ppermute x6, starting transfers between devices, shift(): return lax.ppermute(x, axis, [(i, (i + by) % count) for i in range(count)])  8.6 us
    all_to_all x1, starting transfers between devices, shards(): kv_own = lax.all_to_all(kvp, 'seq', 0, 0, axis_index_groups=groups)  8.19 us
    all_to_all x1, starting transfers between devices, shards(): lax.all_to_all(spread_sum(grad_scale, mine, seq_count), 'seq', 0, 0)  7.91 us
  transfers between devices with their start and end apart: 11, of which 4 were waited for; matrix products, arithmetic and copies ran while one was open for 0% of the time, Pallas kernels for 59%

profile of v3, /device:TPU:1, one launch (start us, length us, event | category | flops | bytes accessed | tf_op | source)
XLA Modules:
  0.0 184.8 jit_solution(17236862180747450417)
XLA Ops:
  0.6 3.4 %collective-permute-start.3 = (bf16[192,2048]{1,0:T(8,128)(2,1)}, bf16[192,2048]{1,0:T(8,128)(2,1)S(1)}, u32[]{:S(2)}, u32[]{:S(2)}) collective-permute-start(bf16[192,2048]{1,0:T(8,128)(2,1)} %bitcast.21), channel_id=1, source_target_pairs={{0,12},{4,0},{8,4},{12,8},{1,13},{5,1},{9,5},{13,9},{2,14},{6,2},{... | collective-permute-start | bytes 2359304 | tf_op jit(solution)/shard_map/ppermute | solution.py:563
  4.0 0.5 collective-permute-start.2
  4.5 0.6 collective-permute-start.1
  5.1 3.8 %pick.1 = (bf16[192,128]{1,0:T(8,128)(2,1)}, bf16[8,2,192,128]{3,2,1,0:T(8,128)(2,1)}) custom-call(s32[3]{0:T(128)} %r_0_.3, bf16[192,2048]{1,0:T(8,128)(2,1)} %bitcast.25, bf16[192,2048]{1,0:T(8,128)(2,1)} %bitcast.29, bf16[192,2048]{1,0:T(8,128)(2,1)} %bitcast.34), custom_call_target="tpu_custom_call" | custom-call | flops 2300000000 | tf_op jit(solution)/shard_map/pick/pallas_call | solution.py:370
  8.9 8.2 %all-to-all-start = ((bf16[8,2,192,128]{3,2,1,0:T(8,128)(2,1)}), bf16[8,2,192,128]{3,2,1,0:T(8,128)(2,1)S(1)}, u32[]{:S(2)}, u32[]{:S(2)}) async-start(bf16[8,2,192,128]{3,2,1,0:T(8,128)(2,1)} %get-tuple-element.35), calls=%async_computation | async-start | bytes 1572864 | tf_op jit(solution)/shard_map/all_to_all | solution.py:583
  17.8 0.6 stack.19.info.r_0_
  18.4 63.8 %fwd.1 = (bf16[3,2048,2048]{2,1,0:T(8,128)(2,1)}, f32[192,2048]{1,0:T(8,128)}, f32[3,8,2048]{2,1,0:T(8,128)}, bf16[3,128,2048]{2,1,0:T(8,128)(2,1)}, f32[3,128,64]{2,1,0:T(8,128)}, /*index=5*/f32[3,128,64]{2,1,0:T(8,128)}) custom-call(s32[5]{0:T(128)} %stack.19.info.r_0_, bf16[192,2048]{1,0:T(8,128)(2,1)} %bitcast.26, bf16[192,2048]{1,0:T(8,128)(2,1)} %bitcast.30, ...), custom_call_target="tpu_custom_call" | custom-call | flops 20700000256 | tf_op jit(solution)/shard_map/fwd/pallas_call | solution.py:390
  82.3 0.9 copy-done
  83.1 1.8 collective-permute-start
  85.0 2.1 %collective-permute-done.r_4_ = bf16[8,2,192,128]{3,2,1,0:T(8,128)(2,1)S(1)} collective-permute-done((bf16[8,2,192,128]{3,2,1,0:T(8,128)(2,1)}, bf16[8,2,192,128]{3,2,1,0:T(8,128)(2,1)S(1)}, u32[]{:S(2)}, u32[]{:S(2)}) %collective-permute-start) | collective-permute-done | bytes 786464 | tf_op jit(solution)/shard_map/ppermute | solution.py:588
  87.1 0.9 copy-done.8
  87.9 15.4 %mid.1 = (bf16[192,2048]{1,0:T(8,128)(2,1)}, bf16[192,2048]{1,0:T(8,128)(2,1)}, bf16[192,2048]{1,0:T(8,128)(2,1)}, bf16[192,2048]{1,0:T(8,128)(2,1)}, bf16[3,128...) custom-call(s32[5]{0:T(128)} %stack.19.info.r_0_, ...), custom_call_target="tpu_custom_call" | custom-call | flops 23000000512 | tf_op jit(solution)/shard_map/mid/pallas_call | solution.py:422
  103.4 0.5 collective-permute-start.4
  103.8 2.4 %collective-permute-done.4 = bf16[8,480,128]{2,1,0:T(8,128)(2,1)S(1)} collective-permute-done((bf16[8,480,128]{2,1,0:T(8,128)(2,1)}, bf16[8,480,128]{2,1,0:T(8,128)(2,1)S(1)}, u32[]{:S(2)}, u32[]{:S(2)}) %collective-permute-start.4) | collective-permute-done | bytes 983072 | tf_op jit(solution)/shard_map/ppermute | solution.py:592
  106.2 2.5 %add_convert_fusion.refs_9_.refs_3_ = bf16[8,480,128]{2,1,0:T(8,128)(2,1)} fusion(bf16[8,480,128]{2,1,0:T(8,128)(2,1)S(1)} %collective-permute-done.4, bf16[8,480,128]{2,1,0:T(8,128)(2,1)} %get-tuple-element.45), kind=kLoop, calls=%fused_computation | loop fusion | flops 1966080 | bytes 2949120 | tf_op jit(solution)/shard_map/convert_element_type | solution.py:593
  108.7 6.9 %all-to-all-start.1 = ((bf16[8,480,128]{2,1,0:T(8,128)(2,1)}), bf16[8,480,128]{2,1,0:T(8,128)(2,1)S(1)}, u32[]{:S(2)}, u32[]{:S(2)}) async-start(bf16[8,480,128]{2,1,0:T(8,128)(2,1)} %add_convert_fusion.refs_9_.refs_3_), calls=%async_computation.1 | async-start | bytes 1966080 | tf_op jit(solution)/shard_map/all_to_all | solution.py:594
  115.6 1.6 collective-permute-start.5
  117.2 1.7 collective-permute-start.6
  119.0 0.8 collective-permute-start.7
  119.7 21.9 %bwd.1 = (bf16[192,2048]{1,0:T(8,128)(2,1)}, f32[128,2048]{1,0:T(8,128)}, f32[128,2048]{1,0:T(8,128)}) custom-call(s32[3]{0:T(128)} %r_0_.3, bf16[3,2048,2048]{2,1,0:T(8,128)(2,1)} %get-tuple-element.34.refs_1_.r_1_, bf16[3,128,2048]{2,1,0:T(8,128)(2,1)} %get-tuple-element.41.refs_2_.r_2_, bf16[192,2048]{1,0:T(8,128)(2,1)} %bitcast.27, ...), custom_call_target="tpu_custom_call" | custom-call | flops 25300000768 | tf_op jit(solution)/shard_map/bwd/pallas_call | solution.py:522
  141.6 1.8 all-to-all-done.1.r_9_.r_10_.r_13_.r_14_.parts
  143.4 1.0 copy-done.1
  144.4 1.6 total.1
  146.1 9.2 %all_to_all.20.r_0_ = f32[4,24,384]{2,1,0:T(8,128)} all-to-all(f32[4,24,384]{2,1,0:T(8,128)} %total.1), channel_id=1, replica_groups=mesh['seq'=16,'head'=4,'dp'=4] {'dp'}, dimensions={0} | all-to-all | bytes 294912 | tf_op jit(solution)/shard_map/all_to_all | solution.py:600
  155.3 1.8 spread.1
  157.0 7.9 %all-to-all-start.3 = ((f32[16,24,384]{2,1,0:T(8,128)}), f32[16,24,384]{2,1,0:T(8,128)S(1)}, u32[]{:S(2)}, u32[]{:S(2)}) async-start(f32[16,24,384]{2,1,0:T(8,128)} %spread.1), calls=%async_computation.3 | async-start | bytes 1179648 | tf_op jit(solution)/shard_map/all_to_all | solution.py:601
  165.0 0.8 copy-done.5
  166.1 0.3 copy-done.7
  166.3 15.8 %last.1 = (bf16[192,2048]{1,0:T(8,128)(2,1)}, bf16[192,2048]{1,0:T(8,128)(2,1)}, bf16[192,2048]{1,0:T(8,128)(2,1)}, bf16[192,2048]{1,0:T(8,128)(2,1)}) custom-call(s32[3]{0:T(128)} %r_0_.3, bf16[3,2048,2048]{2,1,0:T(8,128)(2,1)} %get-tuple-element.34.refs_1_.r_1_, ...), custom_call_target="tpu_custom_call", output_to_operand_aliasing={{0}: (19, {})} | custom-call | flops 14949999616 | tf_op jit(solution)/shard_map/last/pallas_call | solution.py:544
  182.1 1.5 all-to-all-done.3
  183.6 0.3 copy.17
  183.9 0.9 copy.18
  (22 shorter events, 0.3 us)
Async XLA Ops:
  0.6 84.3 %collective-permute-start.3 = (bf16[192,2048]{1,0:T(8,128)(2,1)}, bf16[192,2048]{1,0:T(8,128)(2,1)S(1)}, u32[]{:S(2)}, u32[]{:S(2)}) collective-permute-start(bf16[192,2048]{1,0:T(8,128)(2,1)} %bitcast.21), channel_id=1, source_target_pairs={{0,12},{4,0},{8,4},{12,8},{1,13},{5,1},{9,5},{13,9},{2,14},{6,2},{... | collective-permute-start | bytes 2359304 | tf_op jit(solution)/shard_map/ppermute | solution.py:563
  4.0 80.9 %collective-permute-start.2 = (bf16[192,2048]{1,0:T(8,128)(2,1)}, bf16[192,2048]{1,0:T(8,128)(2,1)S(1)}, u32[]{:S(2)}, u32[]{:S(2)}) collective-permute-start(bf16[192,2048]{1,0:T(8,128)(2,1)} %bitcast.22), channel_id=1, source_target_pairs={{0,8},{4,12},{8,0},{12,4},{1,9},{5,13},{9,1},{13,5},{2,10},{6,14},... | collective-permute-start | bytes 2359304 | tf_op jit(solution)/shard_map/ppermute | solution.py:563
  4.5 80.4 %collective-permute-start.1 = (bf16[192,2048]{1,0:T(8,128)(2,1)}, bf16[192,2048]{1,0:T(8,128)(2,1)S(1)}, u32[]{:S(2)}, u32[]{:S(2)}) collective-permute-start(bf16[192,2048]{1,0:T(8,128)(2,1)} %bitcast.23), channel_id=1, source_target_pairs={{0,4},{4,8},{8,12},{12,0},{1,5},{5,9},{9,13},{13,1},{2,6},{6,10},{... | collective-permute-start | bytes 2359304 | tf_op jit(solution)/shard_map/ppermute | solution.py:563
  8.9 73.3 %all-to-all-start = ((bf16[8,2,192,128]{3,2,1,0:T(8,128)(2,1)}), bf16[8,2,192,128]{3,2,1,0:T(8,128)(2,1)S(1)}, u32[]{:S(2)}, u32[]{:S(2)}) async-start(bf16[8,2,192,128]{3,2,1,0:T(8,128)(2,1)} %get-tuple-element.35), calls=%async_computation | async-start | bytes 1572864 | tf_op jit(solution)/shard_map/all_to_all | solution.py:583
  82.3 0.9 copy-start
  83.1 3.9 %collective-permute-start = (bf16[8,2,192,128]{3,2,1,0:T(8,128)(2,1)}, bf16[8,2,192,128]{3,2,1,0:T(8,128)(2,1)S(1)}, u32[]{:S(2)}, u32[]{:S(2)}) collective-permute-start(bf16[8,2,192,128]{3,2,1,0:T(8,128)(2,1)} %hold.2.r_3_), channel_id=1, source_target_pairs={{0,16},{16,0},{32,48},{48,32},{64,80},{80,64},{96,112},{112,96},{1... | collective-permute-start | bytes 2359304 | tf_op jit(solution)/shard_map/ppermute | solution.py:588
  84.9 2.1 %copy-start.2 = (bf16[192,2048]{1,0:T(8,128)(2,1)}, bf16[192,2048]{1,0:T(8,128)(2,1)S(1)}, u32[]{:S(2)}) copy-start(bf16[192,2048]{1,0:T(8,128)(2,1)S(1)} %collective-permute-done.3.r_16_) | copy-start | bytes 2359300
  84.9 2.1 %copy-start.3 = (bf16[192,2048]{1,0:T(8,128)(2,1)}, bf16[192,2048]{1,0:T(8,128)(2,1)S(1)}, u32[]{:S(2)}) copy-start(bf16[192,2048]{1,0:T(8,128)(2,1)S(1)} %collective-permute-done.2.r_15_) | copy-start | bytes 2359300
  85.0 2.1 %copy-start.4 = (bf16[192,2048]{1,0:T(8,128)(2,1)}, bf16[192,2048]{1,0:T(8,128)(2,1)S(1)}, u32[]{:S(2)}) copy-start(bf16[192,2048]{1,0:T(8,128)(2,1)S(1)} %collective-permute-done.1.r_14_) | copy-start | bytes 2359300
  87.1 0.9 copy-start.8
  103.4 2.9 %collective-permute-start.4 = (bf16[8,480,128]{2,1,0:T(8,128)(2,1)}, bf16[8,480,128]{2,1,0:T(8,128)(2,1)S(1)}, u32[]{:S(2)}, u32[]{:S(2)}) collective-permute-start(bf16[8,480,128]{2,1,0:T(8,128)(2,1)} %get-tuple-element.46), channel_id=1, source_target_pairs={{0,16},{16,0},{32,48},{48,32},{64,80},{80,64},{96,112},{112,96},{1... | collective-permute-start | bytes 2949128 | tf_op jit(solution)/shard_map/ppermute | solution.py:592
  108.7 34.7 %all-to-all-start.1 = ((bf16[8,480,128]{2,1,0:T(8,128)(2,1)}), bf16[8,480,128]{2,1,0:T(8,128)(2,1)S(1)}, u32[]{:S(2)}, u32[]{:S(2)}) async-start(bf16[8,480,128]{2,1,0:T(8,128)(2,1)} %add_convert_fusion.refs_9_.refs_3_), calls=%async_computation.1 | async-start | bytes 1966080 | tf_op jit(solution)/shard_map/all_to_all | solution.py:594
  115.6 49.3 %collective-permute-start.5 = (bf16[192,2048]{1,0:T(8,128)(2,1)}, bf16[192,2048]{1,0:T(8,128)(2,1)S(1)}, u32[]{:S(2)}, u32[]{:S(2)}) collective-permute-start(bf16[192,2048]{1,0:T(8,128)(2,1)} %get-tuple-element.53), channel_id=1, source_target_pairs={{0,4},{4,8},{8,12},{12,0},{1,5},{5,9},{9,13},{13,1},{2,6},{6,10},{... | collective-permute-start | bytes 2359304 | tf_op jit(solution)/shard_map/ppermute | solution.py:563
  117.2 47.7 %collective-permute-start.6 = (bf16[192,2048]{1,0:T(8,128)(2,1)}, bf16[192,2048]{1,0:T(8,128)(2,1)S(1)}, u32[]{:S(2)}, u32[]{:S(2)}) collective-permute-start(bf16[192,2048]{1,0:T(8,128)(2,1)} %get-tuple-element.54), channel_id=1, source_target_pairs={{0,8},{4,12},{8,0},{12,4},{1,9},{5,13},{9,1},{13,5},{2,10},{6,14},... | collective-permute-start | bytes 2359304 | tf_op jit(solution)/shard_map/ppermute | solution.py:563
  119.0 46.0 %collective-permute-start.7 = (bf16[192,2048]{1,0:T(8,128)(2,1)}, bf16[192,2048]{1,0:T(8,128)(2,1)S(1)}, u32[]{:S(2)}, u32[]{:S(2)}) collective-permute-start(bf16[192,2048]{1,0:T(8,128)(2,1)} %get-tuple-element.55), channel_id=1, source_target_pairs={{0,12},{4,0},{8,4},{12,8},{1,13},{5,1},{9,5},{13,9},{2,14},{6,2},{... | collective-permute-start | bytes 2359304 | tf_op jit(solution)/shard_map/ppermute | solution.py:563
  143.4 1.0 copy-start.1
  157.0 26.6 %all-to-all-start.3 = ((f32[16,24,384]{2,1,0:T(8,128)}), f32[16,24,384]{2,1,0:T(8,128)S(1)}, u32[]{:S(2)}, u32[]{:S(2)}) async-start(f32[16,24,384]{2,1,0:T(8,128)} %spread.1), calls=%async_computation.3 | async-start | bytes 1179648 | tf_op jit(solution)/shard_map/all_to_all | solution.py:601
  164.9 0.9 copy-start.5
  165.0 1.1 copy-start.6
  165.0 1.4 copy-start.7

commit v4 on v3

--- a/solution.py
+++ b/solution.py
@@ -34,7 +34,7 @@
     return hi, mid, (rest - mid.astype(F32)).astype(BF)
 
 
-def call(kern, name, grid, in_specs, out_specs, out_shape, scratch=(), us=1):
+def call(kern, name, grid, in_specs, out_specs, out_shape, scratch=(), us=1, mib=60):
     return pl.pallas_call(
         kern,
         name=name,
@@ -43,7 +43,7 @@
         out_specs=out_specs,
         out_shape=out_shape,
         scratch_shapes=list(scratch),
-        compiler_params=pltpu.CompilerParams(vmem_limit_bytes=VMEM_BYTES),
+        compiler_params=pltpu.CompilerParams(vmem_limit_bytes=mib * 2**20),
         cost_estimate=work(us),
     )
 
@@ -69,12 +69,15 @@
 
 
 def pick_kernel(rate, offs, q, k, v, qp, kvp):
-    sel = sel_matrix(offs[pl.program_id(0)], rate, q.shape[1], qp.shape[1])
-    got = dot(jnp.concatenate([q[...], k[...], v[...]], axis=0), sel, 1, 0).astype(BF)
-    qp[...] = got[:HD]
-    for c in range(kvp.shape[0]):
-        kvp[c, 0] = got[HD : 2 * HD]
-        kvp[c, 1] = got[2 * HD :]
+    for h in range(q.shape[0] // HD):
+        rows = slice(h * HD, (h + 1) * HD)
+        sel = sel_matrix(offs[h], rate, q.shape[1], qp.shape[1])
+        got = dot(jnp.concatenate([q[rows, :], k[rows, :], v[rows, :]], axis=0), sel, 1, 0)
+        got = got.astype(BF)
+        qp[rows, :] = got[:HD]
+        for c in range(kvp.shape[0]):
+            kvp[c, 0, rows, :] = got[HD : 2 * HD]
+            kvp[c, 1, rows, :] = got[2 * HD :]
 
 
 def stack_rows(count, parts):
@@ -160,9 +163,9 @@
 
 
 def mid_kernel(
-    rate, info, offs, qp, kv_own, kv_oth, k, v, stats, w, pa, oa_p, lse_p, out_a, c0, c1, c2, c3,
-    t0, t1, t2, t3, dob, kept, sent, dqp, dkp, dvp,
-    wt, attn, pb, g_buf, oa, cot, t_buf, dob_buf, in_sems, out_sems,
+    rate, info, offs, qp, kv_own, kv_oth, stats, w, oa_p, lse_p, k_in, v_in, pa_in, out_a,
+    c0, c1, c2, c3, t0, t1, t2, t3, dob, dkp, dvp, kept, sent, dqp,
+    k, v, pa, dkp_buf, dvp_buf, wt, attn, pb, g_buf, oa, cot, t_buf, dob_buf, in_sems, out_sems,
 ):
     part = c0.shape[0]
     count = cot.shape[0] // part
@@ -179,6 +182,9 @@
         owner = lax.rem(info[2] + (count - s), count)
         there = cot.at[pl.ds(pl.multiple_of(owner * part, part), part), :]
         copies.append(pltpu.make_async_copy(block, there, in_sems.at[s]))
+        copies[-1].start()
+    for n, (there, here) in enumerate(((k_in, k), (v_in, v), (pa_in, pa))):
+        copies.append(pltpu.make_async_copy(there, here, in_sems.at[count + 1 + n]))
         copies[-1].start()
 
     here = lax.broadcasted_iota(jnp.int32, (1, tok), 1)
@@ -223,7 +229,7 @@
         sends.append(pltpu.make_async_copy(t_buf.at[s], term, out_sems.at[s]))
         sends[-1].start()
 
-    for copy in copies:
+    for copy in copies[:count]:
         copy.wait()
     for h in range(heads):
         rows = slice(h * HD, (h + 1) * HD)
@@ -239,6 +245,8 @@
     sends.append(pltpu.make_async_copy(dob_buf, dob, out_sems.at[count]))
     sends[-1].start()
 
+    for copy in copies[count:]:
+        copy.wait()
     for h in range(heads):
         rows = slice(h * HD, (h + 1) * HD)
         g = dot(sel_matrix(offs[h], rate, tok, picks), g_buf[rows, :], 0, 1)
@@ -256,14 +264,17 @@
         dq_a, dk_a, dv_a = back(k[rows, :], v[rows, :], pa[h], (near * g).astype(BF), o_a, dlse)
         dq_b, dk_b, dv_b = back(kf, vf, pb[h], (far * g).astype(BF), o_b, -dlse)
         dqp[h] = (dq_a + dq_b).astype(BF)
-        dkp[rows, :] = dk_a.astype(BF)
-        dvp[rows, :] = dv_a.astype(BF)
+        dkp_buf[rows, :] = dk_a.astype(BF)
+        dvp_buf[rows, :] = dv_a.astype(BF)
         for n, grad in enumerate((dk_b.astype(BF), dv_b.astype(BF))):
             first = n * width + h * HD
             for i, ref in enumerate((kept, sent)):
                 for c in range(chips):
                     cols = slice((i * chips + c) * picks, (i * chips + c + 1) * picks)
                     ref[c, first : first + HD, :] = grad[:, cols]
+    for n, (buf, out) in enumerate(((dkp_buf, dkp), (dvp_buf, dvp))):
+        sends.append(pltpu.make_async_copy(buf, out, out_sems.at[count + 1 + n]))
+        sends[-1].start()
     grad = dot(attn[...], cot[...], 1, 1)
     size = grad.shape[0] // chips
     half = grad.shape[1] // 2
@@ -331,10 +342,18 @@
 def last_kernel(
     rate, last, offs, e, dob, q, k, v, dqp, dkp, dvp, far_k, far_v,
     dk_old, dv_old, old_k, old_v, t0, t1, t2, t3, dq_old,
-    dq, kg, vg, mixed, dk, dv, k_buf, v_buf, vt, sems,
+    dq, kg, vg, mixed, dk, dv, k_buf, v_buf, vt, sems, t_buf, t_sems,
 ):
     tok = k.shape[1]
     step = pl.program_id(1)
+    size = mixed.shape[0]
+    slab = pl.ds(pl.multiple_of(step * size, size), size)
+    loads = [
+        pltpu.make_async_copy(t.at[slab, :], t_buf.at[n], t_sems.at[n])
+        for n, t in enumerate((t0, t1, t2, t3))
+    ]
+    for load in loads:
+        load.start()
     bwd_step(rate, offs[last], e, dob, q, k, v, dqp, dkp, dvp, dq, dk, dv, vt)
 
     def store(slot, head, near_k, near_v, spread):
@@ -349,9 +368,11 @@
             pltpu.make_async_copy(buf.at[slot], out.at[:HD, :], sems.at[slot, n]).wait()
 
     store(step, step, dk_old[...], dv_old[...], far_sum(rate, offs[step], old_k, old_v, tok))
-    total = t0[...].astype(F32)
-    for t in (t1, t2, t3):
-        total = total + t[...].astype(F32)
+    for load in loads:
+        load.wait()
+    total = t_buf[0].astype(F32)
+    for n in range(1, len(loads)):
+        total = total + t_buf[n].astype(F32)
     mixed[...] = total.astype(BF)
 
     @pl.when(step == last - 1)
@@ -365,17 +386,10 @@
 
 
 def pick(rate, offs, q, k, v, picks, copies):
-    rows, tok = q.shape
-    by_head = pl.BlockSpec((HD, tok), lambda h: (h, 0))
+    rows = q.shape[0]
     return call(
-        lambda *r: pick_kernel(rate, *r), "pick", (rows // HD,),
-        [SMEM, by_head, by_head, by_head],
-        [
-            pl.BlockSpec((HD, picks), lambda h: (h, 0)),
-            pl.BlockSpec((copies, 2, HD, picks), lambda h: (0, 0, h, 0)),
-        ],
-        [SDS((rows, picks), BF), SDS((copies, 2, rows, picks), BF)],
-        us=2,
+        lambda *r: pick_kernel(rate, *r), "pick", (), [SMEM] + [WHOLE] * 3, [WHOLE] * 2,
+        [SDS((rows, picks), BF), SDS((copies, 2, rows, picks), BF)], us=2,
     )(offs, q, k, v)
 
 
@@ -421,23 +435,25 @@
     dob = (heads, 2 * HD, tok)
     return call(
         lambda *r: mid_kernel(rate, *r), "mid", (),
-        [SMEM, SMEM] + [WHOLE] * 10 + [anywhere] * 5,
-        [anywhere] * 5 + [WHOLE] * 5,
+        [SMEM, SMEM] + [WHOLE] * 7 + [anywhere] * 8,
+        [anywhere] * 7 + [WHOLE] * 3,
         [SDS((rows, tok), BF)] * count
         + [
-            SDS(dob, BF), half, half, SDS((heads, picks, HD), BF), SDS((rows, tok), BF),
-            SDS((rows, tok), BF),
+            SDS(dob, BF), SDS((rows, tok), BF), SDS((rows, tok), BF), half, half,
+            SDS((heads, picks, HD), BF),
         ],
         scratch=[
-            pltpu.VMEM((count * rows, rows), BF), pltpu.VMEM((rows, tok), BF),
-            pltpu.VMEM((heads, picks, far), BF),
+            pltpu.VMEM((rows, tok), BF), pltpu.VMEM((rows, tok), BF),
+            pltpu.VMEM((heads, picks, tok), BF), pltpu.VMEM((rows, tok), BF),
+            pltpu.VMEM((rows, tok), BF), pltpu.VMEM((count * rows, rows), BF),
+            pltpu.VMEM((rows, tok), BF), pltpu.VMEM((heads, picks, far), BF),
             pltpu.VMEM((rows, tok), BF), pltpu.VMEM((rows, tok), F32),
             pltpu.VMEM((count * rows, tok), BF), pltpu.VMEM((count, rows, tok), BF),
-            pltpu.VMEM(dob, BF), pltpu.SemaphoreType.DMA((count + 1,)),
-            pltpu.SemaphoreType.DMA((count + 1,)),
+            pltpu.VMEM(dob, BF), pltpu.SemaphoreType.DMA((count + 4,)),
+            pltpu.SemaphoreType.DMA((count + 3,)),
         ],
-        us=20,
-    )(info, offs, qp, kv_own, kv_oth, k, v, stats, w, *near, out_a, *blocks)
+        us=16,
+    )(info, offs, qp, kv_own, kv_oth, stats, w, *near[1:], k, v, near[0], out_a, *blocks)
 
 
 def hold_all(arrays, after):
@@ -477,7 +493,7 @@
             pl.BlockSpec(memory_space=pl.ANY),
         ],
         pl.BlockSpec(shape, lambda i: (0, 0, 0)),
-        SDS(shape, F32), us=1,
+        SDS(shape, F32), us=1, mib=8,
     )(parts, after)
 
 
@@ -493,7 +509,7 @@
 def spread_sum(scale, parts, copies):
     return call(
         lambda *r: spread_kernel(scale, *r), "spread", (), [WHOLE], WHOLE,
-        SDS((copies,) + parts.shape[1:], F32), us=1,
+        SDS((copies,) + parts.shape[1:], F32), us=1, mib=8,
     )(parts)
 
 
@@ -539,7 +555,7 @@
     old = pl.BlockSpec((HD, tok), lambda h, j: (j, 0))
     slab = pl.BlockSpec((rows // last, tok), lambda h, j: (j, 0))
     ins = ins + [of(lambda j: last), of(lambda j: heads + last), old, old]
-    ins = ins + [of(lambda j: j), of(lambda j: heads + j)] + [slab] * len(terms) + [anywhere]
+    ins = ins + [of(lambda j: j), of(lambda j: heads + j)] + [anywhere] * len(terms) + [anywhere]
     buf = pltpu.VMEM((heads, HD, tok), BF)
     return pl.pallas_call(
         lambda *r: last_kernel(rate, last, *r),
@@ -551,6 +567,8 @@
         scratch_shapes=[
             pltpu.VMEM((HD, tok), F32), pltpu.VMEM((HD, tok), F32), buf, buf,
             pltpu.VMEM((tok, 2 * HD), BF), pltpu.SemaphoreType.DMA((heads, 2)),
+            pltpu.VMEM((len(terms), rows // last, tok), BF),
+            pltpu.SemaphoreType.DMA((len(terms),)),
         ],
         input_output_aliases={len(ins) - 1: 0},
         compiler_params=pltpu.CompilerParams(vmem_limit_bytes=VMEM_BYTES),
@@ -586,11 +604,11 @@
     e, out_a, stats, *near = forward(info, q, k, v, qp)
     kv_own = hold(kv_own, stats)
     kv_oth = lax.ppermute(kv_own, "seq", swap)
-    *terms, dob, kept, sent, dqp, dkp, dvp = middle(
+    *terms, dob, dkp, dvp, kept, sent, dqp = middle(
         rate, info, offsets, qp, kv_own, kv_oth, k, v, stats, w_out, near, out_a, blocks
     )
     got = lax.ppermute(sent, "seq", swap)
-    pair = (kept.astype(F32) + got.astype(F32)).astype(BF)
+    pair = kept + got
     far = lax.all_to_all(pair, "seq", 0, 0, axis_index_groups=groups)
     later = hold_all(terms[1:], pair)
     terms = terms[:1] + [shift(t, "head", s + 1) for s, t in enumerate(later)]

time: 185 us -> 180 us (0.973)
  Pallas kernels: 124 us -> 118 us
    add x0 -> x1, other arithmetic: none -> 2.48 us  [shards(): pair = kept + got]
    convert_element_type x1 -> x0, other arithmetic: 2.47 us -> none  [shards(): pair = (kept.astype(F32) + got.astype(F32)).astype(BF)]
    pallas_call x1, Pallas kernels: 15.4 us -> 13.3 us  [middle(): call(lambda *r: mid_kernel(rate, *r), 'mid', (), [SMEM, SMEM] + [WHOLE] *...]
    unnamed x19 -> x21, local copies, waits for them, and re-layouts: 4.99 us -> 5.55 us
  transfers between devices with their start and end apart: 11 -> 11, of which waited for: 4 -> 4; matrix products, arithmetic and copies ran while one was open for 0% -> 0% of each run, Pallas kernels for 59% -> 58%
where the time goes in v4:
time: 180 us
  Pallas kernels  118 us (66%)
  starting transfers between devices  33.7 us (19%)
  blocking collectives  9.08 us (5%)
  waiting for transfers between devices  8.45 us (5%)
  local copies, waits for them, and re-layouts  6.44 us (4%)
  other arithmetic  2.48 us (1%)
    pallas_call x1, Pallas kernels, forward(): call(fwd_kernel, 'fwd', (heads, tok // qb), [SMEM, whole, whole, whole, p...  63.9 us
    pallas_call x1, Pallas kernels, backward(): call(kernel, 'bwd', (heads, tok // qb), ins + spare, [by_q, whole, whole]...  21.9 us
    pallas_call x1, Pallas kernels, backward_last(): pl.pallas_call(lambda *r: last_kernel(rate, last, *r), name='last', grid=...  15.1 us
    pallas_call x1, Pallas kernels, middle(): call(lambda *r: mid_kernel(rate, *r), 'mid', (), [SMEM, SMEM] + [WHOLE] *...  13.3 us
    all_to_all x1, blocking collectives, shards(): mine = lax.all_to_all(mine, 'dp', 0, 0)  9.08 us
    ppermute x6, starting transfers between devices, shift(): return lax.ppermute(x, axis, [(i, (i + by) % count) for i in range(count)])  8.6 us
    all_to_all x1, starting transfers between devices, shards(): kv_own = lax.all_to_all(kvp, 'seq', 0, 0, axis_index_groups=groups)  8.19 us
    all_to_all x1, starting transfers between devices, shards(): lax.all_to_all(spread_sum(grad_scale, mine, seq_count), 'seq', 0, 0)  7.74 us
  transfers between devices with their start and end apart: 11, of which 4 were waited for; matrix products, arithmetic and copies ran while one was open for 0% of the time, Pallas kernels for 58%

profile of v4, /device:TPU:1, one launch (start us, length us, event | category | flops | bytes accessed | tf_op | source)
XLA Modules:
  0.0 179.9 jit_solution(6017469001684227104)
XLA Ops:
  0.6 3.4 %collective-permute-start.3 = (bf16[192,2048]{1,0:T(8,128)(2,1)}, bf16[192,2048]{1,0:T(8,128)(2,1)S(1)}, u32[]{:S(2)}, u32[]{:S(2)}) collective-permute-start(bf16[192,2048]{1,0:T(8,128)(2,1)} %bitcast.21), channel_id=1, source_target_pairs={{0,12},{4,0},{8,4},{12,8},{1,13},{5,1},{9,5},{13,9},{2,14},{6,2},{... | collective-permute-start | bytes 2359304 | tf_op jit(solution)/shard_map/ppermute | solution.py:581
  4.0 0.5 collective-permute-start.2
  4.5 0.6 collective-permute-start.1
  5.1 3.3 %pick.1 = (bf16[192,128]{1,0:T(8,128)(2,1)}, bf16[8,2,192,128]{3,2,1,0:T(8,128)(2,1)}) custom-call(s32[3]{0:T(128)} %r_0_.3, bf16[192,2048]{1,0:T(8,128)(2,1)} %bitcast.25, bf16[192,2048]{1,0:T(8,128)(2,1)} %bitcast.29, bf16[192,2048]{1,0:T(8,128)(2,1)} %bitcast.34), custom_call_target="tpu_custom_call" | custom-call | flops 2300000000 | tf_op jit(solution)/shard_map/pick/pallas_call | solution.py:390
  8.4 8.2 %all-to-all-start = ((bf16[8,2,192,128]{3,2,1,0:T(8,128)(2,1)}), bf16[8,2,192,128]{3,2,1,0:T(8,128)(2,1)S(1)}, u32[]{:S(2)}, u32[]{:S(2)}) async-start(bf16[8,2,192,128]{3,2,1,0:T(8,128)(2,1)} %get-tuple-element.35), calls=%async_computation | async-start | bytes 1572864 | tf_op jit(solution)/shard_map/all_to_all | solution.py:601
  17.3 0.6 stack.19.info.r_0_
  17.9 63.9 %fwd.1 = (bf16[3,2048,2048]{2,1,0:T(8,128)(2,1)}, f32[192,2048]{1,0:T(8,128)}, f32[3,8,2048]{2,1,0:T(8,128)}, bf16[3,128,2048]{2,1,0:T(8,128)(2,1)}, f32[3,128,64]{2,1,0:T(8,128)}, /*index=5*/f32[3,128,64]{2,1,0:T(8,128)}) custom-call(s32[5]{0:T(128)} %stack.19.info.r_0_, bf16[192,2048]{1,0:T(8,128)(2,1)} %bitcast.26, bf16[192,2048]{1,0:T(8,128)(2,1)} %bitcast.30, ...), custom_call_target="tpu_custom_call" | custom-call | flops 20700000256 | tf_op jit(solution)/shard_map/fwd/pallas_call | solution.py:404
  81.8 0.9 copy-done.2
  82.6 1.8 collective-permute-start
  84.5 2.1 %collective-permute-done.r_4_ = bf16[8,2,192,128]{3,2,1,0:T(8,128)(2,1)S(1)} collective-permute-done((bf16[8,2,192,128]{3,2,1,0:T(8,128)(2,1)}, bf16[8,2,192,128]{3,2,1,0:T(8,128)(2,1)S(1)}, u32[]{:S(2)}, u32[]{:S(2)}) %collective-permute-start) | collective-permute-done | bytes 786464 | tf_op jit(solution)/shard_map/ppermute | solution.py:606
  86.6 0.9 copy-done.9
  87.4 13.3 %mid.1 = (bf16[192,2048]{1,0:T(8,128)(2,1)}, bf16[192,2048]{1,0:T(8,128)(2,1)}, bf16[192,2048]{1,0:T(8,128)(2,1)}, bf16[192,2048]{1,0:T(8,128)(2,1)}, bf16[3,128...) custom-call(s32[5]{0:T(128)} %stack.19.info.r_0_, ...), custom_call_target="tpu_custom_call" | custom-call | flops 18400000000 | tf_op jit(solution)/shard_map/mid/pallas_call | solution.py:436
  100.8 0.5 collective-permute-start.4
  101.2 2.4 %collective-permute-done.4 = bf16[8,480,128]{2,1,0:T(8,128)(2,1)S(1)} collective-permute-done((bf16[8,480,128]{2,1,0:T(8,128)(2,1)}, bf16[8,480,128]{2,1,0:T(8,128)(2,1)S(1)}, u32[]{:S(2)}, u32[]{:S(2)}) %collective-permute-start.4) | collective-permute-done | bytes 983072 | tf_op jit(solution)/shard_map/ppermute | solution.py:610
  103.6 2.5 %add.9.refs_9_.refs_3_ = bf16[8,480,128]{2,1,0:T(8,128)(2,1)} add(bf16[8,480,128]{2,1,0:T(8,128)(2,1)} %get-tuple-element.45, bf16[8,480,128]{2,1,0:T(8,128)(2,1)S(1)} %collective-permute-done.4) | non-fusion elementwise | flops 491520 | bytes 2949120 | tf_op jit(solution)/shard_map/add | solution.py:611
  106.1 6.9 %all-to-all-start.1 = ((bf16[8,480,128]{2,1,0:T(8,128)(2,1)}), bf16[8,480,128]{2,1,0:T(8,128)(2,1)S(1)}, u32[]{:S(2)}, u32[]{:S(2)}) async-start(bf16[8,480,128]{2,1,0:T(8,128)(2,1)} %add.9.refs_9_.refs_3_), calls=%async_computation.1 | async-start | bytes 1966080 | tf_op jit(solution)/shard_map/all_to_all | solution.py:612
  113.0 1.6 collective-permute-start.5
  114.6 1.7 collective-permute-start.6
  116.4 0.7 collective-permute-start.7
  117.1 21.9 %bwd.1 = (bf16[192,2048]{1,0:T(8,128)(2,1)}, f32[128,2048]{1,0:T(8,128)}, f32[128,2048]{1,0:T(8,128)}) custom-call(s32[3]{0:T(128)} %r_0_.3, bf16[3,2048,2048]{2,1,0:T(8,128)(2,1)} %get-tuple-element.34.refs_1_.r_1_, bf16[3,128,2048]{2,1,0:T(8,128)(2,1)} %get-tuple-element.41.refs_2_.r_2_, bf16[192,2048]{1,0:T(8,128)(2,1)} %bitcast.27, ...), custom_call_target="tpu_custom_call" | custom-call | flops 25300000768 | tf_op jit(solution)/shard_map/bwd/pallas_call | solution.py:538
  139.0 1.8 %all-to-all-done.1.r_9_.r_10_.r_13_.r_14_.parts = bf16[8,480,128]{2,1,0:T(8,128)(2,1)S(1)} async-done(((bf16[8,480,128]{2,1,0:T(8,128)(2,1)}), bf16[8,480,128]{2,1,0:T(8,128)(2,1)S(1)}, u32[]{:S(2)}, u32[]{:S(2)}) %all-to-all-start.1) | async-done | bytes 983072 | tf_op jit(solution)/shard_map/all_to_all | solution.py:612
  140.8 1.6 copy-done.1
  142.5 9.1 %all_to_all.20.r_0_ = f32[4,24,384]{2,1,0:T(8,128)S(1)} all-to-all(f32[4,24,384]{2,1,0:T(8,128)S(1)} %total.1), channel_id=1, replica_groups=mesh['seq'=16,'head'=4,'dp'=4] {'dp'}, dimensions={0} | all-to-all | bytes 294912 | tf_op jit(solution)/shard_map/all_to_all | solution.py:618
  151.5 0.9 spread.1
  152.4 7.7 %all-to-all-start.3 = ((f32[16,24,384]{2,1,0:T(8,128)}), f32[16,24,384]{2,1,0:T(8,128)S(1)}, u32[]{:S(2)}, u32[]{:S(2)}) async-start(f32[16,24,384]{2,1,0:T(8,128)} %spread.1), calls=%async_computation.3 | async-start | bytes 1179648 | tf_op jit(solution)/shard_map/all_to_all | solution.py:619
  160.2 0.8 copy-done.6
  161.0 0.3 copy-done.7
  161.3 0.3 copy-done.8
  161.5 15.1 %last.1 = (bf16[192,2048]{1,0:T(8,128)(2,1)}, bf16[192,2048]{1,0:T(8,128)(2,1)}, bf16[192,2048]{1,0:T(8,128)(2,1)}, bf16[192,2048]{1,0:T(8,128)(2,1)}) custom-call(s32[3]{0:T(128)} %r_0_.3, bf16[3,2048,2048]{2,1,0:T(8,128)(2,1)} %get-tuple-element.34.refs_1_.r_1_, ...), custom_call_target="tpu_custom_call", output_to_operand_aliasing={{0}: (19, {})} | custom-call | flops 14949999616 | tf_op jit(solution)/shard_map/last/pallas_call | solution.py:560
  176.6 2.1 %all-to-all-done.3 = f32[16,24,384]{2,1,0:T(8,128)S(1)} async-done(((f32[16,24,384]{2,1,0:T(8,128)}), f32[16,24,384]{2,1,0:T(8,128)S(1)}, u32[]{:S(2)}, u32[]{:S(2)}) %all-to-all-start.3) | async-done | bytes 589856 | tf_op jit(solution)/shard_map/all_to_all | solution.py:619
  178.8 0.3 copy.17
  179.1 0.9 copy.18
  (24 shorter events, 0.1 us)
Async XLA Ops:
  0.6 83.8 %collective-permute-start.3 = (bf16[192,2048]{1,0:T(8,128)(2,1)}, bf16[192,2048]{1,0:T(8,128)(2,1)S(1)}, u32[]{:S(2)}, u32[]{:S(2)}) collective-permute-start(bf16[192,2048]{1,0:T(8,128)(2,1)} %bitcast.21), channel_id=1, source_target_pairs={{0,12},{4,0},{8,4},{12,8},{1,13},{5,1},{9,5},{13,9},{2,14},{6,2},{... | collective-permute-start | bytes 2359304 | tf_op jit(solution)/shard_map/ppermute | solution.py:581
  4.0 80.4 %collective-permute-start.2 = (bf16[192,2048]{1,0:T(8,128)(2,1)}, bf16[192,2048]{1,0:T(8,128)(2,1)S(1)}, u32[]{:S(2)}, u32[]{:S(2)}) collective-permute-start(bf16[192,2048]{1,0:T(8,128)(2,1)} %bitcast.22), channel_id=1, source_target_pairs={{0,8},{4,12},{8,0},{12,4},{1,9},{5,13},{9,1},{13,5},{2,10},{6,14},... | collective-permute-start | bytes 2359304 | tf_op jit(solution)/shard_map/ppermute | solution.py:581
  4.5 79.9 %collective-permute-start.1 = (bf16[192,2048]{1,0:T(8,128)(2,1)}, bf16[192,2048]{1,0:T(8,128)(2,1)S(1)}, u32[]{:S(2)}, u32[]{:S(2)}) collective-permute-start(bf16[192,2048]{1,0:T(8,128)(2,1)} %bitcast.23), channel_id=1, source_target_pairs={{0,4},{4,8},{8,12},{12,0},{1,5},{5,9},{9,13},{13,1},{2,6},{6,10},{... | collective-permute-start | bytes 2359304 | tf_op jit(solution)/shard_map/ppermute | solution.py:581
  8.4 73.3 %all-to-all-start = ((bf16[8,2,192,128]{3,2,1,0:T(8,128)(2,1)}), bf16[8,2,192,128]{3,2,1,0:T(8,128)(2,1)S(1)}, u32[]{:S(2)}, u32[]{:S(2)}) async-start(bf16[8,2,192,128]{3,2,1,0:T(8,128)(2,1)} %get-tuple-element.35), calls=%async_computation | async-start | bytes 1572864 | tf_op jit(solution)/shard_map/all_to_all | solution.py:601
  81.8 0.9 copy-start.2
  82.6 3.9 %collective-permute-start = (bf16[8,2,192,128]{3,2,1,0:T(8,128)(2,1)}, bf16[8,2,192,128]{3,2,1,0:T(8,128)(2,1)S(1)}, u32[]{:S(2)}, u32[]{:S(2)}) collective-permute-start(bf16[8,2,192,128]{3,2,1,0:T(8,128)(2,1)} %hold.2.r_3_), channel_id=1, source_target_pairs={{0,16},{16,0},{32,48},{48,32},{64,80},{80,64},{96,112},{112,96},{1... | collective-permute-start | bytes 2359304 | tf_op jit(solution)/shard_map/ppermute | solution.py:606
  84.4 2.1 %copy-start.3 = (bf16[192,2048]{1,0:T(8,128)(2,1)}, bf16[192,2048]{1,0:T(8,128)(2,1)S(1)}, u32[]{:S(2)}) copy-start(bf16[192,2048]{1,0:T(8,128)(2,1)S(1)} %collective-permute-done.3.r_16_) | copy-start | bytes 2359300
  84.4 2.1 %copy-start.4 = (bf16[192,2048]{1,0:T(8,128)(2,1)}, bf16[192,2048]{1,0:T(8,128)(2,1)S(1)}, u32[]{:S(2)}) copy-start(bf16[192,2048]{1,0:T(8,128)(2,1)S(1)} %collective-permute-done.2.r_15_) | copy-start | bytes 2359300
  84.5 2.1 %copy-start.5 = (bf16[192,2048]{1,0:T(8,128)(2,1)}, bf16[192,2048]{1,0:T(8,128)(2,1)S(1)}, u32[]{:S(2)}) copy-start(bf16[192,2048]{1,0:T(8,128)(2,1)S(1)} %collective-permute-done.1.r_14_) | copy-start | bytes 2359300
  86.6 0.9 copy-start.9
  100.8 2.9 %collective-permute-start.4 = (bf16[8,480,128]{2,1,0:T(8,128)(2,1)}, bf16[8,480,128]{2,1,0:T(8,128)(2,1)S(1)}, u32[]{:S(2)}, u32[]{:S(2)}) collective-permute-start(bf16[8,480,128]{2,1,0:T(8,128)(2,1)} %get-tuple-element.46), channel_id=1, source_target_pairs={{0,16},{16,0},{32,48},{48,32},{64,80},{80,64},{96,112},{112,96},{1... | collective-permute-start | bytes 2949128 | tf_op jit(solution)/shard_map/ppermute | solution.py:610
  106.1 34.7 %all-to-all-start.1 = ((bf16[8,480,128]{2,1,0:T(8,128)(2,1)}), bf16[8,480,128]{2,1,0:T(8,128)(2,1)S(1)}, u32[]{:S(2)}, u32[]{:S(2)}) async-start(bf16[8,480,128]{2,1,0:T(8,128)(2,1)} %add.9.refs_9_.refs_3_), calls=%async_computation.1 | async-start | bytes 1966080 | tf_op jit(solution)/shard_map/all_to_all | solution.py:612
  113.0 47.1 %collective-permute-start.5 = (bf16[192,2048]{1,0:T(8,128)(2,1)}, bf16[192,2048]{1,0:T(8,128)(2,1)S(1)}, u32[]{:S(2)}, u32[]{:S(2)}) collective-permute-start(bf16[192,2048]{1,0:T(8,128)(2,1)} %get-tuple-element.53), channel_id=1, source_target_pairs={{0,4},{4,8},{8,12},{12,0},{1,5},{5,9},{9,13},{13,1},{2,6},{6,10},{... | collective-permute-start | bytes 2359304 | tf_op jit(solution)/shard_map/ppermute | solution.py:581
  114.6 45.5 %collective-permute-start.6 = (bf16[192,2048]{1,0:T(8,128)(2,1)}, bf16[192,2048]{1,0:T(8,128)(2,1)S(1)}, u32[]{:S(2)}, u32[]{:S(2)}) collective-permute-start(bf16[192,2048]{1,0:T(8,128)(2,1)} %get-tuple-element.54), channel_id=1, source_target_pairs={{0,8},{4,12},{8,0},{12,4},{1,9},{5,13},{9,1},{13,5},{2,10},{6,14},... | collective-permute-start | bytes 2359304 | tf_op jit(solution)/shard_map/ppermute | solution.py:581
  116.4 43.8 %collective-permute-start.7 = (bf16[192,2048]{1,0:T(8,128)(2,1)}, bf16[192,2048]{1,0:T(8,128)(2,1)S(1)}, u32[]{:S(2)}, u32[]{:S(2)}) collective-permute-start(bf16[192,2048]{1,0:T(8,128)(2,1)} %get-tuple-element.55), channel_id=1, source_target_pairs={{0,12},{4,0},{8,4},{12,8},{1,13},{5,1},{9,5},{13,9},{2,14},{6,2},{... | collective-permute-start | bytes 2359304 | tf_op jit(solution)/shard_map/ppermute | solution.py:581
  140.8 1.6 copy-start
  140.8 1.6 copy-start.1
  152.4 26.4 %all-to-all-start.3 = ((f32[16,24,384]{2,1,0:T(8,128)}), f32[16,24,384]{2,1,0:T(8,128)S(1)}, u32[]{:S(2)}, u32[]{:S(2)}) async-start(f32[16,24,384]{2,1,0:T(8,128)} %spread.1), calls=%async_computation.3 | async-start | bytes 1179648 | tf_op jit(solution)/shard_map/all_to_all | solution.py:619
  160.1 0.9 copy-start.6
  160.2 1.1 copy-start.7
  160.2 1.4 copy-start.8

commit v5 on v4

--- a/solution.py
+++ b/solution.py
@@ -607,11 +607,10 @@
     *terms, dob, dkp, dvp, kept, sent, dqp = middle(
         rate, info, offsets, qp, kv_own, kv_oth, k, v, stats, w_out, near, out_a, blocks
     )
+    terms = terms[:1] + [shift(terms[s], "head", s) for s in (1, 2, 3)]
     got = lax.ppermute(sent, "seq", swap)
     pair = kept + got
     far = lax.all_to_all(pair, "seq", 0, 0, axis_index_groups=groups)
-    later = hold_all(terms[1:], pair)
-    terms = terms[:1] + [shift(t, "head", s + 1) for s, t in enumerate(later)]
     dq, dk, dv = backward(2, rate, offsets, e, dob, q, k, v, dqp, dkp, dvp, (pair,))
     grad_scale = 1.0 / math.sqrt(tok * seq_count * lax.axis_size("dp"))
     mine = total(far, 2 * rows, rows // chips, lax.axis_size("dp"), dk)

time: 180 us -> 179 us (level)
  starting transfers between devices: 33.7 us -> 31.1 us
    all_to_all x1, waiting for transfers between devices: 1.8 us -> 5.88 us  [shards(): far = lax.all_to_all(pair, 'seq', 0, 0, axis_index_groups=groups)]
    all_to_all x1, starting transfers between devices: 7.74 us -> 5.29 us  [shards(): lax.all_to_all(spread_sum(grad_scale, mine, seq_count), 'seq', 0, 0)]
    ppermute x1, waiting for transfers between devices: 2.4 us -> 0.01 us  [shards(): got = lax.ppermute(sent, 'seq', swap)]
  transfers between devices with their start and end apart: 11 -> 11, of which waited for: 4 -> 3; matrix products, arithmetic and copies ran while one was open for 0% -> 2% of each run, Pallas kernels for 58% -> 59%
where the time goes in v5:
time: 179 us
  Pallas kernels  118 us (66%)
  starting transfers between devices  31.1 us (17%)
  waiting for transfers between devices  10.1 us (6%)
  blocking collectives  8.9 us (5%)
  local copies, waits for them, and re-layouts  6.46 us (4%)
  other arithmetic  2.47 us (1%)
    pallas_call x1, Pallas kernels, forward(): call(fwd_kernel, 'fwd', (heads, tok // qb), [SMEM, whole, whole, whole, p...  63.8 us
    pallas_call x1, Pallas kernels, backward(): call(kernel, 'bwd', (heads, tok // qb), ins + spare, [by_q, whole, whole]...  21.9 us
    pallas_call x1, Pallas kernels, backward_last(): pl.pallas_call(lambda *r: last_kernel(rate, last, *r), name='last', grid=...  15.1 us
    pallas_call x1, Pallas kernels, middle(): call(lambda *r: mid_kernel(rate, *r), 'mid', (), [SMEM, SMEM] + [WHOLE] *...  13.3 us
    all_to_all x1, blocking collectives, shards(): mine = lax.all_to_all(mine, 'dp', 0, 0)  8.9 us
    ppermute x6, starting transfers between devices, shift(): return lax.ppermute(x, axis, [(i, (i + by) % count) for i in range(count)])  8.43 us
    all_to_all x1, starting transfers between devices, shards(): kv_own = lax.all_to_all(kvp, 'seq', 0, 0, axis_index_groups=groups)  8.19 us
    all_to_all x1, starting transfers between devices, shards(): far = lax.all_to_all(pair, 'seq', 0, 0, axis_index_groups=groups)  6.93 us
  transfers between devices with their start and end apart: 11, of which 3 were waited for; matrix products, arithmetic and copies ran while one was open for 2% of the time, Pallas kernels for 59%

profile of v5, /device:TPU:1, one launch (start us, length us, event | category | flops | bytes accessed | tf_op | source)
XLA Modules:
  0.0 178.8 jit_solution(13360079846151987404)
XLA Ops:
  0.6 3.4 %collective-permute-start.3 = (bf16[192,2048]{1,0:T(8,128)(2,1)}, bf16[192,2048]{1,0:T(8,128)(2,1)S(1)}, u32[]{:S(2)}, u32[]{:S(2)}) collective-permute-start(bf16[192,2048]{1,0:T(8,128)(2,1)} %bitcast.21), channel_id=1, source_target_pairs={{0,12},{4,0},{8,4},{12,8},{1,13},{5,1},{9,5},{13,9},{2,14},{6,2},{... | collective-permute-start | bytes 2359304 | tf_op jit(solution)/shard_map/ppermute | solution.py:581
  4.0 0.5 collective-permute-start.2
  4.5 0.6 collective-permute-start.1
  5.1 3.3 %pick.1 = (bf16[192,128]{1,0:T(8,128)(2,1)}, bf16[8,2,192,128]{3,2,1,0:T(8,128)(2,1)}) custom-call(s32[3]{0:T(128)} %r_0_.3, bf16[192,2048]{1,0:T(8,128)(2,1)} %bitcast.25, bf16[192,2048]{1,0:T(8,128)(2,1)} %bitcast.29, bf16[192,2048]{1,0:T(8,128)(2,1)} %bitcast.34), custom_call_target="tpu_custom_call" | custom-call | flops 2300000000 | tf_op jit(solution)/shard_map/pick/pallas_call | solution.py:390
  8.4 8.2 %all-to-all-start = ((bf16[8,2,192,128]{3,2,1,0:T(8,128)(2,1)}), bf16[8,2,192,128]{3,2,1,0:T(8,128)(2,1)S(1)}, u32[]{:S(2)}, u32[]{:S(2)}) async-start(bf16[8,2,192,128]{3,2,1,0:T(8,128)(2,1)} %get-tuple-element.32), calls=%async_computation | async-start | bytes 1572864 | tf_op jit(solution)/shard_map/all_to_all | solution.py:601
  17.3 0.6 stack.19.info.r_0_
  17.9 63.8 %fwd.1 = (bf16[3,2048,2048]{2,1,0:T(8,128)(2,1)}, f32[192,2048]{1,0:T(8,128)}, f32[3,8,2048]{2,1,0:T(8,128)}, bf16[3,128,2048]{2,1,0:T(8,128)(2,1)}, f32[3,128,64]{2,1,0:T(8,128)}, /*index=5*/f32[3,128,64]{2,1,0:T(8,128)}) custom-call(s32[5]{0:T(128)} %stack.19.info.r_0_, bf16[192,2048]{1,0:T(8,128)(2,1)} %bitcast.26, bf16[192,2048]{1,0:T(8,128)(2,1)} %bitcast.30, ...), custom_call_target="tpu_custom_call" | custom-call | flops 20700000256 | tf_op jit(solution)/shard_map/fwd/pallas_call | solution.py:404
  81.8 0.0 copy-start.2
  81.8 0.9 copy-done.2
  82.7 1.8 %collective-permute-start = (bf16[8,2,192,128]{3,2,1,0:T(8,128)(2,1)}, bf16[8,2,192,128]{3,2,1,0:T(8,128)(2,1)S(1)}, u32[]{:S(2)}, u32[]{:S(2)}) collective-permute-start(bf16[8,2,192,128]{3,2,1,0:T(8,128)(2,1)} %hold.1.r_3_), channel_id=1, source_target_pairs={{0,16},{16,0},{32,48},{48,32},{64,80},{80,64},{96,112},{112,96},{1... | collective-permute-start | bytes 2359304 | tf_op jit(solution)/shard_map/ppermute | solution.py:606
  84.5 2.1 %collective-permute-done.r_4_ = bf16[8,2,192,128]{3,2,1,0:T(8,128)(2,1)S(1)} collective-permute-done((bf16[8,2,192,128]{3,2,1,0:T(8,128)(2,1)}, bf16[8,2,192,128]{3,2,1,0:T(8,128)(2,1)S(1)}, u32[]{:S(2)}, u32[]{:S(2)}) %collective-permute-start) | collective-permute-done | bytes 786464 | tf_op jit(solution)/shard_map/ppermute | solution.py:606
  86.6 0.9 copy-done.9
  87.5 13.3 %mid.1 = (bf16[192,2048]{1,0:T(8,128)(2,1)}, bf16[192,2048]{1,0:T(8,128)(2,1)}, bf16[192,2048]{1,0:T(8,128)(2,1)}, bf16[192,2048]{1,0:T(8,128)(2,1)}, bf16[3,128...) custom-call(s32[5]{0:T(128)} %stack.19.info.r_0_, ...), custom_call_target="tpu_custom_call" | custom-call | flops 18400000000 | tf_op jit(solution)/shard_map/mid/pallas_call | solution.py:436
  100.8 0.5 collective-permute-start.4
  101.2 1.5 collective-permute-start.5
  102.7 1.7 collective-permute-start.6
  104.5 0.7 collective-permute-start.7
  105.1 2.5 %add.9.refs_9_ = bf16[8,480,128]{2,1,0:T(8,128)(2,1)} add(bf16[8,480,128]{2,1,0:T(8,128)(2,1)} %get-tuple-element.42, bf16[8,480,128]{2,1,0:T(8,128)(2,1)S(1)} %collective-permute-done.4) | non-fusion elementwise | flops 491520 | bytes 2949120 | tf_op jit(solution)/shard_map/add | solution.py:612
  107.6 6.9 %all-to-all-start.1 = ((bf16[8,480,128]{2,1,0:T(8,128)(2,1)}), bf16[8,480,128]{2,1,0:T(8,128)(2,1)S(1)}, u32[]{:S(2)}, u32[]{:S(2)}) async-start(bf16[8,480,128]{2,1,0:T(8,128)(2,1)} %add.9.refs_9_), calls=%async_computation.1 | async-start | bytes 1966080 | tf_op jit(solution)/shard_map/all_to_all | solution.py:613
  114.5 21.9 %bwd.1 = (bf16[192,2048]{1,0:T(8,128)(2,1)}, f32[128,2048]{1,0:T(8,128)}, f32[128,2048]{1,0:T(8,128)}) custom-call(s32[3]{0:T(128)} %r_0_.3, bf16[3,2048,2048]{2,1,0:T(8,128)(2,1)} %get-tuple-element.31.refs_1_.r_1_, bf16[3,128,2048]{2,1,0:T(8,128)(2,1)} %get-tuple-element.38.refs_2_.r_2_, bf16[192,2048]{1,0:T(8,128)(2,1)} %bitcast.27, ...), custom_call_target="tpu_custom_call" | custom-call | flops 25300000768 | tf_op jit(solution)/shard_map/bwd/pallas_call | solution.py:538
  136.4 5.9 %all-to-all-done.1.r_9_.r_10_.r_13_.r_14_.parts = bf16[8,480,128]{2,1,0:T(8,128)(2,1)S(1)} async-done(((bf16[8,480,128]{2,1,0:T(8,128)(2,1)}), bf16[8,480,128]{2,1,0:T(8,128)(2,1)S(1)}, u32[]{:S(2)}, u32[]{:S(2)}) %all-to-all-start.1) | async-done | bytes 983072 | tf_op jit(solution)/shard_map/all_to_all | solution.py:613
  142.3 1.6 copy-done.1
  144.0 8.9 %all_to_all.20.r_0_ = f32[4,24,384]{2,1,0:T(8,128)S(1)} all-to-all(f32[4,24,384]{2,1,0:T(8,128)S(1)} %total.1), channel_id=1, replica_groups=mesh['seq'=16,'head'=4,'dp'=4] {'dp'}, dimensions={0} | all-to-all | bytes 294912 | tf_op jit(solution)/shard_map/all_to_all | solution.py:617
  152.9 0.9 spread.1
  153.7 5.3 %all-to-all-start.3 = ((f32[16,24,384]{2,1,0:T(8,128)}), f32[16,24,384]{2,1,0:T(8,128)S(1)}, u32[]{:S(2)}, u32[]{:S(2)}) async-start(f32[16,24,384]{2,1,0:T(8,128)} %spread.1), calls=%async_computation.3 | async-start | bytes 1179648 | tf_op jit(solution)/shard_map/all_to_all | solution.py:618
  159.1 0.8 copy-done.6
  159.9 0.3 copy-done.7
  160.2 0.2 copy-done.8
  160.4 15.1 %last.1 = (bf16[192,2048]{1,0:T(8,128)(2,1)}, bf16[192,2048]{1,0:T(8,128)(2,1)}, bf16[192,2048]{1,0:T(8,128)(2,1)}, bf16[192,2048]{1,0:T(8,128)(2,1)}) custom-call(s32[3]{0:T(128)} %r_0_.3, bf16[3,2048,2048]{2,1,0:T(8,128)(2,1)} %get-tuple-element.31.refs_1_.r_1_, ...), custom_call_target="tpu_custom_call", output_to_operand_aliasing={{0}: (19, {})} | custom-call | flops 14949999616 | tf_op jit(solution)/shard_map/last/pallas_call | solution.py:560
  175.5 2.2 %all-to-all-done.3 = f32[16,24,384]{2,1,0:T(8,128)S(1)} async-done(((f32[16,24,384]{2,1,0:T(8,128)}), f32[16,24,384]{2,1,0:T(8,128)S(1)}, u32[]{:S(2)}, u32[]{:S(2)}) %all-to-all-start.3) | async-done | bytes 589856 | tf_op jit(solution)/shard_map/all_to_all | solution.py:618
  177.7 0.3 copy.14
  178.0 0.9 copy.15
  (23 shorter events, 0.1 us)
Async XLA Ops:
  0.6 83.8 %collective-permute-start.3 = (bf16[192,2048]{1,0:T(8,128)(2,1)}, bf16[192,2048]{1,0:T(8,128)(2,1)S(1)}, u32[]{:S(2)}, u32[]{:S(2)}) collective-permute-start(bf16[192,2048]{1,0:T(8,128)(2,1)} %bitcast.21), channel_id=1, source_target_pairs={{0,12},{4,0},{8,4},{12,8},{1,13},{5,1},{9,5},{13,9},{2,14},{6,2},{... | collective-permute-start | bytes 2359304 | tf_op jit(solution)/shard_map/ppermute | solution.py:581
  4.0 80.4 %collective-permute-start.2 = (bf16[192,2048]{1,0:T(8,128)(2,1)}, bf16[192,2048]{1,0:T(8,128)(2,1)S(1)}, u32[]{:S(2)}, u32[]{:S(2)}) collective-permute-start(bf16[192,2048]{1,0:T(8,128)(2,1)} %bitcast.22), channel_id=1, source_target_pairs={{0,8},{4,12},{8,0},{12,4},{1,9},{5,13},{9,1},{13,5},{2,10},{6,14},... | collective-permute-start | bytes 2359304 | tf_op jit(solution)/shard_map/ppermute | solution.py:581
  4.5 79.9 %collective-permute-start.1 = (bf16[192,2048]{1,0:T(8,128)(2,1)}, bf16[192,2048]{1,0:T(8,128)(2,1)S(1)}, u32[]{:S(2)}, u32[]{:S(2)}) collective-permute-start(bf16[192,2048]{1,0:T(8,128)(2,1)} %bitcast.23), channel_id=1, source_target_pairs={{0,4},{4,8},{8,12},{12,0},{1,5},{5,9},{9,13},{13,1},{2,6},{6,10},{... | collective-permute-start | bytes 2359304 | tf_op jit(solution)/shard_map/ppermute | solution.py:581
  8.4 73.3 %all-to-all-start = ((bf16[8,2,192,128]{3,2,1,0:T(8,128)(2,1)}), bf16[8,2,192,128]{3,2,1,0:T(8,128)(2,1)S(1)}, u32[]{:S(2)}, u32[]{:S(2)}) async-start(bf16[8,2,192,128]{3,2,1,0:T(8,128)(2,1)} %get-tuple-element.32), calls=%async_computation | async-start | bytes 1572864 | tf_op jit(solution)/shard_map/all_to_all | solution.py:601
  81.8 0.9 copy-start.2
  82.7 3.9 %collective-permute-start = (bf16[8,2,192,128]{3,2,1,0:T(8,128)(2,1)}, bf16[8,2,192,128]{3,2,1,0:T(8,128)(2,1)S(1)}, u32[]{:S(2)}, u32[]{:S(2)}) collective-permute-start(bf16[8,2,192,128]{3,2,1,0:T(8,128)(2,1)} %hold.1.r_3_), channel_id=1, source_target_pairs={{0,16},{16,0},{32,48},{48,32},{64,80},{80,64},{96,112},{112,96},{1... | collective-permute-start | bytes 2359304 | tf_op jit(solution)/shard_map/ppermute | solution.py:606
  84.5 2.1 %copy-start.3 = (bf16[192,2048]{1,0:T(8,128)(2,1)}, bf16[192,2048]{1,0:T(8,128)(2,1)S(1)}, u32[]{:S(2)}) copy-start(bf16[192,2048]{1,0:T(8,128)(2,1)S(1)} %collective-permute-done.3.r_16_) | copy-start | bytes 2359300
  84.5 2.1 %copy-start.4 = (bf16[192,2048]{1,0:T(8,128)(2,1)}, bf16[192,2048]{1,0:T(8,128)(2,1)S(1)}, u32[]{:S(2)}) copy-start(bf16[192,2048]{1,0:T(8,128)(2,1)S(1)} %collective-permute-done.2.r_15_) | copy-start | bytes 2359300
  84.5 2.1 %copy-start.5 = (bf16[192,2048]{1,0:T(8,128)(2,1)}, bf16[192,2048]{1,0:T(8,128)(2,1)S(1)}, u32[]{:S(2)}) copy-start(bf16[192,2048]{1,0:T(8,128)(2,1)S(1)} %collective-permute-done.1.r_14_) | copy-start | bytes 2359300
  86.6 0.9 copy-start.9
  100.8 4.4 %collective-permute-start.4 = (bf16[8,480,128]{2,1,0:T(8,128)(2,1)}, bf16[8,480,128]{2,1,0:T(8,128)(2,1)S(1)}, u32[]{:S(2)}, u32[]{:S(2)}) collective-permute-start(bf16[8,480,128]{2,1,0:T(8,128)(2,1)} %get-tuple-element.43), channel_id=1, source_target_pairs={{0,16},{16,0},{32,48},{48,32},{64,80},{80,64},{96,112},{112,96},{1... | collective-permute-start | bytes 2949128 | tf_op jit(solution)/shard_map/ppermute | solution.py:611
  101.2 57.8 %collective-permute-start.5 = (bf16[192,2048]{1,0:T(8,128)(2,1)}, bf16[192,2048]{1,0:T(8,128)(2,1)S(1)}, u32[]{:S(2)}, u32[]{:S(2)}) collective-permute-start(bf16[192,2048]{1,0:T(8,128)(2,1)} %get-tuple-element.47), channel_id=1, source_target_pairs={{0,4},{4,8},{8,12},{12,0},{1,5},{5,9},{9,13},{13,1},{2,6},{6,10},{... | collective-permute-start | bytes 2359304 | tf_op jit(solution)/shard_map/ppermute | solution.py:581
  102.7 56.3 %collective-permute-start.6 = (bf16[192,2048]{1,0:T(8,128)(2,1)}, bf16[192,2048]{1,0:T(8,128)(2,1)S(1)}, u32[]{:S(2)}, u32[]{:S(2)}) collective-permute-start(bf16[192,2048]{1,0:T(8,128)(2,1)} %get-tuple-element.48), channel_id=1, source_target_pairs={{0,8},{4,12},{8,0},{12,4},{1,9},{5,13},{9,1},{13,5},{2,10},{6,14},... | collective-permute-start | bytes 2359304 | tf_op jit(solution)/shard_map/ppermute | solution.py:581
  104.5 54.6 %collective-permute-start.7 = (bf16[192,2048]{1,0:T(8,128)(2,1)}, bf16[192,2048]{1,0:T(8,128)(2,1)S(1)}, u32[]{:S(2)}, u32[]{:S(2)}) collective-permute-start(bf16[192,2048]{1,0:T(8,128)(2,1)} %get-tuple-element.49), channel_id=1, source_target_pairs={{0,12},{4,0},{8,4},{12,8},{1,13},{5,1},{9,5},{13,9},{2,14},{6,2},{... | collective-permute-start | bytes 2359304 | tf_op jit(solution)/shard_map/ppermute | solution.py:581
  107.6 34.7 %all-to-all-start.1 = ((bf16[8,480,128]{2,1,0:T(8,128)(2,1)}), bf16[8,480,128]{2,1,0:T(8,128)(2,1)S(1)}, u32[]{:S(2)}, u32[]{:S(2)}) async-start(bf16[8,480,128]{2,1,0:T(8,128)(2,1)} %add.9.refs_9_), calls=%async_computation.1 | async-start | bytes 1966080 | tf_op jit(solution)/shard_map/all_to_all | solution.py:613
  142.3 1.6 copy-start
  142.3 1.6 copy-start.1
  153.7 23.9 %all-to-all-start.3 = ((f32[16,24,384]{2,1,0:T(8,128)}), f32[16,24,384]{2,1,0:T(8,128)S(1)}, u32[]{:S(2)}, u32[]{:S(2)}) async-start(f32[16,24,384]{2,1,0:T(8,128)} %spread.1), calls=%async_computation.3 | async-start | bytes 1179648 | tf_op jit(solution)/shard_map/all_to_all | solution.py:618
  159.0 0.9 copy-start.6
  159.0 1.1 copy-start.7
  159.1 1.3 copy-start.8
